TPU v7x, 512 devices: a whole 4x4x16 slice. The times are simulated.
512 devices in a mesh: ep: 128 (over y_hi, z, x), rep: 4 (over y_lo, core).
Axes of the slice: x: 4, y: 4 (y_hi: 2, y_lo: 2; y = y_hi * 2 + y_lo), z: 16, core: 2. Of those that a mesh axis runs over, the one named last changes fastest.
Arguments:
- out_grad: bfloat16 [4096, 3584], P('ep', 'rep'), may hold values from -0.3984375 to 0.3984375
- route_weight: float32 [4096, 4], P('ep'), may hold values from 0.05 to 0.5
- expert_ids: int32 [4096, 4], P('ep'), may hold values from 0 to 95, all different within a row; in each aligned block of 32 rows (0 to 31, 32 to 63, ...) at most 2 rows name the same one
- slot_expert: int32 [128], replicated, may hold values from 0 to 95, as said below
- replica_pick: int32 [128, 96], P('ep'), may hold values from 0 to 1, as said below
- saved_gu: bfloat16 [128, 256, 2, 1024], P('ep', None, None, 'rep'), may hold values from -6 to 6
- down_weight: bfloat16 [128, 1024, 3584], P('ep', None, 'rep'), as said below
Outputs:
- down_grad: bfloat16 [128, 1024, 3584], P('ep', None, 'rep')
- route_grad: float32 [4096, 4], P('ep')
Inputs may be any that keep to these rules, and one draw needn't show every extreme that they name: `expert_ids`: no expert is named by more than 2 of the tokens of one index of ep. `slot_expert`: every expert is held by one or two slots; an expert held by two slots is held by slots s and s + 64. `replica_pick`: entry [i, e] is less than the number of slots that hold expert e. `down_weight`: slots that hold the same expert hold equal weights.
All inputs are finite; a program needn't handle non-finite values.
Results may differ from a plain program's by a relative error of at most 0.0067.
Values may be sent and summed in bfloat16 or wider, within the bound.
No kernel may reach another device: no remote copies, remote signals or barrier semaphores. Data moves between devices by JAX's collectives and lax.ppermute only.
A program may use at most 64 MiB of HBM per device.

v0:
```python
import jax
import jax.numpy as jnp
from jax import lax
from jax.sharding import PartitionSpec as P


def on_device(out_grad, route_weight, expert_ids, slot_expert, replica_pick, saved_gu, down_weight):
    sources = lax.axis_size("ep")
    token_count, top_count = expert_ids.shape
    experts = replica_pick.shape[1]
    slot_count = slot_expert.shape[0]
    rows_total = saved_gu.shape[1]
    pair_rows = rows_total // sources
    features = out_grad.shape[1]
    slot_index = jnp.arange(slot_count, dtype=jnp.int32)
    same_expert = slot_expert[:, None] == slot_expert[None, :]
    copy_rank = jnp.sum(
        (same_expert & (slot_index[None, :] < slot_index[:, None])).astype(jnp.int32), axis=1
    )
    expert_range = jnp.arange(experts, dtype=jnp.int32)
    chosen = expert_ids[:, :, None] == expert_range
    chosen_copy = jnp.sum(jnp.where(chosen, replica_pick[0], 0), axis=2)
    matched = (slot_expert == expert_ids[:, :, None]) & (copy_rank == chosen_copy[:, :, None])
    route_slot = jnp.sum(jnp.where(matched, slot_index, 0), axis=2)
    onehot = chosen.reshape(token_count * top_count, experts).astype(jnp.int32)
    before = jnp.cumsum(onehot, axis=0) - onehot
    position = jnp.sum(before * onehot, axis=1)
    target = route_slot.reshape(-1) * pair_rows + position
    token_of = jnp.arange(token_count * top_count, dtype=jnp.int32) // top_count
    send_rows = (
        jnp.zeros((slot_count * pair_rows, features), out_grad.dtype)
        .at[target]
        .set(out_grad[token_of])
    )
    send_weights = (
        jnp.zeros((slot_count * pair_rows,), jnp.bfloat16)
        .at[target]
        .set(route_weight.reshape(-1).astype(jnp.bfloat16))
    )
    arrived_rows, arrived_weights = (
        lax.all_to_all(
            send_rows.reshape(slot_count, pair_rows, features),
            "ep",
            split_axis=0,
            concat_axis=0,
            tiled=True,
        ),
        lax.all_to_all(
            send_weights.reshape(slot_count, pair_rows),
            "ep",
            split_axis=0,
            concat_axis=0,
            tiled=True,
        ),
    )
    grad_rows = arrived_rows.reshape(rows_total, features)
    weights = arrived_weights.reshape(rows_total).astype(jnp.float32)
    scaled = (weights[:, None] * grad_rows.astype(jnp.float32)).astype(jnp.bfloat16)
    weight = down_weight[0]
    hidden_units = weight.shape[0]
    values = lax.all_gather(saved_gu[0], "rep", axis=2, tiled=True).astype(jnp.float32)
    activated = (jax.nn.silu(values[:, 0]) * values[:, 1]).astype(jnp.bfloat16)
    outputs = jnp.dot(activated, weight, preferred_element_type=jnp.float32)
    grad_block = lax.dot_general(
        activated, scaled, (((0,), (0,)), ((), ())), preferred_element_type=jnp.float32
    )
    gradients = grad_block
    outputs, gradients = (outputs, gradients)
    partial_dot = jnp.sum(grad_rows.astype(jnp.float32) * outputs, axis=1)
    route_dot = lax.psum(partial_dot, "rep")
    returned = lax.all_to_all(
        route_dot.reshape(sources, pair_rows), "ep", split_axis=0, concat_axis=0, tiled=True
    )
    route_grad = returned.reshape(-1)[target].reshape(token_count, top_count)
    own_part = gradients.astype(jnp.bfloat16)
    pieces = own_part.reshape(sources, hidden_units // sources, features)
    members = same_expert.astype(jnp.bfloat16)
    summed = jnp.einsum(
        "st,tiw->siw",
        members,
        lax.all_to_all(pieces, "ep", split_axis=0, concat_axis=0, tiled=True),
        preferred_element_type=jnp.float32,
    ).astype(jnp.bfloat16)
    summed_all = lax.all_to_all(summed, "ep", split_axis=0, concat_axis=0, tiled=True)
    down_grad = summed_all.reshape(hidden_units, features)[None]
    return (down_grad, route_grad)


def solution(mesh):
    placed = (
        P("ep", "rep"),
        P("ep", None),
        P("ep", None),
        P(),
        P("ep", None),
        P("ep", None, None, "rep"),
        P("ep", None, "rep"),
    )
    return jax.shard_map(
        on_device,
        mesh=mesh,
        in_specs=placed,
        out_specs=(P("ep", None, "rep"), P("ep", None)),
        check_vma=False,
    )
```

profile of v0, /device:TPU:1, one launch (start us, length us, event | category | flops | bytes accessed | tf_op | source)
XLA Modules:
  0.0 318.8 jit_solution(16675269415381559086)
XLA Ops:
  7.2 1.8 copy.33
  9.1 0.9 convert_reduce_fusion
  10.0 0.8 copy.35
  10.7 0.9 select_reduce_fusion.2
  11.7 0.9 select_reduce_fusion.1
  13.4 0.7 convert_element_type.60
  14.3 1.3 scatter_custom_fusion
  15.6 0.8 all_to_all.28
  16.4 23.0 %all-to-all-start = ((bf16[128,1,2]{2,1,0:T(2,128)(2,1)}), bf16[128,1,2]{2,1,0:T(2,128)(2,1)S(1)}, u32[]{:S(2)}, u32[]{:S(2)}) async-start(bf16[128,1,2]{2,1,0:T(2,128)(2,1)} %all_to_all.28), calls=%async_computation | async-start | bytes 131072 | tf_op jit(solution)/shard_map/all_to_all | solution.py:48
  39.4 3.0 scatter_custom_fusion.1
  42.4 0.9 reshape.127
  43.4 11.9 %all-to-all-done = bf16[128,1,2]{2,1,0:T(2,128)(2,1)S(1)} async-done(((bf16[128,1,2]{2,1,0:T(2,128)(2,1)}), bf16[128,1,2]{2,1,0:T(2,128)(2,1)S(1)}, u32[]{:S(2)}, u32[]{:S(2)}) %all-to-all-start) | async-done | bytes 544 | tf_op jit(solution)/shard_map/all_to_all | solution.py:48
  55.3 6.2 %all-to-all-start.1 = ((bf16[128,2,896]{2,1,0:T(2,128)(2,1)}), bf16[128,2,896]{2,1,0:T(2,128)(2,1)S(1)}, u32[]{:S(2)}, u32[]{:S(2)}) async-start(bf16[128,2,896]{2,1,0:T(2,128)(2,1)} %reshape.127), calls=%async_computation.1 | async-start | bytes 917504 | tf_op jit(solution)/shard_map/all_to_all | solution.py:41
  61.7 1.5 bitcast_convert_fusion
  63.4 28.1 %all-to-all-done.1 = bf16[128,2,896]{2,1,0:T(2,128)(2,1)S(1)} async-done(((bf16[128,2,896]{2,1,0:T(2,128)(2,1)}), bf16[128,2,896]{2,1,0:T(2,128)(2,1)S(1)}, u32[]{:S(2)}, u32[]{:S(2)}) %all-to-all-start.1) | async-done | bytes 458784 | tf_op jit(solution)/shard_map/all_to_all | solution.py:41
  92.0 0.9 convert_element_type.66
  92.9 3.0 convert_bitcast_fusion
  95.9 9.3 %all-to-all-start.2 = ((bf16[128,8,896]{2,1,0:T(8,128)(2,1)}), bf16[128,8,896]{2,1,0:T(8,128)(2,1)}, u32[]{:S(2)}, u32[]{:S(2)}) async-start(bf16[128,8,896]{2,1,0:T(8,128)(2,1)} %convert_bitcast_fusion), calls=%async_computation.2 | async-start | bytes 3670016 | tf_op jit(solution)/shard_map/all_to_all | solution.py:81
  105.2 1.1 reshape.132
  106.3 2.0 fusion.10
  108.4 13.9 %psum.7 = f32[128,1,2]{2,0,1:T(8,128)} all-reduce(f32[128,1,2]{2,0,1:T(8,128)S(1)} %all_to_all.26), channel_id=1, replica_groups=mesh['ep'=128,'rep'=4] {'rep'}, use_global_device_ids=true, to_apply=%region_8.9 | all-reduce | flops 256 | bytes 2048 | tf_op jit(solution)/shard_map/psum | solution.py:70
  122.3 68.7 %all-to-all-done.2 = bf16[128,8,896]{2,1,0:T(8,128)(2,1)} async-done(((bf16[128,8,896]{2,1,0:T(8,128)(2,1)}), bf16[128,8,896]{2,1,0:T(8,128)(2,1)}, u32[]{:S(2)}, u32[]{:S(2)}) %all-to-all-start.2) | async-done | bytes 1835040 | tf_op jit(solution)/shard_map/all_to_all | solution.py:81
  191.0 9.8 %all-to-all-start.4 = ((f32[128,1,2]{2,1,0:T(1,128)}), f32[128,1,2]{2,1,0:T(1,128)S(1)}, u32[]{:S(2)}, u32[]{:S(2)}) async-start(f32[128,1,2]{2,1,0:T(1,128)} %bitcast.12), calls=%async_computation.4 | async-start | bytes 131072 | tf_op jit(solution)/shard_map/all_to_all | solution.py:71
  200.8 2.2 fusion.4
  203.0 2.3 copy.39
  205.3 11.4 %all-to-all-done.4 = f32[128,1,2]{2,1,0:T(1,128)S(1)} async-done(((f32[128,1,2]{2,1,0:T(1,128)}), f32[128,1,2]{2,1,0:T(1,128)S(1)}, u32[]{:S(2)}, u32[]{:S(2)}) %all-to-all-start.4) | async-done | bytes 1056 | tf_op jit(solution)/shard_map/all_to_all | solution.py:71
  216.7 7.3 %all-to-all-start.3 = ((bf16[128,8,896]{2,1,0:T(8,128)(2,1)}), bf16[128,8,896]{2,1,0:T(8,128)(2,1)}, u32[]{:S(2)}, u32[]{:S(2)}) async-start(bf16[128,8,896]{2,1,0:T(8,128)(2,1)} %copy.39), calls=%async_computation.3 | async-start | bytes 3670016 | tf_op jit(solution)/shard_map/all_to_all | solution.py:84
  224.5 0.8 reduce.3
  225.5 1.3 gather_fusion
  226.8 0.7 copy.41
  227.5 81.6 %all-to-all-done.3 = bf16[128,8,896]{2,1,0:T(8,128)(2,1)} async-done(((bf16[128,8,896]{2,1,0:T(8,128)(2,1)}), bf16[128,8,896]{2,1,0:T(8,128)(2,1)}, u32[]{:S(2)}, u32[]{:S(2)}) %all-to-all-start.3) | async-done | bytes 1835040 | tf_op jit(solution)/shard_map/all_to_all | solution.py:84
  309.1 2.9 copy.47
  (27 shorter events, 2.8 us)
Async XLA Ops:
  7.2 99.1 %copy-start = (bf16[1,1024,896]{2,1,0:T(8,128)(2,1)S(1)}, bf16[1,1024,896]{2,1,0:T(8,128)(2,1)}, u32[]{:S(2)}) copy-start(bf16[1,1024,896]{2,1,0:T(8,128)(2,1)} %param.13) | copy-start | bytes 5505028
  7.2 54.5 %all-gather.3.cloned.1.call-start = ((), (), s32[]{:S(2)}) async-start(), calls=%async_computation.5 | async-start | bytes 1310720 | tf_op jit(solution)/shard_map/all_gather | solution.py:61
  16.4 38.9 %all-to-all-start = ((bf16[128,1,2]{2,1,0:T(2,128)(2,1)}), bf16[128,1,2]{2,1,0:T(2,128)(2,1)S(1)}, u32[]{:S(2)}, u32[]{:S(2)}) async-start(bf16[128,1,2]{2,1,0:T(2,128)(2,1)} %all_to_all.28), calls=%async_computation | async-start | bytes 131072 | tf_op jit(solution)/shard_map/all_to_all | solution.py:48
  55.3 36.2 %all-to-all-start.1 = ((bf16[128,2,896]{2,1,0:T(2,128)(2,1)}), bf16[128,2,896]{2,1,0:T(2,128)(2,1)S(1)}, u32[]{:S(2)}, u32[]{:S(2)}) async-start(bf16[128,2,896]{2,1,0:T(2,128)(2,1)} %reshape.127), calls=%async_computation.1 | async-start | bytes 917504 | tf_op jit(solution)/shard_map/all_to_all | solution.py:41
  95.9 95.1 %all-to-all-start.2 = ((bf16[128,8,896]{2,1,0:T(8,128)(2,1)}), bf16[128,8,896]{2,1,0:T(8,128)(2,1)}, u32[]{:S(2)}, u32[]{:S(2)}) async-start(bf16[128,8,896]{2,1,0:T(8,128)(2,1)} %convert_bitcast_fusion), calls=%async_computation.2 | async-start | bytes 3670016 | tf_op jit(solution)/shard_map/all_to_all | solution.py:81
  106.3 94.5 %copy-start.1 = (s32[128]{0:T(128)S(1)}, s32[128]{0:T(128)}, u32[]{:S(2)}) copy-start(s32[128]{0:T(128)} %param.10) | copy-start | bytes 1540
  191.0 25.7 %all-to-all-start.4 = ((f32[128,1,2]{2,1,0:T(1,128)}), f32[128,1,2]{2,1,0:T(1,128)S(1)}, u32[]{:S(2)}, u32[]{:S(2)}) async-start(f32[128,1,2]{2,1,0:T(1,128)} %bitcast.12), calls=%async_computation.4 | async-start | bytes 131072 | tf_op jit(solution)/shard_map/all_to_all | solution.py:71
  216.7 92.4 %all-to-all-start.3 = ((bf16[128,8,896]{2,1,0:T(8,128)(2,1)}), bf16[128,8,896]{2,1,0:T(8,128)(2,1)}, u32[]{:S(2)}, u32[]{:S(2)}) async-start(bf16[128,8,896]{2,1,0:T(8,128)(2,1)} %copy.39), calls=%async_computation.3 | async-start | bytes 3670016 | tf_op jit(solution)/shard_map/all_to_all | solution.py:84
Sparse Core Ops, SparseCore 0:
  10.1 34.0 all-gather.2
where the time goes:
time: 325 us; the launch traced here: 319 us
  waiting for transfers between devices  202 us (62%)
  starting transfers between devices  55.6 us (17%)
  local copies, waits for them, and re-layouts  19.2 us (6%)
  between operations  14.3 us (4%)
  blocking collectives  13.9 us (4%)
  matrix products  7.16 us (2%)
  other arithmetic  6.96 us (2%)
    all_to_all x1, waiting for transfers between devices, on_device(): lax.all_to_all(summed, 'ep', split_axis=0, concat_axis=0, tiled=True)  81.6 us
    all_to_all x1, waiting for transfers between devices, on_device(): lax.all_to_all(pieces, 'ep', split_axis=0, concat_axis=0, tiled=True)  68.7 us
    all_to_all x1, waiting for transfers between devices, on_device(): lax.all_to_all(send_rows.reshape(slot_count, pair_rows, features), 'ep',...  28.1 us
    all_to_all x1, starting transfers between devices, on_device(): lax.all_to_all(send_weights.reshape(slot_count, pair_rows), 'ep', split_a...  23 us
    psum x1, blocking collectives, on_device(): route_dot = lax.psum(partial_dot, 'rep')  13.9 us
    all_to_all x1, waiting for transfers between devices, on_device(): lax.all_to_all(send_weights.reshape(slot_count, pair_rows), 'ep', split_a...  11.9 us
    all_to_all x1, waiting for transfers between devices, on_device(): lax.all_to_all(route_dot.reshape(sources, pair_rows), 'ep', split_axis=0,...  11.4 us
    all_to_all x1, starting transfers between devices, on_device(): lax.all_to_all(route_dot.reshape(sources, pair_rows), 'ep', split_axis=0,...  9.81 us
  transfers between devices with their start and end apart: 6, of which 5 were waited for; matrix products, arithmetic and copies ran while one was open for 7% of the time, Pallas kernels for 0%

commit v1 on v0

v1 whole, which is shorter than its diff:
```python
import jax
import jax.numpy as jnp
from jax import lax
from jax.experimental import pallas as pl
from jax.experimental.pallas import tpu as pltpu
from jax.sharding import PartitionSpec as P


def pack_kernel(ids_ref, weight_ref, slot_expert_ref, pick_ref, grad_ref, rows_ref, target_ref):
    top, tokens = ids_ref.shape
    experts = pick_ref.shape[1]
    slots = slot_expert_ref.shape[1]
    pair_rows = rows_ref.shape[0] // slots
    slot_expert = slot_expert_ref[...]
    lane = lax.broadcasted_iota(jnp.int32, (1, slots), 1)
    twin = pltpu.roll(slot_expert, slots // 2, 1)
    rank = jnp.where((lane >= slots // 2) & (twin == slot_expert), 1.0, 0.0)
    holds = lax.broadcasted_iota(jnp.int32, (experts, slots), 0) == slot_expert
    pick = jnp.dot(
        pick_ref[...].astype(jnp.bfloat16),
        jnp.where(holds, 1.0, 0.0).astype(jnp.bfloat16),
        preferred_element_type=jnp.float32,
    )
    serves = holds & (pick == rank)
    slot_of = jnp.sum(jnp.where(serves, lane, 0).astype(jnp.float32), axis=1, keepdims=True)
    expert = lax.broadcasted_iota(jnp.int32, (experts, tokens), 0)
    chosen = [expert == ids_ref[k : k + 1, :] for k in range(top)]
    named = sum(jnp.where(c, 1.0, 0.0) for c in chosen)
    earlier = lax.broadcasted_iota(jnp.int32, (tokens, tokens), 0) < lax.broadcasted_iota(
        jnp.int32, (tokens, tokens), 1
    )
    before = jnp.dot(
        named.astype(jnp.bfloat16),
        jnp.where(earlier, 1.0, 0.0).astype(jnp.bfloat16),
        preferred_element_type=jnp.float32,
    )
    place = slot_of * pair_rows + before
    row = lax.broadcasted_iota(jnp.int32, (slots * pair_rows, tokens), 0)
    mix = jnp.zeros((slots * pair_rows, tokens), jnp.float32)
    for k in range(top):
        target = jnp.sum(jnp.where(chosen[k], place, 0.0), axis=0, keepdims=True).astype(jnp.int32)
        target_ref[k : k + 1, :] = target
        mix += jnp.where(row == target, weight_ref[k : k + 1, :], 0.0)
    rows_ref[...] = jnp.dot(
        mix.astype(jnp.bfloat16), grad_ref[...], preferred_element_type=jnp.float32
    ).astype(rows_ref.dtype)


def pick_kernel(returned_ref, target_ref, weight_ref, out_ref):
    top, tokens = target_ref.shape
    slots, pair_rows = returned_ref.shape
    slot = lax.broadcasted_iota(jnp.int32, (slots, tokens), 0)
    for k in range(top):
        target = target_ref[k : k + 1, :]
        found = jnp.zeros((slots, tokens), jnp.float32)
        for p in range(pair_rows):
            found += jnp.where(slot * pair_rows + p == target, returned_ref[:, p : p + 1], 0.0)
        weight = weight_ref[k : k + 1, :].astype(jnp.bfloat16).astype(jnp.float32)
        out_ref[k : k + 1, :] = jnp.sum(found, axis=0, keepdims=True) / weight


def grad_kernel(shared_ref, hidden_ref, twin_hidden_ref, rows_ref, twin_rows_ref, out_ref):
    over_rows = (((0,), (0,)), ((), ()))
    own = lax.dot_general(
        hidden_ref[...], rows_ref[...], over_rows, preferred_element_type=jnp.float32
    )
    twin_rows = jnp.where(shared_ref[0, 0] > 0, twin_rows_ref[...], jnp.zeros((), jnp.bfloat16))
    twin = lax.dot_general(
        twin_hidden_ref[...], twin_rows, over_rows, preferred_element_type=jnp.float32
    )
    out_ref[...] = (own + twin).astype(out_ref.dtype)


def on_device(out_grad, route_weight, expert_ids, slot_expert, replica_pick, saved_gu, down_weight):
    sources = lax.axis_size("ep")
    token_count, top_count = expert_ids.shape
    slot_count = slot_expert.shape[0]
    rows_total = saved_gu.shape[1]
    pair_rows = rows_total // sources
    features = out_grad.shape[1]
    hidden_units = down_weight.shape[1]
    half = slot_count // 2
    swap = [(i, (i + half) % slot_count) for i in range(slot_count)]
    ids_t = expert_ids.T
    weight_t = route_weight.T
    send_rows, target = pl.pallas_call(
        pack_kernel,
        out_shape=(
            jax.ShapeDtypeStruct((rows_total, features), jnp.bfloat16),
            jax.ShapeDtypeStruct((top_count, token_count), jnp.int32),
        ),
        name="pack",
    )(ids_t, weight_t, slot_expert[None], replica_pick, out_grad)
    arrived = lax.all_to_all(
        send_rows.reshape(slot_count, pair_rows, features),
        "ep",
        split_axis=0,
        concat_axis=0,
        tiled=True,
    )
    values = saved_gu[0].astype(jnp.float32)
    part = (jax.nn.silu(values[:, 0]) * values[:, 1]).astype(jnp.bfloat16)
    twin_part = lax.ppermute(part, "ep", swap)
    hidden = lax.all_gather(part, "rep", axis=1, tiled=True)
    twin_hidden = lax.all_gather(twin_part, "rep", axis=1, tiled=True)
    outputs = jnp.dot(hidden, down_weight[0], preferred_element_type=jnp.float32)
    dots = jnp.sum(
        arrived.astype(jnp.float32) * outputs.reshape(sources, pair_rows, features), axis=2
    )
    dots = lax.psum(dots, "rep")
    returned = lax.all_to_all(
        dots.reshape(sources, 1, pair_rows), "ep", split_axis=0, concat_axis=0, tiled=True
    )
    route_grad = pl.pallas_call(
        pick_kernel,
        out_shape=jax.ShapeDtypeStruct((top_count, token_count), jnp.float32),
        name="pick",
    )(returned.reshape(slot_count, pair_rows), target, weight_t).T
    rows = arrived.reshape(rows_total, features)
    twin_rows = lax.ppermute(rows, "ep", swap)
    me = lax.axis_index("ep")
    own_expert = lax.dynamic_slice(slot_expert, (me,), (1,))
    twin_expert = lax.dynamic_slice(slot_expert, ((me + half) % slot_count,), (1,))
    shared = (own_expert == twin_expert).astype(jnp.int32).reshape(1, 1)
    steps = 4
    block = hidden_units // steps
    down_grad = pl.pallas_call(
        grad_kernel,
        grid=(steps,),
        in_specs=[
            pl.BlockSpec(memory_space=pltpu.SMEM),
            pl.BlockSpec((rows_total, block), lambda i: (0, i)),
            pl.BlockSpec((rows_total, block), lambda i: (0, i)),
            pl.BlockSpec((rows_total, features), lambda i: (0, 0)),
            pl.BlockSpec((rows_total, features), lambda i: (0, 0)),
        ],
        out_specs=pl.BlockSpec((block, features), lambda i: (i, 0)),
        out_shape=jax.ShapeDtypeStruct((hidden_units, features), jnp.bfloat16),
        cost_estimate=pl.CostEstimate(
            flops=4 * rows_total * hidden_units * features,
            bytes_accessed=4 * hidden_units * features,
            transcendentals=0,
        ),
        name="down_grad",
    )(shared, hidden, twin_hidden, rows, twin_rows)
    return (down_grad[None], route_grad)


def solution(mesh):
    placed = (
        P("ep", "rep"),
        P("ep", None),
        P("ep", None),
        P(),
        P("ep", None),
        P("ep", None, None, "rep"),
        P("ep", None, "rep"),
    )
    return jax.shard_map(
        on_device,
        mesh=mesh,
        in_specs=placed,
        out_specs=(P("ep", None, "rep"), P("ep", None)),
        check_vma=False,
    )
```

time: 325 us -> 109 us (0.34); the launches traced: 319 us -> 108 us
  waiting for transfers between devices: 202 us -> 22.3 us
  starting transfers between devices: 55.6 us -> 39.9 us
  local copies, waits for them, and re-layouts: 19.2 us -> 5.13 us
  blocking collectives: 13.9 us -> 27.8 us
  between operations: 14.3 us -> 2.08 us
  Pallas kernels: 0 us -> 8.74 us
  other arithmetic: 6.96 us -> 0.12 us
  matrix products: 7.16 us -> 1.84 us
    all_to_all x4 -> x1, waiting for transfers between devices: 174 us -> 7.3 us  [on_device(): lax.all_to_all(dots.reshape(sources, 1, pair_rows), 'ep', split_axis=0, c...]
    all_to_all x4 -> x1, starting transfers between devices: 49.4 us -> 10.7 us  [on_device(): lax.all_to_all(dots.reshape(sources, 1, pair_rows), 'ep', split_axis=0, c...]
    all_gather x0 -> x2, blocking collectives: none -> 17.2 us  [the longest x1 8.68 us: on_device(): hidden = lax.all_gather(part, 'rep', axis=1, tiled=True)]
    all_to_all x1, starting transfers between devices: 6.21 us -> 23 us  [on_device(): lax.all_to_all(send_rows.reshape(slot_count, pair_rows, features), 'ep',...]
    all_to_all x1, waiting for transfers between devices: 28.1 us -> 14.9 us  [on_device(): lax.all_to_all(send_rows.reshape(slot_count, pair_rows, features), 'ep',...]
    pallas_call x0 -> x3, Pallas kernels: none -> 8.74 us  [the longest x1 4.77 us: on_device(): pl.pallas_call(grad_kernel, grid=(steps,), in_specs=[pl.BlockSpec(memory_...]
    ppermute x0 -> x2, starting transfers between devices: none -> 6.23 us  [the longest x1 4.3 us: on_device(): twin_part = lax.ppermute(part, 'ep', swap)]
    unnamed x8 -> x12, local copies, waits for them, and re-layouts: 6.14 us -> 0.65 us
  transfers between devices with their start and end apart: 6 -> 4, of which waited for: 5 -> 2; matrix products, arithmetic and copies ran while one was open for 7% -> 4% of each run, Pallas kernels for 0% -> 2%
where the time goes in v1:
time: 109 us; the launch traced here: 108 us
  starting transfers between devices  39.9 us (37%)
  blocking collectives  27.8 us (26%)
  waiting for transfers between devices  22.3 us (20%)
  Pallas kernels  8.74 us (8%)
  local copies, waits for them, and re-layouts  5.13 us (5%)
  between operations  2.08 us (2%)
  matrix products  1.84 us (2%)
    all_to_all x1, starting transfers between devices, on_device(): lax.all_to_all(send_rows.reshape(slot_count, pair_rows, features), 'ep',...  23 us
    all_to_all x1, waiting for transfers between devices, on_device(): lax.all_to_all(send_rows.reshape(slot_count, pair_rows, features), 'ep',...  14.9 us
    all_to_all x1, starting transfers between devices, on_device(): lax.all_to_all(dots.reshape(sources, 1, pair_rows), 'ep', split_axis=0, c...  10.7 us
    psum x1, blocking collectives, on_device(): dots = lax.psum(dots, 'rep')  10.6 us
    all_gather x1, blocking collectives, on_device(): hidden = lax.all_gather(part, 'rep', axis=1, tiled=True)  8.68 us
    all_gather x1, blocking collectives, on_device(): twin_hidden = lax.all_gather(twin_part, 'rep', axis=1, tiled=True)  8.57 us
    all_to_all x1, waiting for transfers between devices, on_device(): lax.all_to_all(dots.reshape(sources, 1, pair_rows), 'ep', split_axis=0, c...  7.3 us
    pallas_call x1, Pallas kernels, on_device(): pl.pallas_call(grad_kernel, grid=(steps,), in_specs=[pl.BlockSpec(memory_...  4.77 us
  transfers between devices with their start and end apart: 4, of which 2 were waited for; matrix products, arithmetic and copies ran while one was open for 4% of the time, Pallas kernels for 2%

profile of v1, /device:TPU:1, one launch (start us, length us, event | category | flops | bytes accessed | tf_op | source)
XLA Modules:
  0.0 107.8 jit_solution(14781768847781485528)
XLA Ops:
  0.6 0.0 copy-start
  0.6 0.0 copy-start.5
  0.7 0.0 copy-start.3
  0.7 2.3 %pack.1 = (bf16[256,896]{1,0:T(8,128)(2,1)}, s32[4,32]{1,0:T(4,128)}) custom-call(s32[4,32]{1,0:T(4,128)} %bitcast.34, f32[4,32]{1,0:T(4,128)} %bitcast.31, s32[1,128]{1,0:T(1,128)} %bitcast.33, s32[1,96]{1,0:T(1,128)} %pick_ref.1, bf16[32,896]{1,0:T(8,128)(2,1)} %grad_ref.1), custom_call_target="tpu_custom_call" | custom-call | tf_op jit(solution)/shard_map/pack/pallas_call | solution.py:86
  3.0 2.0 %reshape.27 = bf16[128,2,896]{2,1,0:T(2,128)(2,1)} reshape(bf16[256,896]{1,0:T(8,128)(2,1)} %get-tuple-element.4) | data formatting | bytes 917504 | tf_op jit(solution)/shard_map/reshape | solution.py:95
  5.0 23.0 %all-to-all-start = ((bf16[128,2,896]{2,1,0:T(2,128)(2,1)}), bf16[128,2,896]{2,1,0:T(2,128)(2,1)S(1)}, u32[]{:S(2)}, u32[]{:S(2)}) async-start(bf16[128,2,896]{2,1,0:T(2,128)(2,1)} %reshape.27), calls=%async_computation | async-start | bytes 917504 | tf_op jit(solution)/shard_map/all_to_all | solution.py:94
  27.9 0.0 copy-done.3
  28.0 0.1 fusion.10
  28.1 4.3 %collective-permute-start = (bf16[256,256]{1,0:T(8,128)(2,1)S(1)}, bf16[256,256]{1,0:T(8,128)(2,1)S(1)}, u32[]{:S(2)}, u32[]{:S(2)}) collective-permute-start(bf16[256,256]{1,0:T(8,128)(2,1)S(1)} %fusion.10), channel_id=1, source_target_pairs={{0,256},{4,260},{8,264},{12,268},{16,272},{20,276},{24,280},{28,28... | collective-permute-start | bytes 393224 | tf_op jit(solution)/shard_map/ppermute | solution.py:103
  32.4 0.0 copy-done.5
  32.4 0.6 fusion.11
  34.3 8.7 %all_gather.6.hidden_ref = bf16[256,1024]{1,0:T(8,128)(2,1)S(1)} all-gather(bf16[256,256]{1,0:T(8,128)(2,1)S(1)} %fusion.10), channel_id=1, replica_groups=mesh['ep'=128,'rep'=4] {'rep'}, dimensions={1}, use_global_device_ids=true | all-gather | bytes 655360 | tf_op jit(solution)/shard_map/all_gather | solution.py:104
  43.0 0.0 copy-start.1
  43.0 1.0 dot_general.5
  44.0 14.9 %all-to-all-done = bf16[128,2,896]{2,1,0:T(2,128)(2,1)S(1)} async-done(((bf16[128,2,896]{2,1,0:T(2,128)(2,1)}), bf16[128,2,896]{2,1,0:T(2,128)(2,1)S(1)}, u32[]{:S(2)}, u32[]{:S(2)}) %all-to-all-start) | async-done | bytes 458784 | tf_op jit(solution)/shard_map/all_to_all | solution.py:94
  58.9 0.2 reshape.28.rows_ref
  59.1 0.0 copy-start.2
  59.1 1.9 %collective-permute-start.1 = (bf16[256,896]{1,0:T(8,128)(2,1)S(1)}, bf16[256,896]{1,0:T(8,128)(2,1)}, u32[]{:S(2)}, u32[]{:S(2)}) collective-permute-start(bf16[256,896]{1,0:T(8,128)(2,1)S(1)} %reshape.28.rows_ref), channel_id=1, source_target_pairs={{0,256},{4,260},{8,264},{12,268},{16,272},{20,276},{24,280},{28,28... | collective-permute-start | bytes 1376264 | tf_op jit(solution)/shard_map/ppermute | solution.py:120
  61.0 0.0 copy-done
  61.0 1.8 %fusion.5 = f32[128,2]{0,1:T(2,128)S(1)} fusion(bf16[1,1024,896]{2,1,0:T(8,128)(2,1)S(1)} %copy-done, bf16[128,2,1024]{2,1,0:T(2,128)(2,1)} %dot_general.5, bf16[128,2,896]{2,1,0:T(2,128)(2,1)S(1)} %all-to-all-done), kind=kOutput, calls=%fused_computation.3 | convolution fusion | flops 470449920 | bytes 2819072 | tf_op jit(solution)/shard_map/dot_general | solution.py:106
  62.9 0.0 copy-done.1
  62.9 0.0 copy-done.2
  62.9 10.6 %psum.7 = f32[128,1,2]{0,2,1:T(2,128)S(1)} all-reduce(f32[128,1,2]{0,2,1:T(2,128)S(1)} %bitcast.36), channel_id=1, replica_groups=mesh['ep'=128,'rep'=4] {'rep'}, use_global_device_ids=true, to_apply=%region_1.2 | all-reduce | flops 256 | bytes 2048 | tf_op jit(solution)/shard_map/psum | solution.py:110
  73.5 0.7 copy.16
  74.2 10.7 %all-to-all-start.1 = ((f32[128,1,2]{2,1,0:T(1,128)}), f32[128,1,2]{2,1,0:T(1,128)S(1)}, u32[]{:S(2)}, u32[]{:S(2)}) async-start(f32[128,1,2]{2,1,0:T(1,128)} %copy.16), calls=%async_computation.1 | async-start | bytes 131072 | tf_op jit(solution)/shard_map/all_to_all | solution.py:111
  84.9 0.0 collective-permute-done
  84.9 8.6 %all_gather.7.twin_hidden_ref = bf16[256,1024]{1,0:T(8,128)(2,1)} all-gather(bf16[256,256]{1,0:T(8,128)(2,1)S(1)} %collective-permute-done), channel_id=1, replica_groups=mesh['ep'=128,'rep'=4] {'rep'}, dimensions={1}, use_global_device_ids=true | all-gather | bytes 655360 | tf_op jit(solution)/shard_map/all_gather | solution.py:105
  93.5 7.3 %all-to-all-done.1 = f32[128,1,2]{2,1,0:T(1,128)S(1)} async-done(((f32[128,1,2]{2,1,0:T(1,128)}), f32[128,1,2]{2,1,0:T(1,128)S(1)}, u32[]{:S(2)}, u32[]{:S(2)}) %all-to-all-start.1) | async-done | bytes 1056 | tf_op jit(solution)/shard_map/all_to_all | solution.py:111
  100.8 0.6 copy-done.4
  101.4 1.6 %pick.1 = f32[4,32]{1,0:T(4,128)} custom-call(f32[128,2]{1,0:T(8,128)} %bitcast.30, s32[4,32]{1,0:T(4,128)} %get-tuple-element.5.target_ref, f32[4,32]{1,0:T(4,128)} %bitcast.32), custom_call_target="tpu_custom_call" | custom-call | tf_op jit(solution)/shard_map/pick/pallas_call | solution.py:114
  103.0 0.0 collective-permute-done.1.twin_rows_ref
  103.0 4.8 %down_grad.1 = bf16[1024,896]{1,0:T(8,128)(2,1)} custom-call(s32[1,1]{1,0:T(1,128)} %bitcast.shared_ref, bf16[256,1024]{1,0:T(8,128)(2,1)} %copy-done.1, bf16[256,1024]{1,0:T(8,128)(2,1)} %all_gather.7.twin_hidden_ref, bf16[256,896]{1,0:T(8,128)(2,1)} %copy-done.2, bf16[256,896]{1,0:T(8,128)(2,1)} %collective-permute-done.1.twin_rows_ref), custom_call_target="tpu_custom_call" | custom-call | flops 939524096 | bytes 3670016 | tf_op jit(solution)/shard_map/down_grad/pallas_call | solution.py:127
  (2 shorter events, 0.0 us)
Async XLA Ops:
  0.6 60.4 %copy-start = (bf16[1,1024,896]{2,1,0:T(8,128)(2,1)S(1)}, bf16[1,1024,896]{2,1,0:T(8,128)(2,1)}, u32[]{:S(2)}) copy-start(bf16[1,1024,896]{2,1,0:T(8,128)(2,1)} %param.13) | copy-start | bytes 5505028
  0.6 31.8 %copy-start.5 = (s32[128]{0:T(128)S(1)}, s32[128]{0:T(128)}, u32[]{:S(2)}) copy-start(s32[128]{0:T(128)} %param.10) | copy-start | bytes 1540
  0.7 27.3 %copy-start.3 = (bf16[1,256,2,256]{3,2,1,0:T(2,128)(2,1)S(1)}, bf16[1,256,2,256]{3,2,1,0:T(2,128)(2,1)}, u32[]{:S(2)}) copy-start(bf16[1,256,2,256]{3,2,1,0:T(2,128)(2,1)} %param.12) | copy-start | bytes 786436
  5.0 54.0 %all-to-all-start = ((bf16[128,2,896]{2,1,0:T(2,128)(2,1)}), bf16[128,2,896]{2,1,0:T(2,128)(2,1)S(1)}, u32[]{:S(2)}, u32[]{:S(2)}) async-start(bf16[128,2,896]{2,1,0:T(2,128)(2,1)} %reshape.27), calls=%async_computation | async-start | bytes 917504 | tf_op jit(solution)/shard_map/all_to_all | solution.py:94
  28.1 56.8 %collective-permute-start = (bf16[256,256]{1,0:T(8,128)(2,1)S(1)}, bf16[256,256]{1,0:T(8,128)(2,1)S(1)}, u32[]{:S(2)}, u32[]{:S(2)}) collective-permute-start(bf16[256,256]{1,0:T(8,128)(2,1)S(1)} %fusion.10), channel_id=1, source_target_pairs={{0,256},{4,260},{8,264},{12,268},{16,272},{20,276},{24,280},{28,28... | collective-permute-start | bytes 393224 | tf_op jit(solution)/shard_map/ppermute | solution.py:103
  43.0 19.9 %copy-start.1 = (bf16[256,1024]{1,0:T(8,128)(2,1)}, bf16[256,1024]{1,0:T(8,128)(2,1)S(1)}, u32[]{:S(2)}) copy-start(bf16[256,1024]{1,0:T(8,128)(2,1)S(1)} %all_gather.6.hidden_ref) | copy-start | bytes 1572868
  59.1 3.8 %copy-start.2 = (bf16[256,896]{1,0:T(8,128)(2,1)}, bf16[256,896]{1,0:T(8,128)(2,1)S(1)}, u32[]{:S(2)}) copy-start(bf16[256,896]{1,0:T(8,128)(2,1)S(1)} %reshape.28.rows_ref) | copy-start | bytes 1376260
  59.1 43.9 %collective-permute-start.1 = (bf16[256,896]{1,0:T(8,128)(2,1)S(1)}, bf16[256,896]{1,0:T(8,128)(2,1)}, u32[]{:S(2)}, u32[]{:S(2)}) collective-permute-start(bf16[256,896]{1,0:T(8,128)(2,1)S(1)} %reshape.28.rows_ref), channel_id=1, source_target_pairs={{0,256},{4,260},{8,264},{12,268},{16,272},{20,276},{24,280},{28,28... | collective-permute-start | bytes 1376264 | tf_op jit(solution)/shard_map/ppermute | solution.py:120
  74.2 26.6 %all-to-all-start.1 = ((f32[128,1,2]{2,1,0:T(1,128)}), f32[128,1,2]{2,1,0:T(1,128)S(1)}, u32[]{:S(2)}, u32[]{:S(2)}) async-start(f32[128,1,2]{2,1,0:T(1,128)} %copy.16), calls=%async_computation.1 | async-start | bytes 131072 | tf_op jit(solution)/shard_map/all_to_all | solution.py:111
  100.8 0.6 copy-start.4

commit v2 on v1

--- a/solution.py
+++ b/solution.py
@@ -10,7 +10,7 @@
     top, tokens = ids_ref.shape
     experts = pick_ref.shape[1]
     slots = slot_expert_ref.shape[1]
-    pair_rows = rows_ref.shape[0] // slots
+    pair_rows = rows_ref.shape[1]
     slot_expert = slot_expert_ref[...]
     lane = lax.broadcasted_iota(jnp.int32, (1, slots), 1)
     twin = pltpu.roll(slot_expert, slots // 2, 1)
@@ -41,12 +41,37 @@
         target = jnp.sum(jnp.where(chosen[k], place, 0.0), axis=0, keepdims=True).astype(jnp.int32)
         target_ref[k : k + 1, :] = target
         mix += jnp.where(row == target, weight_ref[k : k + 1, :], 0.0)
-    rows_ref[...] = jnp.dot(
-        mix.astype(jnp.bfloat16), grad_ref[...], preferred_element_type=jnp.float32
-    ).astype(rows_ref.dtype)
-
-
-def pick_kernel(returned_ref, target_ref, weight_ref, out_ref):
+    rows = jnp.dot(mix.astype(jnp.bfloat16), grad_ref[...], preferred_element_type=jnp.float32)
+    rows_ref[...] = rows.astype(rows_ref.dtype).reshape(rows_ref.shape)
+
+
+def hidden_kernel(saved_ref, out_ref):
+    gate = saved_ref[:, 0, :].astype(jnp.float32)
+    up = saved_ref[:, 1, :].astype(jnp.float32)
+    out_ref[...] = (gate / (1.0 + jnp.exp(-gate)) * up).astype(out_ref.dtype)
+
+
+def forward_kernel(hidden_ref, weight_ref, out_ref):
+    out_ref[...] = jnp.dot(hidden_ref[...], weight_ref[...], preferred_element_type=jnp.float32)
+
+
+def dots_kernel(arrived_ref, outputs_ref, _, dots_ref, scratch):
+    rows = arrived_ref[...].reshape(outputs_ref.shape)
+    total = jnp.sum(rows.astype(jnp.float32) * outputs_ref[...], axis=1, keepdims=True)
+    scratch[...] = jnp.broadcast_to(total, scratch.shape)
+    sources, pair_rows = dots_ref.shape
+    lane = lax.broadcasted_iota(jnp.int32, (sources, scratch.shape[1]), 1)
+    found = scratch[pl.ds(0, sources, stride=pair_rows), :]
+    for p in range(1, pair_rows):
+        found = jnp.where(lane == p, scratch[pl.ds(p, sources, stride=pair_rows), :], found)
+    dots_ref[...] = found[:, :pair_rows]
+
+
+def matrix_kernel(arrived_ref, _, rows_ref):
+    rows_ref[...] = arrived_ref[...].reshape(rows_ref.shape)
+
+
+def pick_kernel(returned_ref, target_ref, weight_ref, _, out_ref):
     top, tokens = target_ref.shape
     slots, pair_rows = returned_ref.shape
     slot = lax.broadcasted_iota(jnp.int32, (slots, tokens), 0)
@@ -59,7 +84,7 @@
         out_ref[k : k + 1, :] = jnp.sum(found, axis=0, keepdims=True) / weight
 
 
-def grad_kernel(shared_ref, hidden_ref, twin_hidden_ref, rows_ref, twin_rows_ref, out_ref):
+def grad_kernel(shared_ref, hidden_ref, twin_hidden_ref, rows_ref, twin_rows_ref, out_ref, order_ref):
     over_rows = (((0,), (0,)), ((), ()))
     own = lax.dot_general(
         hidden_ref[...], rows_ref[...], over_rows, preferred_element_type=jnp.float32
@@ -69,6 +94,7 @@
         twin_hidden_ref[...], twin_rows, over_rows, preferred_element_type=jnp.float32
     )
     out_ref[...] = (own + twin).astype(out_ref.dtype)
+    order_ref[...] = jnp.zeros_like(order_ref)
 
 
 def on_device(out_grad, route_weight, expert_ids, slot_expert, replica_pick, saved_gu, down_weight):
@@ -86,37 +112,50 @@
     send_rows, target = pl.pallas_call(
         pack_kernel,
         out_shape=(
-            jax.ShapeDtypeStruct((rows_total, features), jnp.bfloat16),
+            jax.ShapeDtypeStruct((slot_count, pair_rows, features), jnp.bfloat16),
             jax.ShapeDtypeStruct((top_count, token_count), jnp.int32),
         ),
         name="pack",
     )(ids_t, weight_t, slot_expert[None], replica_pick, out_grad)
-    arrived = lax.all_to_all(
-        send_rows.reshape(slot_count, pair_rows, features),
-        "ep",
-        split_axis=0,
-        concat_axis=0,
-        tiled=True,
-    )
-    values = saved_gu[0].astype(jnp.float32)
-    part = (jax.nn.silu(values[:, 0]) * values[:, 1]).astype(jnp.bfloat16)
+    arrived = lax.all_to_all(send_rows, "ep", split_axis=0, concat_axis=0, tiled=True)
+    part = pl.pallas_call(
+        hidden_kernel,
+        out_shape=jax.ShapeDtypeStruct((rows_total, saved_gu.shape[3]), jnp.bfloat16),
+        compiler_params=pltpu.CompilerParams(vmem_limit_bytes=8 << 20),
+        name="hidden",
+    )(saved_gu[0])
     twin_part = lax.ppermute(part, "ep", swap)
     hidden = lax.all_gather(part, "rep", axis=1, tiled=True)
     twin_hidden = lax.all_gather(twin_part, "rep", axis=1, tiled=True)
-    outputs = jnp.dot(hidden, down_weight[0], preferred_element_type=jnp.float32)
-    dots = jnp.sum(
-        arrived.astype(jnp.float32) * outputs.reshape(sources, pair_rows, features), axis=2
-    )
+    outputs = pl.pallas_call(
+        forward_kernel,
+        out_shape=pltpu.VMEM((rows_total, features), jnp.float32),
+        compiler_params=pltpu.CompilerParams(vmem_limit_bytes=12 << 20),
+        name="forward",
+    )(hidden, down_weight[0])
+    dots = pl.pallas_call(
+        dots_kernel,
+        in_specs=[
+            pl.BlockSpec(memory_space=pltpu.VMEM),
+            pl.BlockSpec(memory_space=pltpu.VMEM),
+            pl.BlockSpec(memory_space=pl.ANY),
+        ],
+        out_shape=jax.ShapeDtypeStruct((sources, pair_rows), jnp.float32),
+        scratch_shapes=[pltpu.VMEM((rows_total, 128), jnp.float32)],
+        compiler_params=pltpu.CompilerParams(vmem_limit_bytes=8 << 20),
+        name="dots",
+    )(arrived, outputs, twin_hidden)
     dots = lax.psum(dots, "rep")
     returned = lax.all_to_all(
         dots.reshape(sources, 1, pair_rows), "ep", split_axis=0, concat_axis=0, tiled=True
     )
-    route_grad = pl.pallas_call(
-        pick_kernel,
-        out_shape=jax.ShapeDtypeStruct((top_count, token_count), jnp.float32),
-        name="pick",
-    )(returned.reshape(slot_count, pair_rows), target, weight_t).T
-    rows = arrived.reshape(rows_total, features)
+    rows = pl.pallas_call(
+        matrix_kernel,
+        in_specs=[pl.BlockSpec(memory_space=pltpu.VMEM), pl.BlockSpec(memory_space=pl.ANY)],
+        out_shape=jax.ShapeDtypeStruct((rows_total, features), jnp.bfloat16),
+        compiler_params=pltpu.CompilerParams(vmem_limit_bytes=8 << 20),
+        name="matrix",
+    )(arrived, dots)
     twin_rows = lax.ppermute(rows, "ep", swap)
     me = lax.axis_index("ep")
     own_expert = lax.dynamic_slice(slot_expert, (me,), (1,))
@@ -124,7 +163,7 @@
     shared = (own_expert == twin_expert).astype(jnp.int32).reshape(1, 1)
     steps = 4
     block = hidden_units // steps
-    down_grad = pl.pallas_call(
+    down_grad, order = pl.pallas_call(
         grad_kernel,
         grid=(steps,),
         in_specs=[
@@ -134,15 +173,29 @@
             pl.BlockSpec((rows_total, features), lambda i: (0, 0)),
             pl.BlockSpec((rows_total, features), lambda i: (0, 0)),
         ],
-        out_specs=pl.BlockSpec((block, features), lambda i: (i, 0)),
-        out_shape=jax.ShapeDtypeStruct((hidden_units, features), jnp.bfloat16),
+        out_specs=(
+            pl.BlockSpec((block, features), lambda i: (i, 0)),
+            pl.BlockSpec((8, 128), lambda i: (0, 0)),
+        ),
+        out_shape=(
+            jax.ShapeDtypeStruct((hidden_units, features), jnp.bfloat16),
+            jax.ShapeDtypeStruct((8, 128), jnp.float32),
+        ),
         cost_estimate=pl.CostEstimate(
             flops=4 * rows_total * hidden_units * features,
             bytes_accessed=4 * hidden_units * features,
             transcendentals=0,
         ),
+        compiler_params=pltpu.CompilerParams(vmem_limit_bytes=16 << 20),
         name="down_grad",
     )(shared, hidden, twin_hidden, rows, twin_rows)
+    route_grad = pl.pallas_call(
+        pick_kernel,
+        in_specs=[pl.BlockSpec(memory_space=pltpu.VMEM)] * 3 + [pl.BlockSpec(memory_space=pl.ANY)],
+        out_shape=jax.ShapeDtypeStruct((top_count, token_count), jnp.float32),
+        compiler_params=pltpu.CompilerParams(vmem_limit_bytes=4 << 20),
+        name="pick",
+    )(returned.reshape(slot_count, pair_rows), target, weight_t, order).T
     return (down_grad[None], route_grad)
 
 

time: 109 us -> 103 us (0.945)
  waiting for transfers between devices: 22.3 us -> 17.9 us
  blocking collectives: 27.8 us -> 32 us
  local copies, waits for them, and re-layouts: 5.13 us -> 3.12 us
  matrix products: 1.84 us -> 0 us
    all_to_all x1, waiting for transfers between devices: 14.9 us -> 5.08 us  [on_device(): lax.all_to_all(send_rows, 'ep', split_axis=0, concat_axis=0, tiled=True)]
    all_to_all x1, waiting for transfers between devices: 7.3 us -> 12.3 us  [on_device(): lax.all_to_all(dots.reshape(sources, 1, pair_rows), 'ep', split_axis=0, c...]
    psum x1, blocking collectives: 10.6 us -> 14.3 us  [on_device(): dots = lax.psum(dots, 'rep')]
    reshape x2 -> x0, local copies, waits for them, and re-layouts: 2.14 us -> none  [the longest x1 1.97 us: on_device(): send_rows.reshape(slot_count, pair_rows, features)]
    dot_general x1 -> x0, matrix products: 1.84 us -> none  [on_device(): jnp.dot(hidden, down_weight[0], preferred_element_type=jnp.float32)]
    unnamed x12 -> x10, local copies, waits for them, and re-layouts: 0.65 us -> 2.46 us
    pallas_call x1, Pallas kernels: 4.77 us -> 3.07 us  [on_device(): pl.pallas_call(grad_kernel, grid=(steps,), in_specs=[pl.BlockSpec(memory_...]
    all_gather x1, blocking collectives: 8.68 us -> 10.1 us  [on_device(): hidden = lax.all_gather(part, 'rep', axis=1, tiled=True)]
  transfers between devices with their start and end apart: 4 -> 4, of which waited for: 2 -> 3; matrix products, arithmetic and copies ran while one was open for 4% -> 1% of each run, Pallas kernels for 2% -> 4%
where the time goes in v2:
time: 103 us; the launch traced here: 102 us
  starting transfers between devices  38.9 us (38%)
  blocking collectives  32 us (31%)
  waiting for transfers between devices  17.9 us (17%)
  Pallas kernels  7.88 us (8%)
  local copies, waits for them, and re-layouts  3.12 us (3%)
  between operations  2.02 us (2%)
    all_to_all x1, starting transfers between devices, on_device(): lax.all_to_all(send_rows, 'ep', split_axis=0, concat_axis=0, tiled=True)  23 us
    psum x1, blocking collectives, on_device(): dots = lax.psum(dots, 'rep')  14.3 us
    all_to_all x1, waiting for transfers between devices, on_device(): lax.all_to_all(dots.reshape(sources, 1, pair_rows), 'ep', split_axis=0, c...  12.3 us
    all_gather x1, blocking collectives, on_device(): hidden = lax.all_gather(part, 'rep', axis=1, tiled=True)  10.1 us
    all_to_all x1, starting transfers between devices, on_device(): lax.all_to_all(dots.reshape(sources, 1, pair_rows), 'ep', split_axis=0, c...  9.76 us
    all_gather x1, blocking collectives, on_device(): twin_hidden = lax.all_gather(twin_part, 'rep', axis=1, tiled=True)  7.66 us
    all_to_all x1, waiting for transfers between devices, on_device(): lax.all_to_all(send_rows, 'ep', split_axis=0, concat_axis=0, tiled=True)  5.08 us
    ppermute x1, starting transfers between devices, on_device(): twin_part = lax.ppermute(part, 'ep', swap)  4.3 us
  transfers between devices with their start and end apart: 4, of which 3 were waited for; matrix products, arithmetic and copies ran while one was open for 1% of the time, Pallas kernels for 4%

profile of v2, /device:TPU:1, one launch (start us, length us, event | category | flops | bytes accessed | tf_op | source)
XLA Modules:
  0.0 101.9 jit_solution(18198519514060637209)
XLA Ops:
  0.6 2.2 %pack.1 = (bf16[128,2,896]{2,1,0:T(2,128)(2,1)}, s32[4,32]{1,0:T(4,128)}) custom-call(s32[4,32]{1,0:T(4,128)} %bitcast.18, f32[4,32]{1,0:T(4,128)} %bitcast.15, s32[1,128]{1,0:T(1,128)} %bitcast.17, s32[1,96]{1,0:T(1,128)} %pick_ref.1, bf16[32,896]{1,0:T(8,128)(2,1)} %grad_ref.1), custom_call_target="tpu_custom_call" | custom-call | tf_op jit(solution)/shard_map/pack/pallas_call | solution.py:112
  2.8 23.0 %all-to-all-start = ((bf16[128,2,896]{2,1,0:T(2,128)(2,1)}), bf16[128,2,896]{2,1,0:T(2,128)(2,1)S(1)}, u32[]{:S(2)}, u32[]{:S(2)}) async-start(bf16[128,2,896]{2,1,0:T(2,128)(2,1)} %get-tuple-element.6), calls=%async_computation | async-start | bytes 917504 | tf_op jit(solution)/shard_map/all_to_all | solution.py:120
  25.8 0.0 copy-start.1
  25.8 0.9 copy-done.1
  26.8 0.7 hidden.1
  27.4 4.3 %collective-permute-start = (bf16[256,256]{1,0:T(8,128)(2,1)S(1)}, bf16[256,256]{1,0:T(8,128)(2,1)S(1)}, u32[]{:S(2)}, u32[]{:S(2)}) collective-permute-start(bf16[256,256]{1,0:T(8,128)(2,1)S(1)} %hidden.1), channel_id=1, source_target_pairs={{0,256},{4,260},{8,264},{12,268},{16,272},{20,276},{24,280},{28,28... | collective-permute-start | bytes 393224 | tf_op jit(solution)/shard_map/ppermute | solution.py:127
  31.7 10.1 %all_gather.6.hidden_ref = bf16[256,1024]{1,0:T(8,128)(2,1)S(1)} all-gather(bf16[256,256]{1,0:T(8,128)(2,1)S(1)} %hidden.1), channel_id=1, replica_groups=mesh['ep'=128,'rep'=4] {'rep'}, dimensions={1}, use_global_device_ids=true | all-gather | bytes 655360 | tf_op jit(solution)/shard_map/all_gather | solution.py:128
  41.8 0.0 copy-start
  41.8 1.5 %copy-done = bf16[1,1024,896]{2,1,0:T(8,128)(2,1)S(1)} copy-done((bf16[1,1024,896]{2,1,0:T(8,128)(2,1)S(1)}, bf16[1,1024,896]{2,1,0:T(8,128)(2,1)}, u32[]{:S(2)}) %copy-start) | copy-done | bytes 1835032
  43.3 0.7 forward.1.outputs_ref
  44.0 0.0 copy-start.4
  44.1 0.0 collective-permute-done
  44.1 7.7 %all_gather.7._.twin_hidden_ref = bf16[256,1024]{1,0:T(8,128)(2,1)S(1)} all-gather(bf16[256,256]{1,0:T(8,128)(2,1)S(1)} %collective-permute-done), channel_id=1, replica_groups=mesh['ep'=128,'rep'=4] {'rep'}, dimensions={1}, use_global_device_ids=true | all-gather | bytes 655360 | tf_op jit(solution)/shard_map/all_gather | solution.py:129
  51.7 5.1 %all-to-all-done.arrived_ref = bf16[128,2,896]{2,1,0:T(2,128)(2,1)S(1)} async-done(((bf16[128,2,896]{2,1,0:T(2,128)(2,1)}), bf16[128,2,896]{2,1,0:T(2,128)(2,1)S(1)}, u32[]{:S(2)}, u32[]{:S(2)}) %all-to-all-start) | async-done | bytes 458784 | tf_op jit(solution)/shard_map/all_to_all | solution.py:120
  56.8 0.4 dots.1
  57.2 14.3 %psum.7._ = f32[128,2]{1,0:T(8,128)} all-reduce(f32[128,2]{1,0:T(8,128)S(1)} %dots.1), channel_id=1, replica_groups=mesh['ep'=128,'rep'=4] {'rep'}, use_global_device_ids=true, to_apply=%region_0.0 | all-reduce | flops 256 | bytes 2048 | tf_op jit(solution)/shard_map/psum | solution.py:148
  71.4 0.1 matrix.1.rows_ref
  71.5 1.9 %collective-permute-start.1 = (bf16[256,896]{1,0:T(8,128)(2,1)S(1)}, bf16[256,896]{1,0:T(8,128)(2,1)S(1)}, u32[]{:S(2)}, u32[]{:S(2)}) collective-permute-start(bf16[256,896]{1,0:T(8,128)(2,1)S(1)} %matrix.1.rows_ref), channel_id=1, source_target_pairs={{0,256},{4,260},{8,264},{12,268},{16,272},{20,276},{24,280},{28,28... | collective-permute-start | bytes 1376264 | tf_op jit(solution)/shard_map/ppermute | solution.py:159
  73.4 0.0 copy-start.2
  73.5 0.0 copy-start.3
  73.5 0.0 copy-done.4
  73.5 0.7 fusion
  75.4 9.8 %all-to-all-start.1 = ((f32[128,1,2]{2,1,0:T(1,128)}), f32[128,1,2]{2,1,0:T(1,128)S(1)}, u32[]{:S(2)}, u32[]{:S(2)}) async-start(f32[128,1,2]{2,1,0:T(1,128)} %bitcast.8), calls=%async_computation.1 | async-start | bytes 131072 | tf_op jit(solution)/shard_map/all_to_all | solution.py:149
  85.2 0.5 collective-permute-done.1.twin_rows_ref
  85.7 3.1 %down_grad.1 = (bf16[1024,896]{1,0:T(8,128)(2,1)}, f32[8,128]{1,0:T(8,128)S(1)}) custom-call(s32[1,1]{1,0:T(1,128)} %bitcast.shared_ref, bf16[256,1024]{1,0:T(8,128)(2,1)S(1)} %all_gather.6.hidden_ref, bf16[256,1024]{1,0:T(8,128)(2,1)S(1)} %all_gather.7._.twin_hidden_ref, bf16[256,896]{1,0:T(8,128)(2,1)S(1)} %matrix.1.rows_ref, ...), custom_call_target="tpu_custom_call" | custom-call | flops 939524096 | bytes 3670016 | tf_op jit(solution)/shard_map/down_grad/pallas_call | solution.py:166
  88.8 12.3 %all-to-all-done.1 = f32[128,1,2]{2,1,0:T(1,128)S(1)} async-done(((f32[128,1,2]{2,1,0:T(1,128)}), f32[128,1,2]{2,1,0:T(1,128)S(1)}, u32[]{:S(2)}, u32[]{:S(2)}) %all-to-all-start.1) | async-done | bytes 1056 | tf_op jit(solution)/shard_map/all_to_all | solution.py:149
  101.1 0.0 copy-done.2
  101.1 0.0 copy-done.3
  101.1 0.8 pick.1
Async XLA Ops:
  2.8 54.0 %all-to-all-start = ((bf16[128,2,896]{2,1,0:T(2,128)(2,1)}), bf16[128,2,896]{2,1,0:T(2,128)(2,1)S(1)}, u32[]{:S(2)}, u32[]{:S(2)}) async-start(bf16[128,2,896]{2,1,0:T(2,128)(2,1)} %get-tuple-element.6), calls=%async_computation | async-start | bytes 917504 | tf_op jit(solution)/shard_map/all_to_all | solution.py:120
  25.8 1.0 copy-start.1
  27.4 16.6 %collective-permute-start = (bf16[256,256]{1,0:T(8,128)(2,1)S(1)}, bf16[256,256]{1,0:T(8,128)(2,1)S(1)}, u32[]{:S(2)}, u32[]{:S(2)}) collective-permute-start(bf16[256,256]{1,0:T(8,128)(2,1)S(1)} %hidden.1), channel_id=1, source_target_pairs={{0,256},{4,260},{8,264},{12,268},{16,272},{20,276},{24,280},{28,28... | collective-permute-start | bytes 393224 | tf_op jit(solution)/shard_map/ppermute | solution.py:127
  41.8 1.5 %copy-start = (bf16[1,1024,896]{2,1,0:T(8,128)(2,1)S(1)}, bf16[1,1024,896]{2,1,0:T(8,128)(2,1)}, u32[]{:S(2)}) copy-start(bf16[1,1024,896]{2,1,0:T(8,128)(2,1)} %param.13) | copy-start | bytes 5505028
  44.0 29.4 %copy-start.4 = (s32[128]{0:T(128)S(1)}, s32[128]{0:T(128)}, u32[]{:S(2)}) copy-start(s32[128]{0:T(128)} %param.10) | copy-start | bytes 1540
  71.5 14.2 %collective-permute-start.1 = (bf16[256,896]{1,0:T(8,128)(2,1)S(1)}, bf16[256,896]{1,0:T(8,128)(2,1)S(1)}, u32[]{:S(2)}, u32[]{:S(2)}) collective-permute-start(bf16[256,896]{1,0:T(8,128)(2,1)S(1)} %matrix.1.rows_ref), channel_id=1, source_target_pairs={{0,256},{4,260},{8,264},{12,268},{16,272},{20,276},{24,280},{28,28... | collective-permute-start | bytes 1376264 | tf_op jit(solution)/shard_map/ppermute | solution.py:159
  73.4 27.7 %copy-start.2 = (f32[32,4]{0,1:T(4,128)S(1)}, f32[32,4]{0,1:T(4,128)}, u32[]{:S(2)}) copy-start(f32[32,4]{0,1:T(4,128)} %param.8) | copy-start | bytes 1540
  73.5 27.7 %copy-start.3 = (s32[4,32]{1,0:T(4,128)S(1)}, s32[4,32]{1,0:T(4,128)}, u32[]{:S(2)}) copy-start(s32[4,32]{1,0:T(4,128)} %get-tuple-element.8.target_ref) | copy-start | bytes 1540
  75.4 25.7 %all-to-all-start.1 = ((f32[128,1,2]{2,1,0:T(1,128)}), f32[128,1,2]{2,1,0:T(1,128)S(1)}, u32[]{:S(2)}, u32[]{:S(2)}) async-start(f32[128,1,2]{2,1,0:T(1,128)} %bitcast.8), calls=%async_computation.1 | async-start | bytes 131072 | tf_op jit(solution)/shard_map/all_to_all | solution.py:149

commit v3 on v2

--- a/solution.py
+++ b/solution.py
@@ -84,12 +84,15 @@
         out_ref[k : k + 1, :] = jnp.sum(found, axis=0, keepdims=True) / weight
 
 
-def grad_kernel(shared_ref, hidden_ref, twin_hidden_ref, rows_ref, twin_rows_ref, out_ref, order_ref):
+def grad_kernel(slot_expert_ref, hidden_ref, twin_hidden_ref, rows_ref, twin_rows_ref, out_ref, order_ref):
     over_rows = (((0,), (0,)), ((), ()))
     own = lax.dot_general(
         hidden_ref[...], rows_ref[...], over_rows, preferred_element_type=jnp.float32
     )
-    twin_rows = jnp.where(shared_ref[0, 0] > 0, twin_rows_ref[...], jnp.zeros((), jnp.bfloat16))
+    me = lax.axis_index("ep")
+    slots = slot_expert_ref.shape[0]
+    shared = slot_expert_ref[me] == slot_expert_ref[lax.rem(me + slots // 2, slots)]
+    twin_rows = jnp.where(shared, twin_rows_ref[...], jnp.zeros((), jnp.bfloat16))
     twin = lax.dot_general(
         twin_hidden_ref[...], twin_rows, over_rows, preferred_element_type=jnp.float32
     )
@@ -145,7 +148,6 @@
         compiler_params=pltpu.CompilerParams(vmem_limit_bytes=8 << 20),
         name="dots",
     )(arrived, outputs, twin_hidden)
-    dots = lax.psum(dots, "rep")
     returned = lax.all_to_all(
         dots.reshape(sources, 1, pair_rows), "ep", split_axis=0, concat_axis=0, tiled=True
     )
@@ -157,10 +159,6 @@
         name="matrix",
     )(arrived, dots)
     twin_rows = lax.ppermute(rows, "ep", swap)
-    me = lax.axis_index("ep")
-    own_expert = lax.dynamic_slice(slot_expert, (me,), (1,))
-    twin_expert = lax.dynamic_slice(slot_expert, ((me + half) % slot_count,), (1,))
-    shared = (own_expert == twin_expert).astype(jnp.int32).reshape(1, 1)
     steps = 4
     block = hidden_units // steps
     down_grad, order = pl.pallas_call(
@@ -181,22 +179,17 @@
             jax.ShapeDtypeStruct((hidden_units, features), jnp.bfloat16),
             jax.ShapeDtypeStruct((8, 128), jnp.float32),
         ),
-        cost_estimate=pl.CostEstimate(
-            flops=4 * rows_total * hidden_units * features,
-            bytes_accessed=4 * hidden_units * features,
-            transcendentals=0,
-        ),
         compiler_params=pltpu.CompilerParams(vmem_limit_bytes=16 << 20),
         name="down_grad",
-    )(shared, hidden, twin_hidden, rows, twin_rows)
-    route_grad = pl.pallas_call(
+    )(slot_expert, hidden, twin_hidden, rows, twin_rows)
+    route_part = pl.pallas_call(
         pick_kernel,
         in_specs=[pl.BlockSpec(memory_space=pltpu.VMEM)] * 3 + [pl.BlockSpec(memory_space=pl.ANY)],
         out_shape=jax.ShapeDtypeStruct((top_count, token_count), jnp.float32),
         compiler_params=pltpu.CompilerParams(vmem_limit_bytes=4 << 20),
         name="pick",
-    )(returned.reshape(slot_count, pair_rows), target, weight_t, order).T
-    return (down_grad[None], route_grad)
+    )(returned.reshape(slot_count, pair_rows), target, weight_t, order)
+    return (down_grad[None], lax.psum(route_part, "rep").T)
 
 
 def solution(mesh):

time: 103 us -> 96.9 us (0.941)
  blocking collectives: 32 us -> 25.6 us
  starting transfers between devices: 38.9 us -> 42 us
  between operations: 2.02 us -> 0.72 us
    psum x1, blocking collectives: 14.3 us -> 7.86 us  [on_device(): return (down_grad[None], lax.psum(route_part, 'rep').T)]
    all_to_all x1, starting transfers between devices: 9.76 us -> 12.8 us  [on_device(): lax.all_to_all(dots.reshape(sources, 1, pair_rows), 'ep', split_axis=0, c...]
  transfers between devices with their start and end apart: 4 -> 4, of which waited for: 3 -> 2; matrix products, arithmetic and copies ran while one was open for 1% -> 0% of each run, Pallas kernels for 4% -> 5%
where the time goes in v3:
time: 96.9 us; the launch traced here: 96.5 us
  starting transfers between devices  42 us (43%)
  blocking collectives  25.6 us (26%)
  waiting for transfers between devices  17.2 us (18%)
  Pallas kernels  8.44 us (9%)
  local copies, waits for them, and re-layouts  2.46 us (3%)
    all_to_all x1, starting transfers between devices, on_device(): lax.all_to_all(send_rows, 'ep', split_axis=0, concat_axis=0, tiled=True)  23 us
    all_to_all x1, starting transfers between devices, on_device(): lax.all_to_all(dots.reshape(sources, 1, pair_rows), 'ep', split_axis=0, c...  12.8 us
    all_to_all x1, waiting for transfers between devices, on_device(): lax.all_to_all(dots.reshape(sources, 1, pair_rows), 'ep', split_axis=0, c...  12.1 us
    all_gather x1, blocking collectives, on_device(): hidden = lax.all_gather(part, 'rep', axis=1, tiled=True)  10.1 us
    psum x1, blocking collectives, on_device(): return (down_grad[None], lax.psum(route_part, 'rep').T)  7.86 us
    all_gather x1, blocking collectives, on_device(): twin_hidden = lax.all_gather(twin_part, 'rep', axis=1, tiled=True)  7.66 us
    all_to_all x1, waiting for transfers between devices, on_device(): lax.all_to_all(send_rows, 'ep', split_axis=0, concat_axis=0, tiled=True)  5.09 us
    ppermute x1, starting transfers between devices, on_device(): twin_part = lax.ppermute(part, 'ep', swap)  4.3 us
  transfers between devices with their start and end apart: 4, of which 2 were waited for; matrix products, arithmetic and copies ran while one was open for 0% of the time, Pallas kernels for 5%

profile of v3, /device:TPU:1, one launch (start us, length us, event | category | flops | bytes accessed | tf_op | source)
XLA Modules:
  0.0 96.5 jit_solution(15187625128807079295)
XLA Ops:
  0.6 2.2 %pack.1 = (bf16[128,2,896]{2,1,0:T(2,128)(2,1)}, s32[4,32]{1,0:T(4,128)}) custom-call(s32[4,32]{1,0:T(4,128)} %bitcast.18, f32[4,32]{1,0:T(4,128)} %bitcast.14, s32[1,128]{1,0:T(1,128)} %bitcast.17, s32[1,96]{1,0:T(1,128)} %pick_ref.1, bf16[32,896]{1,0:T(8,128)(2,1)} %grad_ref.1), custom_call_target="tpu_custom_call" | custom-call | tf_op jit(solution)/shard_map/pack/pallas_call | solution.py:115
  2.8 23.0 %all-to-all-start = ((bf16[128,2,896]{2,1,0:T(2,128)(2,1)}), bf16[128,2,896]{2,1,0:T(2,128)(2,1)S(1)}, u32[]{:S(2)}, u32[]{:S(2)}) async-start(bf16[128,2,896]{2,1,0:T(2,128)(2,1)} %get-tuple-element.6), calls=%async_computation | async-start | bytes 917504 | tf_op jit(solution)/shard_map/all_to_all | solution.py:123
  25.8 0.0 copy-start.1
  25.8 0.9 copy-done.1
  26.8 0.7 hidden.1
  27.4 4.3 %collective-permute-start = (bf16[256,256]{1,0:T(8,128)(2,1)S(1)}, bf16[256,256]{1,0:T(8,128)(2,1)S(1)}, u32[]{:S(2)}, u32[]{:S(2)}) collective-permute-start(bf16[256,256]{1,0:T(8,128)(2,1)S(1)} %hidden.1), channel_id=1, source_target_pairs={{0,256},{4,260},{8,264},{12,268},{16,272},{20,276},{24,280},{28,28... | collective-permute-start | bytes 393224 | tf_op jit(solution)/shard_map/ppermute | solution.py:130
  31.7 10.1 %all_gather.6.hidden_ref = bf16[256,1024]{1,0:T(8,128)(2,1)S(1)} all-gather(bf16[256,256]{1,0:T(8,128)(2,1)S(1)} %hidden.1), channel_id=1, replica_groups=mesh['ep'=128,'rep'=4] {'rep'}, dimensions={1}, use_global_device_ids=true | all-gather | bytes 655360 | tf_op jit(solution)/shard_map/all_gather | solution.py:131
  41.8 0.0 copy-start
  41.8 1.5 %copy-done = bf16[1,1024,896]{2,1,0:T(8,128)(2,1)S(1)} copy-done((bf16[1,1024,896]{2,1,0:T(8,128)(2,1)S(1)}, bf16[1,1024,896]{2,1,0:T(8,128)(2,1)}, u32[]{:S(2)}) %copy-start) | copy-done | bytes 1835032
  43.3 0.7 forward.1.outputs_ref
  44.0 0.0 copy-start.3
  44.0 0.0 collective-permute-done
  44.1 7.7 %all_gather.7._.twin_hidden_ref = bf16[256,1024]{1,0:T(8,128)(2,1)S(1)} all-gather(bf16[256,256]{1,0:T(8,128)(2,1)S(1)} %collective-permute-done), channel_id=1, replica_groups=mesh['ep'=128,'rep'=4] {'rep'}, dimensions={1}, use_global_device_ids=true | all-gather | bytes 655360 | tf_op jit(solution)/shard_map/all_gather | solution.py:132
  51.7 5.1 %all-to-all-done.arrived_ref = bf16[128,2,896]{2,1,0:T(2,128)(2,1)S(1)} async-done(((bf16[128,2,896]{2,1,0:T(2,128)(2,1)}), bf16[128,2,896]{2,1,0:T(2,128)(2,1)S(1)}, u32[]{:S(2)}, u32[]{:S(2)}) %all-to-all-start) | async-done | bytes 458784 | tf_op jit(solution)/shard_map/all_to_all | solution.py:123
  56.8 1.0 %dots.1._ = f32[128,2]{1,0:T(8,128)} custom-call(bf16[128,2,896]{2,1,0:T(2,128)(2,1)S(1)} %all-to-all-done.arrived_ref, f32[256,896]{1,0:T(8,128)S(1)} %forward.1.outputs_ref, bf16[256,1024]{1,0:T(8,128)(2,1)S(1)} %all_gather.7._.twin_hidden_ref), custom_call_target="tpu_custom_call" | custom-call | tf_op jit(solution)/shard_map/dots/pallas_call | solution.py:139
  57.8 0.0 copy-start.2
  57.8 0.0 copy-start.4
  57.8 0.1 matrix.1.rows_ref
  57.9 1.9 %collective-permute-start.1 = (bf16[256,896]{1,0:T(8,128)(2,1)S(1)}, bf16[256,896]{1,0:T(8,128)(2,1)S(1)}, u32[]{:S(2)}, u32[]{:S(2)}) collective-permute-start(bf16[256,896]{1,0:T(8,128)(2,1)S(1)} %matrix.1.rows_ref), channel_id=1, source_target_pairs={{0,256},{4,260},{8,264},{12,268},{16,272},{20,276},{24,280},{28,28... | collective-permute-start | bytes 1376264 | tf_op jit(solution)/shard_map/ppermute | solution.py:161
  59.8 12.8 %all-to-all-start.1 = ((f32[128,1,2]{2,1,0:T(1,128)}), f32[128,1,2]{2,1,0:T(1,128)S(1)}, u32[]{:S(2)}, u32[]{:S(2)}) async-start(f32[128,1,2]{2,1,0:T(1,128)} %bitcast.7), calls=%async_computation.1 | async-start | bytes 131072 | tf_op jit(solution)/shard_map/all_to_all | solution.py:151
  72.7 0.0 collective-permute-done.1.twin_rows_ref
  72.7 0.0 copy-done.3
  72.7 3.6 %down_grad.1 = (bf16[1024,896]{1,0:T(8,128)(2,1)}, f32[8,128]{1,0:T(8,128)S(1)}) custom-call(s32[128]{0:T(128)S(1)} %copy-done.3, bf16[256,1024]{1,0:T(8,128)(2,1)S(1)} %all_gather.6.hidden_ref, bf16[256,1024]{1,0:T(8,128)(2,1)S(1)} %all_gather.7._.twin_hidden_ref, bf16[256,896]{1,0:T(8,128)(2,1)S(1)} %matrix.1.rows_ref, ...), custom_call_target="tpu_custom_call" | custom-call | tf_op jit(solution)/shard_map/down_grad/pallas_call | solution.py:164
  76.3 12.1 %all-to-all-done.1 = f32[128,1,2]{2,1,0:T(1,128)S(1)} async-done(((f32[128,1,2]{2,1,0:T(1,128)}), f32[128,1,2]{2,1,0:T(1,128)S(1)}, u32[]{:S(2)}, u32[]{:S(2)}) %all-to-all-start.1) | async-done | bytes 1056 | tf_op jit(solution)/shard_map/all_to_all | solution.py:151
  88.4 0.0 copy-done.2
  88.4 0.0 copy-done.4
  88.4 0.2 pick.1
  88.6 7.9 %psum.7 = f32[32,4]{0,1:T(4,128)} all-reduce(f32[32,4]{0,1:T(4,128)S(1)} %bitcast.16), channel_id=1, replica_groups=mesh['ep'=128,'rep'=4] {'rep'}, use_global_device_ids=true, to_apply=%region_0.0 | all-reduce | flops 128 | bytes 1024 | tf_op jit(solution)/shard_map/psum | solution.py:192
Async XLA Ops:
  2.8 54.0 %all-to-all-start = ((bf16[128,2,896]{2,1,0:T(2,128)(2,1)}), bf16[128,2,896]{2,1,0:T(2,128)(2,1)S(1)}, u32[]{:S(2)}, u32[]{:S(2)}) async-start(bf16[128,2,896]{2,1,0:T(2,128)(2,1)} %get-tuple-element.6), calls=%async_computation | async-start | bytes 917504 | tf_op jit(solution)/shard_map/all_to_all | solution.py:123
  25.8 1.0 copy-start.1
  27.4 16.6 %collective-permute-start = (bf16[256,256]{1,0:T(8,128)(2,1)S(1)}, bf16[256,256]{1,0:T(8,128)(2,1)S(1)}, u32[]{:S(2)}, u32[]{:S(2)}) collective-permute-start(bf16[256,256]{1,0:T(8,128)(2,1)S(1)} %hidden.1), channel_id=1, source_target_pairs={{0,256},{4,260},{8,264},{12,268},{16,272},{20,276},{24,280},{28,28... | collective-permute-start | bytes 393224 | tf_op jit(solution)/shard_map/ppermute | solution.py:130
  41.8 1.5 %copy-start = (bf16[1,1024,896]{2,1,0:T(8,128)(2,1)S(1)}, bf16[1,1024,896]{2,1,0:T(8,128)(2,1)}, u32[]{:S(2)}) copy-start(bf16[1,1024,896]{2,1,0:T(8,128)(2,1)} %param.13) | copy-start | bytes 5505028
  44.0 28.6 %copy-start.3 = (s32[128]{0:T(128)S(1)}, s32[128]{0:T(128)}, u32[]{:S(2)}) copy-start(s32[128]{0:T(128)} %slot_expert_ref.1) | copy-start | bytes 1540
  57.8 30.6 %copy-start.2 = (f32[32,4]{0,1:T(4,128)S(1)}, f32[32,4]{0,1:T(4,128)}, u32[]{:S(2)}) copy-start(f32[32,4]{0,1:T(4,128)} %param.8) | copy-start | bytes 1540
  57.8 30.6 %copy-start.4 = (s32[4,32]{1,0:T(4,128)S(1)}, s32[4,32]{1,0:T(4,128)}, u32[]{:S(2)}) copy-start(s32[4,32]{1,0:T(4,128)} %get-tuple-element.8.target_ref) | copy-start | bytes 1540
  57.9 14.8 %collective-permute-start.1 = (bf16[256,896]{1,0:T(8,128)(2,1)S(1)}, bf16[256,896]{1,0:T(8,128)(2,1)S(1)}, u32[]{:S(2)}, u32[]{:S(2)}) collective-permute-start(bf16[256,896]{1,0:T(8,128)(2,1)S(1)} %matrix.1.rows_ref), channel_id=1, source_target_pairs={{0,256},{4,260},{8,264},{12,268},{16,272},{20,276},{24,280},{28,28... | collective-permute-start | bytes 1376264 | tf_op jit(solution)/shard_map/ppermute | solution.py:161
  59.8 28.6 %all-to-all-start.1 = ((f32[128,1,2]{2,1,0:T(1,128)}), f32[128,1,2]{2,1,0:T(1,128)S(1)}, u32[]{:S(2)}, u32[]{:S(2)}) async-start(f32[128,1,2]{2,1,0:T(1,128)} %bitcast.7), calls=%async_computation.1 | async-start | bytes 131072 | tf_op jit(solution)/shard_map/all_to_all | solution.py:151

commit v4 on v3

--- a/solution.py
+++ b/solution.py
@@ -3,10 +3,15 @@
 from jax import lax
 from jax.experimental import pallas as pl
 from jax.experimental.pallas import tpu as pltpu
-from jax.sharding import PartitionSpec as P
-
-
-def pack_kernel(ids_ref, weight_ref, slot_expert_ref, pick_ref, grad_ref, rows_ref, target_ref):
+from jax.sharding import Mesh, PartitionSpec as P
+
+
+def prepare_kernel(
+    ids_ref, weight_ref, slot_expert_ref, pick_ref, grad_ref, saved_ref, rows_ref, target_ref, hidden_ref
+):
+    gate = saved_ref[:, 0, :].astype(jnp.float32)
+    up = saved_ref[:, 1, :].astype(jnp.float32)
+    hidden_ref[...] = (gate / (1.0 + jnp.exp(-gate)) * up).astype(hidden_ref.dtype)
     top, tokens = ids_ref.shape
     experts = pick_ref.shape[1]
     slots = slot_expert_ref.shape[1]
@@ -45,17 +50,15 @@
     rows_ref[...] = rows.astype(rows_ref.dtype).reshape(rows_ref.shape)
 
 
-def hidden_kernel(saved_ref, out_ref):
-    gate = saved_ref[:, 0, :].astype(jnp.float32)
-    up = saved_ref[:, 1, :].astype(jnp.float32)
-    out_ref[...] = (gate / (1.0 + jnp.exp(-gate)) * up).astype(out_ref.dtype)
-
-
 def forward_kernel(hidden_ref, weight_ref, out_ref):
-    out_ref[...] = jnp.dot(hidden_ref[...], weight_ref[...], preferred_element_type=jnp.float32)
-
-
-def dots_kernel(arrived_ref, outputs_ref, _, dots_ref, scratch):
+    units = weight_ref.shape[0]
+    own = pl.multiple_of(lax.axis_index("half") * units, units)
+    out_ref[...] = jnp.dot(
+        hidden_ref[:, pl.ds(own, units)], weight_ref[...], preferred_element_type=jnp.float32
+    )
+
+
+def dots_kernel(arrived_ref, outputs_ref, dots_ref, scratch):
     rows = arrived_ref[...].reshape(outputs_ref.shape)
     total = jnp.sum(rows.astype(jnp.float32) * outputs_ref[...], axis=1, keepdims=True)
     scratch[...] = jnp.broadcast_to(total, scratch.shape)
@@ -84,52 +87,44 @@
         out_ref[k : k + 1, :] = jnp.sum(found, axis=0, keepdims=True) / weight
 
 
-def grad_kernel(slot_expert_ref, hidden_ref, twin_hidden_ref, rows_ref, twin_rows_ref, out_ref, order_ref):
+def grad_kernel(slot_expert_ref, hidden_ref, twin_hidden_ref, rows_ref, out_ref, order_ref):
     over_rows = (((0,), (0,)), ((), ()))
-    own = lax.dot_general(
-        hidden_ref[...], rows_ref[...], over_rows, preferred_element_type=jnp.float32
-    )
-    me = lax.axis_index("ep")
-    slots = slot_expert_ref.shape[0]
-    shared = slot_expert_ref[me] == slot_expert_ref[lax.rem(me + slots // 2, slots)]
-    twin_rows = jnp.where(shared, twin_rows_ref[...], jnp.zeros((), jnp.bfloat16))
-    twin = lax.dot_general(
-        twin_hidden_ref[...], twin_rows, over_rows, preferred_element_type=jnp.float32
-    )
-    out_ref[...] = (own + twin).astype(out_ref.dtype)
+    half = lax.axis_index("half")
+    place = lax.axis_index("place")
+    shared = slot_expert_ref[place] == slot_expert_ref[place + slot_expert_ref.shape[0] // 2]
+    count = hidden_ref.shape[0]
+    total = jnp.zeros(out_ref.shape, jnp.float32)
+    for part, ref in enumerate((hidden_ref, twin_hidden_ref)):
+        rows = rows_ref[part * count : (part + 1) * count, :]
+        rows = jnp.where(shared | (half == part), rows, jnp.zeros((), rows.dtype))
+        total += lax.dot_general(ref[...], rows, over_rows, preferred_element_type=jnp.float32)
+    out_ref[...] = total.astype(out_ref.dtype)
     order_ref[...] = jnp.zeros_like(order_ref)
 
 
 def on_device(out_grad, route_weight, expert_ids, slot_expert, replica_pick, saved_gu, down_weight):
-    sources = lax.axis_size("ep")
+    ep = ("half", "place")
+    sources = lax.axis_size(ep)
     token_count, top_count = expert_ids.shape
     slot_count = slot_expert.shape[0]
     rows_total = saved_gu.shape[1]
     pair_rows = rows_total // sources
     features = out_grad.shape[1]
     hidden_units = down_weight.shape[1]
-    half = slot_count // 2
-    swap = [(i, (i + half) % slot_count) for i in range(slot_count)]
     ids_t = expert_ids.T
     weight_t = route_weight.T
-    send_rows, target = pl.pallas_call(
-        pack_kernel,
+    send_rows, target, part = pl.pallas_call(
+        prepare_kernel,
         out_shape=(
             jax.ShapeDtypeStruct((slot_count, pair_rows, features), jnp.bfloat16),
             jax.ShapeDtypeStruct((top_count, token_count), jnp.int32),
+            jax.ShapeDtypeStruct((rows_total, saved_gu.shape[3]), jnp.bfloat16),
         ),
-        name="pack",
-    )(ids_t, weight_t, slot_expert[None], replica_pick, out_grad)
-    arrived = lax.all_to_all(send_rows, "ep", split_axis=0, concat_axis=0, tiled=True)
-    part = pl.pallas_call(
-        hidden_kernel,
-        out_shape=jax.ShapeDtypeStruct((rows_total, saved_gu.shape[3]), jnp.bfloat16),
-        compiler_params=pltpu.CompilerParams(vmem_limit_bytes=8 << 20),
-        name="hidden",
-    )(saved_gu[0])
-    twin_part = lax.ppermute(part, "ep", swap)
-    hidden = lax.all_gather(part, "rep", axis=1, tiled=True)
-    twin_hidden = lax.all_gather(twin_part, "rep", axis=1, tiled=True)
+
+        name="prepare",
+    )(ids_t, weight_t, slot_expert[None], replica_pick, out_grad, saved_gu[0])
+    arrived = lax.all_to_all(send_rows, ep, split_axis=0, concat_axis=0, tiled=True)
+    hidden = lax.all_gather(part, ("half", "rep"), axis=1, tiled=True)
     outputs = pl.pallas_call(
         forward_kernel,
         out_shape=pltpu.VMEM((rows_total, features), jnp.float32),
@@ -138,18 +133,14 @@
     )(hidden, down_weight[0])
     dots = pl.pallas_call(
         dots_kernel,
-        in_specs=[
-            pl.BlockSpec(memory_space=pltpu.VMEM),
-            pl.BlockSpec(memory_space=pltpu.VMEM),
-            pl.BlockSpec(memory_space=pl.ANY),
-        ],
+        in_specs=[pl.BlockSpec(memory_space=pltpu.VMEM)] * 2,
         out_shape=jax.ShapeDtypeStruct((sources, pair_rows), jnp.float32),
         scratch_shapes=[pltpu.VMEM((rows_total, 128), jnp.float32)],
         compiler_params=pltpu.CompilerParams(vmem_limit_bytes=8 << 20),
         name="dots",
-    )(arrived, outputs, twin_hidden)
+    )(arrived, outputs)
     returned = lax.all_to_all(
-        dots.reshape(sources, 1, pair_rows), "ep", split_axis=0, concat_axis=0, tiled=True
+        dots.reshape(sources, 1, pair_rows), ep, split_axis=0, concat_axis=0, tiled=True
     )
     rows = pl.pallas_call(
         matrix_kernel,
@@ -158,7 +149,7 @@
         compiler_params=pltpu.CompilerParams(vmem_limit_bytes=8 << 20),
         name="matrix",
     )(arrived, dots)
-    twin_rows = lax.ppermute(rows, "ep", swap)
+    rows = lax.all_gather(rows, "half", axis=0, tiled=True)
     steps = 4
     block = hidden_units // steps
     down_grad, order = pl.pallas_call(
@@ -167,9 +158,8 @@
         in_specs=[
             pl.BlockSpec(memory_space=pltpu.SMEM),
             pl.BlockSpec((rows_total, block), lambda i: (0, i)),
-            pl.BlockSpec((rows_total, block), lambda i: (0, i)),
-            pl.BlockSpec((rows_total, features), lambda i: (0, 0)),
-            pl.BlockSpec((rows_total, features), lambda i: (0, 0)),
+            pl.BlockSpec((rows_total, block), lambda i: (0, i + steps)),
+            pl.BlockSpec((2 * rows_total, features), lambda i: (0, 0)),
         ],
         out_specs=(
             pl.BlockSpec((block, features), lambda i: (i, 0)),
@@ -181,7 +171,7 @@
         ),
         compiler_params=pltpu.CompilerParams(vmem_limit_bytes=16 << 20),
         name="down_grad",
-    )(slot_expert, hidden, twin_hidden, rows, twin_rows)
+    )(slot_expert, hidden, hidden, rows)
     route_part = pl.pallas_call(
         pick_kernel,
         in_specs=[pl.BlockSpec(memory_space=pltpu.VMEM)] * 3 + [pl.BlockSpec(memory_space=pl.ANY)],
@@ -193,19 +183,22 @@
 
 
 def solution(mesh):
+    ep, rep = mesh.shape["ep"], mesh.shape["rep"]
+    halves = Mesh(mesh.devices.reshape(2, ep // 2, rep), ("half", "place", "rep"))
+    ep = ("half", "place")
     placed = (
-        P("ep", "rep"),
-        P("ep", None),
-        P("ep", None),
+        P(ep, "rep"),
+        P(ep, None),
+        P(ep, None),
         P(),
-        P("ep", None),
-        P("ep", None, None, "rep"),
-        P("ep", None, "rep"),
+        P(ep, None),
+        P(ep, None, None, "rep"),
+        P(ep, None, "rep"),
     )
     return jax.shard_map(
         on_device,
-        mesh=mesh,
+        mesh=halves,
         in_specs=placed,
-        out_specs=(P("ep", None, "rep"), P("ep", None)),
+        out_specs=(P(ep, None, "rep"), P(ep, None)),
         check_vma=False,
     )

time: 96.9 us -> 106 us (1.094)
  between operations: 0.72 us -> 14.1 us
  starting transfers between devices: 42 us -> 30.8 us
  waiting for transfers between devices: 17.2 us -> 27.6 us
  blocking collectives: 25.6 us -> 21.3 us
    all_gather x0 -> x1, waiting for transfers between devices: none -> 14.4 us  [on_device(): hidden = lax.all_gather(part, ('half', 'rep'), axis=1, tiled=True)]
    ppermute x2 -> x0, starting transfers between devices: 6.22 us -> none  [the longest x1 4.3 us: on_device(): twin_part = lax.ppermute(part, 'ep', swap)]
    all_gather x2 -> x1, blocking collectives: 17.7 us -> 12.5 us  [on_device(): rows = lax.all_gather(rows, 'half', axis=0, tiled=True)]
    all_to_all x2, starting transfers between devices: 35.8 us -> 30.8 us  [the longest x1 23 us: on_device(): lax.all_to_all(send_rows, ep, split_axis=0, concat_axis=0, tiled=True)]
    all_to_all x2, waiting for transfers between devices: 17.2 us -> 13.1 us  [the longest x1 13.1 us: on_device(): lax.all_to_all(send_rows, ep, split_axis=0, concat_axis=0, tiled=True)]
    pallas_call x2 -> x1, Pallas kernels: 2.86 us -> 3.16 us  [on_device(): pl.pallas_call(prepare_kernel, out_shape=(jax.ShapeDtypeStruct((slot_coun...]
    unnamed x10 -> x12, local copies, waits for them, and re-layouts: 2.46 us -> 2.74 us
  transfers between devices with their start and end apart: 4 -> 3, of which waited for: 2 -> 2; matrix products, arithmetic and copies ran while one was open for 0% -> 0% of each run, Pallas kernels for 5% -> 4%
where the time goes in v4:
time: 106 us; the launch traced here: 105 us
  starting transfers between devices  30.8 us (29%)
  waiting for transfers between devices  27.6 us (26%)
  blocking collectives  21.3 us (20%)
  between operations  14.1 us (13%)
  Pallas kernels  8.96 us (8%)
  local copies, waits for them, and re-layouts  2.74 us (3%)
    all_to_all x1, starting transfers between devices, on_device(): lax.all_to_all(send_rows, ep, split_axis=0, concat_axis=0, tiled=True)  23 us
    all_gather x1, waiting for transfers between devices, on_device(): hidden = lax.all_gather(part, ('half', 'rep'), axis=1, tiled=True)  14.4 us
    all_to_all x1, waiting for transfers between devices, on_device(): lax.all_to_all(send_rows, ep, split_axis=0, concat_axis=0, tiled=True)  13.1 us
    all_gather x1, blocking collectives, on_device(): rows = lax.all_gather(rows, 'half', axis=0, tiled=True)  12.5 us
    psum x1, blocking collectives, on_device(): return (down_grad[None], lax.psum(route_part, 'rep').T)  8.84 us
    all_to_all x1, starting transfers between devices, on_device(): lax.all_to_all(dots.reshape(sources, 1, pair_rows), ep, split_axis=0, con...  7.78 us
    pallas_call x1, Pallas kernels, on_device(): pl.pallas_call(grad_kernel, grid=(steps,), in_specs=[pl.BlockSpec(memory_...  3.81 us
    pallas_call x1, Pallas kernels, on_device(): pl.pallas_call(prepare_kernel, out_shape=(jax.ShapeDtypeStruct((slot_coun...  3.16 us
  transfers between devices with their start and end apart: 3, of which 2 were waited for; matrix products, arithmetic and copies ran while one was open for 0% of the time, Pallas kernels for 4%

profile of v4, /device:TPU:1, one launch (start us, length us, event | category | flops | bytes accessed | tf_op | source)
XLA Modules:
  0.0 105.5 jit_solution(15633306507805499336)
XLA Ops:
  7.2 0.0 all-gather.2.cloned.1.call-start
  7.2 3.2 %prepare.1 = (bf16[128,2,896]{2,1,0:T(2,128)(2,1)}, s32[4,32]{1,0:T(4,128)}, bf16[256,256]{1,0:T(8,128)(2,1)}) custom-call(s32[4,32]{1,0:T(4,128)} %bitcast.18, f32[4,32]{1,0:T(4,128)} %bitcast.13, s32[1,128]{1,0:T(1,128)} %bitcast.16, s32[1,96]{1,0:T(1,128)} %pick_ref.1, bf16[32,896]{1,0:T(8,128)(2,1)} %grad_ref.1, bf16[256,2,256]{2,1,0:T(2,128)(2,1)} %bitcast.17), custom_call_target="tpu_custom_call" | custom-call | tf_op jit(solution)/shard_map/prepare/pallas_call | solution.py:116
  10.4 0.0 all-gather.2.cloned.1.call-update
  10.4 23.0 %all-to-all-start = ((bf16[128,2,896]{2,1,0:T(2,128)(2,1)}), bf16[128,2,896]{2,1,0:T(2,128)(2,1)S(1)}, u32[]{:S(2)}, u32[]{:S(2)}) async-start(bf16[128,2,896]{2,1,0:T(2,128)(2,1)} %get-tuple-element.8), calls=%async_computation | async-start | bytes 917504 | tf_op jit(solution)/shard_map/all_to_all | solution.py:126
  33.4 14.4 %all-gather.2.cloned.1.call-done.hidden_ref.twin_hidden_ref = bf16[256,2048]{1,0:T(8,128)(2,1)} async-done(((bf16[256,256]{1,0:T(8,128)(2,1)}), bf16[256,2048]{1,0:T(8,128)(2,1)}) %all-gather.2.cloned.1.call-update) | async-done | bytes 1048592 | tf_op jit(solution)/shard_map/all_gather | solution.py:127
  47.8 0.0 copy-start
  47.8 1.2 %copy-done = bf16[256,2048]{1,0:T(8,128)(2,1)S(1)} copy-done((bf16[256,2048]{1,0:T(8,128)(2,1)S(1)}, bf16[256,2048]{1,0:T(8,128)(2,1)}, u32[]{:S(2)}) %copy-start) | copy-done | bytes 1048600
  49.0 0.0 copy-start.2
  49.0 1.5 %copy-done.2 = bf16[1,1024,896]{2,1,0:T(8,128)(2,1)S(1)} copy-done((bf16[1,1024,896]{2,1,0:T(8,128)(2,1)S(1)}, bf16[1,1024,896]{2,1,0:T(8,128)(2,1)}, u32[]{:S(2)}) %copy-start.2) | copy-done | bytes 1835032
  50.5 0.7 forward.1.outputs_ref
  51.2 0.0 copy-start.1
  51.2 0.0 copy-start.4
  51.3 13.1 %all-to-all-done.arrived_ref = bf16[128,2,896]{2,1,0:T(2,128)(2,1)S(1)} async-done(((bf16[128,2,896]{2,1,0:T(2,128)(2,1)}), bf16[128,2,896]{2,1,0:T(2,128)(2,1)S(1)}, u32[]{:S(2)}, u32[]{:S(2)}) %all-to-all-start) | async-done | bytes 458784 | tf_op jit(solution)/shard_map/all_to_all | solution.py:126
  64.4 1.0 dots.1._
  65.4 7.8 %all-to-all-start.1 = ((f32[128,1,2]{2,1,0:T(1,128)}), f32[128,1,2]{2,1,0:T(1,128)S(1)}, u32[]{:S(2)}, u32[]{:S(2)}) async-start(f32[128,1,2]{2,1,0:T(1,128)} %bitcast.7), calls=%async_computation.1 | async-start | bytes 131072 | tf_op jit(solution)/shard_map/all_to_all | solution.py:142
  73.2 0.1 matrix.1
  73.2 12.5 %all_gather.7.rows_ref = bf16[512,896]{1,0:T(8,128)(2,1)S(1)} all-gather(bf16[256,896]{1,0:T(8,128)(2,1)S(1)} %matrix.1), channel_id=1, replica_groups=mesh['half'=2,'place'=64,'rep'=4] {'half'}, dimensions={0}, use_global_device_ids=true | all-gather | bytes 1376256 | tf_op jit(solution)/shard_map/all_gather | solution.py:152
  85.7 0.0 copy-done.1
  85.7 0.0 copy-done.4
  85.7 0.0 copy-start.3
  85.7 0.0 copy-start.5
  85.7 3.8 %down_grad.1 = (bf16[1024,896]{1,0:T(8,128)(2,1)}, f32[8,128]{1,0:T(8,128)S(1)}) custom-call(s32[128]{0:T(128)S(1)} %copy-done.4, bf16[256,2048]{1,0:T(8,128)(2,1)S(1)} %copy-done.1, bf16[256,2048]{1,0:T(8,128)(2,1)S(1)} %copy-done.1, bf16[512,896]{1,0:T(8,128)(2,1)S(1)} %all_gather.7.rows_ref), custom_call_target="tpu_custom_call" | custom-call | tf_op jit(solution)/shard_map/down_grad/pallas_call | solution.py:155
  89.5 0.0 all-to-all-done.1
  89.5 0.0 copy-done.3
  89.5 0.0 copy-done.5
  89.5 0.2 pick.1
  89.8 8.8 %psum.7 = f32[32,4]{0,1:T(4,128)} all-reduce(f32[32,4]{0,1:T(4,128)S(1)} %bitcast.15), channel_id=1, replica_groups=mesh['half'=2,'place'=64,'rep'=4] {'rep'}, use_global_device_ids=true, to_apply=%region_0.0 | all-reduce | flops 128 | bytes 1024 | tf_op jit(solution)/shard_map/psum | solution.py:182
Async XLA Ops:
  7.2 40.6 %all-gather.2.cloned.1.call-start = ((), (), s32[]{:S(2)}) async-start(), calls=%async_computation.2 | async-start | bytes 1179648 | tf_op jit(solution)/shard_map/all_gather | solution.py:127
  10.4 54.0 %all-to-all-start = ((bf16[128,2,896]{2,1,0:T(2,128)(2,1)}), bf16[128,2,896]{2,1,0:T(2,128)(2,1)S(1)}, u32[]{:S(2)}, u32[]{:S(2)}) async-start(bf16[128,2,896]{2,1,0:T(2,128)(2,1)} %get-tuple-element.8), calls=%async_computation | async-start | bytes 917504 | tf_op jit(solution)/shard_map/all_to_all | solution.py:126
  47.8 1.2 %copy-start = (bf16[256,2048]{1,0:T(8,128)(2,1)S(1)}, bf16[256,2048]{1,0:T(8,128)(2,1)}, u32[]{:S(2)}) copy-start(bf16[256,2048]{1,0:T(8,128)(2,1)} %all-gather.2.cloned.1.call-done.hidden_ref.twin_hidden_ref) | copy-start | bytes 3145732
  49.0 1.5 %copy-start.2 = (bf16[1,1024,896]{2,1,0:T(8,128)(2,1)S(1)}, bf16[1,1024,896]{2,1,0:T(8,128)(2,1)}, u32[]{:S(2)}) copy-start(bf16[1,1024,896]{2,1,0:T(8,128)(2,1)} %param.13) | copy-start | bytes 5505028
  51.2 34.5 %copy-start.1 = (bf16[256,2048]{1,0:T(8,128)(2,1)S(1)}, bf16[256,2048]{1,0:T(8,128)(2,1)}, u32[]{:S(2)}) copy-start(bf16[256,2048]{1,0:T(8,128)(2,1)} %all-gather.2.cloned.1.call-done.hidden_ref.twin_hidden_ref) | copy-start | bytes 3145732
  51.2 34.5 %copy-start.4 = (s32[128]{0:T(128)S(1)}, s32[128]{0:T(128)}, u32[]{:S(2)}) copy-start(s32[128]{0:T(128)} %slot_expert_ref.1) | copy-start | bytes 1540
  65.4 24.2 %all-to-all-start.1 = ((f32[128,1,2]{2,1,0:T(1,128)}), f32[128,1,2]{2,1,0:T(1,128)S(1)}, u32[]{:S(2)}, u32[]{:S(2)}) async-start(f32[128,1,2]{2,1,0:T(1,128)} %bitcast.7), calls=%async_computation.1 | async-start | bytes 131072 | tf_op jit(solution)/shard_map/all_to_all | solution.py:142
  85.7 3.8 %copy-start.3 = (f32[32,4]{0,1:T(4,128)S(1)}, f32[32,4]{0,1:T(4,128)}, u32[]{:S(2)}) copy-start(f32[32,4]{0,1:T(4,128)} %param.8) | copy-start | bytes 1540
  85.7 3.8 %copy-start.5 = (s32[4,32]{1,0:T(4,128)S(1)}, s32[4,32]{1,0:T(4,128)}, u32[]{:S(2)}) copy-start(s32[4,32]{1,0:T(4,128)} %get-tuple-element.10.target_ref) | copy-start | bytes 1540
Sparse Core Ops, SparseCore 0:
  10.5 37.2 all-gather.1

commit v5 on v3

--- a/solution.py
+++ b/solution.py
@@ -3,7 +3,7 @@
 from jax import lax
 from jax.experimental import pallas as pl
 from jax.experimental.pallas import tpu as pltpu
-from jax.sharding import PartitionSpec as P
+from jax.sharding import Mesh, PartitionSpec as P
 
 
 def pack_kernel(ids_ref, weight_ref, slot_expert_ref, pick_ref, grad_ref, rows_ref, target_ref):
@@ -84,32 +84,39 @@
         out_ref[k : k + 1, :] = jnp.sum(found, axis=0, keepdims=True) / weight
 
 
-def grad_kernel(slot_expert_ref, hidden_ref, twin_hidden_ref, rows_ref, twin_rows_ref, out_ref, order_ref):
+def grad_kernel(slot_expert_ref, hidden_ref, twin_hidden_ref, rows_ref, out_ref, order_ref, used):
     over_rows = (((0,), (0,)), ((), ()))
+    count = hidden_ref.shape[0]
+
+    @pl.when(pl.program_id(0) == 0)
+    def _():
+        half = lax.axis_index("half")
+        place = lax.axis_index("place")
+        shared = slot_expert_ref[place] == slot_expert_ref[place + slot_expert_ref.shape[0] // 2]
+        lower, upper = rows_ref[:count, :], rows_ref[count:, :]
+        twin_rows = jnp.where(half == 0, upper, lower)
+        used[:count, :] = jnp.where(half == 0, lower, upper)
+        used[count:, :] = jnp.where(shared, twin_rows, jnp.zeros((), twin_rows.dtype))
+        order_ref[...] = jnp.zeros_like(order_ref)
+
     own = lax.dot_general(
-        hidden_ref[...], rows_ref[...], over_rows, preferred_element_type=jnp.float32
-    )
-    me = lax.axis_index("ep")
-    slots = slot_expert_ref.shape[0]
-    shared = slot_expert_ref[me] == slot_expert_ref[lax.rem(me + slots // 2, slots)]
-    twin_rows = jnp.where(shared, twin_rows_ref[...], jnp.zeros((), jnp.bfloat16))
+        hidden_ref[...], used[:count, :], over_rows, preferred_element_type=jnp.float32
+    )
     twin = lax.dot_general(
-        twin_hidden_ref[...], twin_rows, over_rows, preferred_element_type=jnp.float32
+        twin_hidden_ref[...], used[count:, :], over_rows, preferred_element_type=jnp.float32
     )
     out_ref[...] = (own + twin).astype(out_ref.dtype)
-    order_ref[...] = jnp.zeros_like(order_ref)
 
 
 def on_device(out_grad, route_weight, expert_ids, slot_expert, replica_pick, saved_gu, down_weight):
-    sources = lax.axis_size("ep")
+    ep = ("half", "place")
+    sources = lax.axis_size(ep)
     token_count, top_count = expert_ids.shape
     slot_count = slot_expert.shape[0]
     rows_total = saved_gu.shape[1]
     pair_rows = rows_total // sources
     features = out_grad.shape[1]
     hidden_units = down_weight.shape[1]
-    half = slot_count // 2
-    swap = [(i, (i + half) % slot_count) for i in range(slot_count)]
     ids_t = expert_ids.T
     weight_t = route_weight.T
     send_rows, target = pl.pallas_call(
@@ -120,14 +127,14 @@
         ),
         name="pack",
     )(ids_t, weight_t, slot_expert[None], replica_pick, out_grad)
-    arrived = lax.all_to_all(send_rows, "ep", split_axis=0, concat_axis=0, tiled=True)
+    arrived = lax.all_to_all(send_rows, ep, split_axis=0, concat_axis=0, tiled=True)
     part = pl.pallas_call(
         hidden_kernel,
         out_shape=jax.ShapeDtypeStruct((rows_total, saved_gu.shape[3]), jnp.bfloat16),
         compiler_params=pltpu.CompilerParams(vmem_limit_bytes=8 << 20),
         name="hidden",
     )(saved_gu[0])
-    twin_part = lax.ppermute(part, "ep", swap)
+    twin_part = lax.ppermute(part, "half", [(0, 1), (1, 0)])
     hidden = lax.all_gather(part, "rep", axis=1, tiled=True)
     twin_hidden = lax.all_gather(twin_part, "rep", axis=1, tiled=True)
     outputs = pl.pallas_call(
@@ -138,18 +145,14 @@
     )(hidden, down_weight[0])
     dots = pl.pallas_call(
         dots_kernel,
-        in_specs=[
-            pl.BlockSpec(memory_space=pltpu.VMEM),
-            pl.BlockSpec(memory_space=pltpu.VMEM),
-            pl.BlockSpec(memory_space=pl.ANY),
-        ],
+        in_specs=[pl.BlockSpec(memory_space=pltpu.VMEM)] * 2 + [pl.BlockSpec(memory_space=pl.ANY)],
         out_shape=jax.ShapeDtypeStruct((sources, pair_rows), jnp.float32),
         scratch_shapes=[pltpu.VMEM((rows_total, 128), jnp.float32)],
         compiler_params=pltpu.CompilerParams(vmem_limit_bytes=8 << 20),
         name="dots",
     )(arrived, outputs, twin_hidden)
     returned = lax.all_to_all(
-        dots.reshape(sources, 1, pair_rows), "ep", split_axis=0, concat_axis=0, tiled=True
+        dots.reshape(sources, 1, pair_rows), ep, split_axis=0, concat_axis=0, tiled=True
     )
     rows = pl.pallas_call(
         matrix_kernel,
@@ -158,8 +161,8 @@
         compiler_params=pltpu.CompilerParams(vmem_limit_bytes=8 << 20),
         name="matrix",
     )(arrived, dots)
-    twin_rows = lax.ppermute(rows, "ep", swap)
-    steps = 4
+    rows = lax.all_gather(rows, "half", axis=0, tiled=True)
+    steps = 2
     block = hidden_units // steps
     down_grad, order = pl.pallas_call(
         grad_kernel,
@@ -168,8 +171,7 @@
             pl.BlockSpec(memory_space=pltpu.SMEM),
             pl.BlockSpec((rows_total, block), lambda i: (0, i)),
             pl.BlockSpec((rows_total, block), lambda i: (0, i)),
-            pl.BlockSpec((rows_total, features), lambda i: (0, 0)),
-            pl.BlockSpec((rows_total, features), lambda i: (0, 0)),
+            pl.BlockSpec((2 * rows_total, features), lambda i: (0, 0)),
         ],
         out_specs=(
             pl.BlockSpec((block, features), lambda i: (i, 0)),
@@ -179,9 +181,10 @@
             jax.ShapeDtypeStruct((hidden_units, features), jnp.bfloat16),
             jax.ShapeDtypeStruct((8, 128), jnp.float32),
         ),
-        compiler_params=pltpu.CompilerParams(vmem_limit_bytes=16 << 20),
+        scratch_shapes=[pltpu.VMEM((2 * rows_total, features), jnp.bfloat16)],
+        compiler_params=pltpu.CompilerParams(vmem_limit_bytes=24 << 20),
         name="down_grad",
-    )(slot_expert, hidden, twin_hidden, rows, twin_rows)
+    )(slot_expert, hidden, twin_hidden, rows)
     route_part = pl.pallas_call(
         pick_kernel,
         in_specs=[pl.BlockSpec(memory_space=pltpu.VMEM)] * 3 + [pl.BlockSpec(memory_space=pl.ANY)],
@@ -193,19 +196,22 @@
 
 
 def solution(mesh):
+    ep, rep = mesh.shape["ep"], mesh.shape["rep"]
+    halves = Mesh(mesh.devices.reshape(2, ep // 2, rep), ("half", "place", "rep"))
+    ep = ("half", "place")
     placed = (
-        P("ep", "rep"),
-        P("ep", None),
-        P("ep", None),
+        P(ep, "rep"),
+        P(ep, None),
+        P(ep, None),
         P(),
-        P("ep", None),
-        P("ep", None, None, "rep"),
-        P("ep", None, "rep"),
+        P(ep, None),
+        P(ep, None, None, "rep"),
+        P(ep, None, "rep"),
     )
     return jax.shard_map(
         on_device,
-        mesh=mesh,
+        mesh=halves,
         in_specs=placed,
-        out_specs=(P("ep", None, "rep"), P("ep", None)),
+        out_specs=(P(ep, None, "rep"), P(ep, None)),
         check_vma=False,
     )

time: 96.9 us -> 94.3 us (0.973)
  blocking collectives: 25.6 us -> 39.1 us
  waiting for transfers between devices: 17.2 us -> 5.1 us
  starting transfers between devices: 42 us -> 38.5 us
    all_gather x0 -> x1, blocking collectives: none -> 14.5 us  [on_device(): rows = lax.all_gather(rows, 'half', axis=0, tiled=True)]
    all_to_all x2, waiting for transfers between devices: 17.2 us -> 5.1 us  [the longest x1 5.1 us: on_device(): lax.all_to_all(send_rows, ep, split_axis=0, concat_axis=0, tiled=True)]
    ppermute x2 -> x1, starting transfers between devices: 6.22 us -> 4.3 us  [on_device(): twin_part = lax.ppermute(part, 'half', [(0, 1), (1, 0)])]
    all_to_all x2, starting transfers between devices: 35.8 us -> 34.2 us  [the longest x1 23 us: on_device(): lax.all_to_all(send_rows, ep, split_axis=0, concat_axis=0, tiled=True)]
    psum x1, blocking collectives: 7.86 us -> 6.86 us  [on_device(): return (down_grad[None], lax.psum(route_part, 'rep').T)]
  transfers between devices with their start and end apart: 4 -> 3, of which waited for: 2 -> 1; matrix products, arithmetic and copies ran while one was open for 0% -> 0% of each run, Pallas kernels for 5% -> 5%
where the time goes in v5:
time: 94.3 us; the launch traced here: 93.9 us
  blocking collectives  39.1 us (41%)
  starting transfers between devices  38.5 us (41%)
  Pallas kernels  7.97 us (8%)
  waiting for transfers between devices  5.1 us (5%)
  local copies, waits for them, and re-layouts  2.46 us (3%)
    all_to_all x1, starting transfers between devices, on_device(): lax.all_to_all(send_rows, ep, split_axis=0, concat_axis=0, tiled=True)  23 us
    all_gather x1, blocking collectives, on_device(): rows = lax.all_gather(rows, 'half', axis=0, tiled=True)  14.5 us
    all_to_all x1, starting transfers between devices, on_device(): lax.all_to_all(dots.reshape(sources, 1, pair_rows), ep, split_axis=0, con...  11.2 us
    all_gather x1, blocking collectives, on_device(): hidden = lax.all_gather(part, 'rep', axis=1, tiled=True)  10.1 us
    all_gather x1, blocking collectives, on_device(): twin_hidden = lax.all_gather(twin_part, 'rep', axis=1, tiled=True)  7.67 us
    psum x1, blocking collectives, on_device(): return (down_grad[None], lax.psum(route_part, 'rep').T)  6.86 us
    all_to_all x1, waiting for transfers between devices, on_device(): lax.all_to_all(send_rows, ep, split_axis=0, concat_axis=0, tiled=True)  5.1 us
    ppermute x1, starting transfers between devices, on_device(): twin_part = lax.ppermute(part, 'half', [(0, 1), (1, 0)])  4.3 us
  transfers between devices with their start and end apart: 3, of which 1 were waited for; matrix products, arithmetic and copies ran while one was open for 0% of the time, Pallas kernels for 5%

profile of v5, /device:TPU:1, one launch (start us, length us, event | category | flops | bytes accessed | tf_op | source)
XLA Modules:
  0.0 93.9 jit_solution(7983496003155126671)
XLA Ops:
  0.6 2.2 %pack.1 = (bf16[128,2,896]{2,1,0:T(2,128)(2,1)}, s32[4,32]{1,0:T(4,128)}) custom-call(s32[4,32]{1,0:T(4,128)} %bitcast.18, f32[4,32]{1,0:T(4,128)} %bitcast.14, s32[1,128]{1,0:T(1,128)} %bitcast.17, s32[1,96]{1,0:T(1,128)} %pick_ref.1, bf16[32,896]{1,0:T(8,128)(2,1)} %grad_ref.1), custom_call_target="tpu_custom_call" | custom-call | tf_op jit(solution)/shard_map/pack/pallas_call | solution.py:122
  2.8 23.0 %all-to-all-start = ((bf16[128,2,896]{2,1,0:T(2,128)(2,1)}), bf16[128,2,896]{2,1,0:T(2,128)(2,1)S(1)}, u32[]{:S(2)}, u32[]{:S(2)}) async-start(bf16[128,2,896]{2,1,0:T(2,128)(2,1)} %get-tuple-element.6), calls=%async_computation | async-start | bytes 917504 | tf_op jit(solution)/shard_map/all_to_all | solution.py:130
  25.8 0.0 copy-start.1
  25.8 0.9 %copy-done.1 = bf16[1,256,2,256]{3,2,1,0:T(2,128)(2,1)S(1)} copy-done((bf16[1,256,2,256]{3,2,1,0:T(2,128)(2,1)S(1)}, bf16[1,256,2,256]{3,2,1,0:T(2,128)(2,1)}, u32[]{:S(2)}) %copy-start.1) | copy-done | bytes 262168
  26.8 0.7 hidden.1
  27.4 4.3 %collective-permute-start = (bf16[256,256]{1,0:T(8,128)(2,1)S(1)}, bf16[256,256]{1,0:T(8,128)(2,1)S(1)}, u32[]{:S(2)}, u32[]{:S(2)}) collective-permute-start(bf16[256,256]{1,0:T(8,128)(2,1)S(1)} %hidden.1), channel_id=1, source_target_pairs={{0,256},{256,0},{1,257},{257,1},{2,258},{258,2},{3,259},{259,3},{4... | collective-permute-start | bytes 393224 | tf_op jit(solution)/shard_map/ppermute | solution.py:137
  31.7 10.1 %all_gather.9.hidden_ref = bf16[256,1024]{1,0:T(8,128)(2,1)S(1)} all-gather(bf16[256,256]{1,0:T(8,128)(2,1)S(1)} %hidden.1), channel_id=1, replica_groups=mesh['half'=2,'place'=64,'rep'=4] {'rep'}, dimensions={1}, use_global_device_ids=true | all-gather | bytes 655360 | tf_op jit(solution)/shard_map/all_gather | solution.py:138
  41.8 0.0 copy-start
  41.8 1.5 %copy-done = bf16[1,1024,896]{2,1,0:T(8,128)(2,1)S(1)} copy-done((bf16[1,1024,896]{2,1,0:T(8,128)(2,1)S(1)}, bf16[1,1024,896]{2,1,0:T(8,128)(2,1)}, u32[]{:S(2)}) %copy-start) | copy-done | bytes 1835032
  43.3 0.7 forward.1.outputs_ref
  44.0 0.0 collective-permute-done
  44.0 7.7 %all_gather.10._.twin_hidden_ref = bf16[256,1024]{1,0:T(8,128)(2,1)S(1)} all-gather(bf16[256,256]{1,0:T(8,128)(2,1)S(1)} %collective-permute-done), channel_id=1, replica_groups=mesh['half'=2,'place'=64,'rep'=4] {'rep'}, dimensions={1}, use_global_device_ids=true | all-gather | bytes 655360 | tf_op jit(solution)/shard_map/all_gather | solution.py:139
  51.7 0.0 copy-start.3
  51.7 5.1 %all-to-all-done.arrived_ref = bf16[128,2,896]{2,1,0:T(2,128)(2,1)S(1)} async-done(((bf16[128,2,896]{2,1,0:T(2,128)(2,1)}), bf16[128,2,896]{2,1,0:T(2,128)(2,1)S(1)}, u32[]{:S(2)}, u32[]{:S(2)}) %all-to-all-start) | async-done | bytes 458784 | tf_op jit(solution)/shard_map/all_to_all | solution.py:130
  56.8 1.0 %dots.1._ = f32[128,2]{1,0:T(8,128)} custom-call(bf16[128,2,896]{2,1,0:T(2,128)(2,1)S(1)} %all-to-all-done.arrived_ref, f32[256,896]{1,0:T(8,128)S(1)} %forward.1.outputs_ref, bf16[256,1024]{1,0:T(8,128)(2,1)S(1)} %all_gather.10._.twin_hidden_ref), custom_call_target="tpu_custom_call" | custom-call | tf_op jit(solution)/shard_map/dots/pallas_call | solution.py:146
  57.8 11.2 %all-to-all-start.1 = ((f32[128,1,2]{2,1,0:T(1,128)}), f32[128,1,2]{2,1,0:T(1,128)S(1)}, u32[]{:S(2)}, u32[]{:S(2)}) async-start(f32[128,1,2]{2,1,0:T(1,128)} %bitcast.7), calls=%async_computation.1 | async-start | bytes 131072 | tf_op jit(solution)/shard_map/all_to_all | solution.py:154
  69.0 0.1 matrix.1
  69.1 0.0 copy-start.2
  69.1 0.0 copy-start.4
  69.1 14.5 %all_gather.11.rows_ref = bf16[512,896]{1,0:T(8,128)(2,1)S(1)} all-gather(bf16[256,896]{1,0:T(8,128)(2,1)S(1)} %matrix.1), channel_id=1, replica_groups=mesh['half'=2,'place'=64,'rep'=4] {'half'}, dimensions={0}, use_global_device_ids=true | all-gather | bytes 1376256 | tf_op jit(solution)/shard_map/all_gather | solution.py:164
  83.6 0.0 copy-done.3
  83.6 3.1 %down_grad.1 = (bf16[1024,896]{1,0:T(8,128)(2,1)}, f32[8,128]{1,0:T(8,128)S(1)}) custom-call(s32[128]{0:T(128)S(1)} %copy-done.3, bf16[256,1024]{1,0:T(8,128)(2,1)S(1)} %all_gather.9.hidden_ref, bf16[256,1024]{1,0:T(8,128)(2,1)S(1)} %all_gather.10._.twin_hidden_ref, bf16[512,896]{1,0:T(8,128)(2,1)S(1)} %all_gather.11.rows_ref), custom_call_target="tpu_custom_call" | custom-call | tf_op jit(solution)/shard_map/down_grad/pallas_call | solution.py:167
  86.8 0.0 all-to-all-done.1
  86.8 0.0 copy-done.2
  86.8 0.0 copy-done.4
  86.8 0.2 pick.1
  87.0 6.9 %psum.7 = f32[32,4]{0,1:T(4,128)} all-reduce(f32[32,4]{0,1:T(4,128)S(1)} %bitcast.16), channel_id=1, replica_groups=mesh['half'=2,'place'=64,'rep'=4] {'rep'}, use_global_device_ids=true, to_apply=%region_0.0 | all-reduce | flops 128 | bytes 1024 | tf_op jit(solution)/shard_map/psum | solution.py:195
Async XLA Ops:
  2.8 54.0 %all-to-all-start = ((bf16[128,2,896]{2,1,0:T(2,128)(2,1)}), bf16[128,2,896]{2,1,0:T(2,128)(2,1)S(1)}, u32[]{:S(2)}, u32[]{:S(2)}) async-start(bf16[128,2,896]{2,1,0:T(2,128)(2,1)} %get-tuple-element.6), calls=%async_computation | async-start | bytes 917504 | tf_op jit(solution)/shard_map/all_to_all | solution.py:130
  25.8 1.0 %copy-start.1 = (bf16[1,256,2,256]{3,2,1,0:T(2,128)(2,1)S(1)}, bf16[1,256,2,256]{3,2,1,0:T(2,128)(2,1)}, u32[]{:S(2)}) copy-start(bf16[1,256,2,256]{3,2,1,0:T(2,128)(2,1)} %param.12) | copy-start | bytes 786436
  27.4 16.6 %collective-permute-start = (bf16[256,256]{1,0:T(8,128)(2,1)S(1)}, bf16[256,256]{1,0:T(8,128)(2,1)S(1)}, u32[]{:S(2)}, u32[]{:S(2)}) collective-permute-start(bf16[256,256]{1,0:T(8,128)(2,1)S(1)} %hidden.1), channel_id=1, source_target_pairs={{0,256},{256,0},{1,257},{257,1},{2,258},{258,2},{3,259},{259,3},{4... | collective-permute-start | bytes 393224 | tf_op jit(solution)/shard_map/ppermute | solution.py:137
  41.8 1.5 %copy-start = (bf16[1,1024,896]{2,1,0:T(8,128)(2,1)S(1)}, bf16[1,1024,896]{2,1,0:T(8,128)(2,1)}, u32[]{:S(2)}) copy-start(bf16[1,1024,896]{2,1,0:T(8,128)(2,1)} %param.13) | copy-start | bytes 5505028
  51.7 31.9 %copy-start.3 = (s32[128]{0:T(128)S(1)}, s32[128]{0:T(128)}, u32[]{:S(2)}) copy-start(s32[128]{0:T(128)} %slot_expert_ref.1) | copy-start | bytes 1540
  57.8 29.0 %all-to-all-start.1 = ((f32[128,1,2]{2,1,0:T(1,128)}), f32[128,1,2]{2,1,0:T(1,128)S(1)}, u32[]{:S(2)}, u32[]{:S(2)}) async-start(f32[128,1,2]{2,1,0:T(1,128)} %bitcast.7), calls=%async_computation.1 | async-start | bytes 131072 | tf_op jit(solution)/shard_map/all_to_all | solution.py:154
  69.1 17.6 %copy-start.2 = (f32[32,4]{0,1:T(4,128)S(1)}, f32[32,4]{0,1:T(4,128)}, u32[]{:S(2)}) copy-start(f32[32,4]{0,1:T(4,128)} %param.8) | copy-start | bytes 1540
  69.1 17.6 %copy-start.4 = (s32[4,32]{1,0:T(4,128)S(1)}, s32[4,32]{1,0:T(4,128)}, u32[]{:S(2)}) copy-start(s32[4,32]{1,0:T(4,128)} %get-tuple-element.8.target_ref) | copy-start | bytes 1540

commit v6 on v5

--- a/solution.py
+++ b/solution.py
@@ -9,20 +9,26 @@
 def pack_kernel(ids_ref, weight_ref, slot_expert_ref, pick_ref, grad_ref, rows_ref, target_ref):
     top, tokens = ids_ref.shape
     experts = pick_ref.shape[1]
-    slots = slot_expert_ref.shape[1]
-    pair_rows = rows_ref.shape[1]
+    slots, pair_rows, _ = rows_ref.shape
+    features = grad_ref.shape[1]
     slot_expert = slot_expert_ref[...]
     lane = lax.broadcasted_iota(jnp.int32, (1, slots), 1)
     twin = pltpu.roll(slot_expert, slots // 2, 1)
-    rank = jnp.where((lane >= slots // 2) & (twin == slot_expert), 1.0, 0.0)
+    shared = jnp.where(twin == slot_expert, 1, 0)
+    rank = jnp.where((lane >= slots // 2) & (shared > 0), 1.0, 0.0)
     holds = lax.broadcasted_iota(jnp.int32, (experts, slots), 0) == slot_expert
     pick = jnp.dot(
         pick_ref[...].astype(jnp.bfloat16),
         jnp.where(holds, 1.0, 0.0).astype(jnp.bfloat16),
         preferred_element_type=jnp.float32,
     )
-    serves = holds & (pick == rank)
+    picked = pick == rank
+    serves = holds & picked
     slot_of = jnp.sum(jnp.where(serves, lane, 0).astype(jnp.float32), axis=1, keepdims=True)
+    other = jnp.where(shared > 0, jnp.where(lane < slots // 2, slots // 2, -(slots // 2)), 0)
+    twin_of = slot_of + jnp.sum(
+        jnp.where(serves, other, 0).astype(jnp.float32), axis=1, keepdims=True
+    )
     expert = lax.broadcasted_iota(jnp.int32, (experts, tokens), 0)
     chosen = [expert == ids_ref[k : k + 1, :] for k in range(top)]
     named = sum(jnp.where(c, 1.0, 0.0) for c in chosen)
@@ -35,14 +41,22 @@
         preferred_element_type=jnp.float32,
     )
     place = slot_of * pair_rows + before
+    twin_place = twin_of * pair_rows + before
     row = lax.broadcasted_iota(jnp.int32, (slots * pair_rows, tokens), 0)
     mix = jnp.zeros((slots * pair_rows, tokens), jnp.float32)
     for k in range(top):
         target = jnp.sum(jnp.where(chosen[k], place, 0.0), axis=0, keepdims=True).astype(jnp.int32)
+        twin_target = jnp.sum(jnp.where(chosen[k], twin_place, 0.0), axis=0, keepdims=True)
         target_ref[k : k + 1, :] = target
-        mix += jnp.where(row == target, weight_ref[k : k + 1, :], 0.0)
+        here = (row == target) | (row == twin_target.astype(jnp.int32))
+        mix += jnp.where(here, weight_ref[k : k + 1, :], 0.0)
     rows = jnp.dot(mix.astype(jnp.bfloat16), grad_ref[...], preferred_element_type=jnp.float32)
-    rows_ref[...] = rows.astype(rows_ref.dtype).reshape(rows_ref.shape)
+    rows_ref[:, :, :features] = rows.astype(rows_ref.dtype).reshape(slots, pair_rows, features)
+    slot = lax.broadcasted_iota(jnp.int32, (slots * pair_rows, slots), 0) // pair_rows
+    chosen_slot = (slot == lane) & picked
+    rows_ref[:, :, features:] = (
+        jnp.where(chosen_slot, 1.0, 0.0).astype(rows_ref.dtype).reshape(slots, pair_rows, slots)
+    )
 
 
 def hidden_kernel(saved_ref, out_ref):
@@ -55,8 +69,8 @@
     out_ref[...] = jnp.dot(hidden_ref[...], weight_ref[...], preferred_element_type=jnp.float32)
 
 
-def dots_kernel(arrived_ref, outputs_ref, _, dots_ref, scratch):
-    rows = arrived_ref[...].reshape(outputs_ref.shape)
+def dots_kernel(arrived_ref, outputs_ref, dots_ref, scratch):
+    rows = arrived_ref[:, :, : outputs_ref.shape[1]].reshape(outputs_ref.shape)
     total = jnp.sum(rows.astype(jnp.float32) * outputs_ref[...], axis=1, keepdims=True)
     scratch[...] = jnp.broadcast_to(total, scratch.shape)
     sources, pair_rows = dots_ref.shape
@@ -65,10 +79,6 @@
     for p in range(1, pair_rows):
         found = jnp.where(lane == p, scratch[pl.ds(p, sources, stride=pair_rows), :], found)
     dots_ref[...] = found[:, :pair_rows]
-
-
-def matrix_kernel(arrived_ref, _, rows_ref):
-    rows_ref[...] = arrived_ref[...].reshape(rows_ref.shape)
 
 
 def pick_kernel(returned_ref, target_ref, weight_ref, _, out_ref):
@@ -84,28 +94,23 @@
         out_ref[k : k + 1, :] = jnp.sum(found, axis=0, keepdims=True) / weight
 
 
-def grad_kernel(slot_expert_ref, hidden_ref, twin_hidden_ref, rows_ref, out_ref, order_ref, used):
-    over_rows = (((0,), (0,)), ((), ()))
-    count = hidden_ref.shape[0]
+def grad_kernel(_, arrived_ref, hidden_ref, twin_hidden_ref, out_ref, order_ref, rows_ref, own_ref):
+    features = out_ref.shape[1]
+    rows = rows_ref.shape[0]
 
     @pl.when(pl.program_id(0) == 0)
     def _():
-        half = lax.axis_index("half")
-        place = lax.axis_index("place")
-        shared = slot_expert_ref[place] == slot_expert_ref[place + slot_expert_ref.shape[0] // 2]
-        lower, upper = rows_ref[:count, :], rows_ref[count:, :]
-        twin_rows = jnp.where(half == 0, upper, lower)
-        used[:count, :] = jnp.where(half == 0, lower, upper)
-        used[count:, :] = jnp.where(shared, twin_rows, jnp.zeros((), twin_rows.dtype))
+        rows_ref[...] = arrived_ref[:, :, :features].reshape(rows_ref.shape)
+        picked = arrived_ref[:, :, features:].reshape(rows, arrived_ref.shape[2] - features)
+        picked = jnp.sum(picked.astype(jnp.float32), axis=1, keepdims=True)
+        own_ref[...] = jnp.broadcast_to(picked, own_ref.shape)
         order_ref[...] = jnp.zeros_like(order_ref)
 
-    own = lax.dot_general(
-        hidden_ref[...], used[:count, :], over_rows, preferred_element_type=jnp.float32
-    )
-    twin = lax.dot_general(
-        twin_hidden_ref[...], used[count:, :], over_rows, preferred_element_type=jnp.float32
-    )
-    out_ref[...] = (own + twin).astype(out_ref.dtype)
+    own = own_ref[:, :1] > 0.5
+    hidden = jnp.where(own, hidden_ref[...], twin_hidden_ref[...])
+    out_ref[...] = lax.dot_general(
+        hidden, rows_ref[...], (((0,), (0,)), ((), ())), preferred_element_type=jnp.float32
+    ).astype(out_ref.dtype)
 
 
 def on_device(out_grad, route_weight, expert_ids, slot_expert, replica_pick, saved_gu, down_weight):
@@ -122,7 +127,7 @@
     send_rows, target = pl.pallas_call(
         pack_kernel,
         out_shape=(
-            jax.ShapeDtypeStruct((slot_count, pair_rows, features), jnp.bfloat16),
+            jax.ShapeDtypeStruct((slot_count, pair_rows, features + slot_count), jnp.bfloat16),
             jax.ShapeDtypeStruct((top_count, token_count), jnp.int32),
         ),
         name="pack",
@@ -145,33 +150,25 @@
     )(hidden, down_weight[0])
     dots = pl.pallas_call(
         dots_kernel,
-        in_specs=[pl.BlockSpec(memory_space=pltpu.VMEM)] * 2 + [pl.BlockSpec(memory_space=pl.ANY)],
+        in_specs=[pl.BlockSpec(memory_space=pltpu.VMEM)] * 2,
         out_shape=jax.ShapeDtypeStruct((sources, pair_rows), jnp.float32),
         scratch_shapes=[pltpu.VMEM((rows_total, 128), jnp.float32)],
         compiler_params=pltpu.CompilerParams(vmem_limit_bytes=8 << 20),
         name="dots",
-    )(arrived, outputs, twin_hidden)
+    )(arrived, outputs)
     returned = lax.all_to_all(
         dots.reshape(sources, 1, pair_rows), ep, split_axis=0, concat_axis=0, tiled=True
     )
-    rows = pl.pallas_call(
-        matrix_kernel,
-        in_specs=[pl.BlockSpec(memory_space=pltpu.VMEM), pl.BlockSpec(memory_space=pl.ANY)],
-        out_shape=jax.ShapeDtypeStruct((rows_total, features), jnp.bfloat16),
-        compiler_params=pltpu.CompilerParams(vmem_limit_bytes=8 << 20),
-        name="matrix",
-    )(arrived, dots)
-    rows = lax.all_gather(rows, "half", axis=0, tiled=True)
     steps = 2
     block = hidden_units // steps
     down_grad, order = pl.pallas_call(
         grad_kernel,
         grid=(steps,),
         in_specs=[
-            pl.BlockSpec(memory_space=pltpu.SMEM),
+            pl.BlockSpec(memory_space=pl.ANY),
+            pl.BlockSpec(arrived.shape, lambda i: (0, 0, 0)),
             pl.BlockSpec((rows_total, block), lambda i: (0, i)),
             pl.BlockSpec((rows_total, block), lambda i: (0, i)),
-            pl.BlockSpec((2 * rows_total, features), lambda i: (0, 0)),
         ],
         out_specs=(
             pl.BlockSpec((block, features), lambda i: (i, 0)),
@@ -181,10 +178,13 @@
             jax.ShapeDtypeStruct((hidden_units, features), jnp.bfloat16),
             jax.ShapeDtypeStruct((8, 128), jnp.float32),
         ),
-        scratch_shapes=[pltpu.VMEM((2 * rows_total, features), jnp.bfloat16)],
+        scratch_shapes=[
+            pltpu.VMEM((rows_total, features), jnp.bfloat16),
+            pltpu.VMEM((rows_total, 128), jnp.float32),
+        ],
         compiler_params=pltpu.CompilerParams(vmem_limit_bytes=24 << 20),
         name="down_grad",
-    )(slot_expert, hidden, twin_hidden, rows)
+    )(dots, arrived, hidden, twin_hidden)
     route_part = pl.pallas_call(
         pick_kernel,
         in_specs=[pl.BlockSpec(memory_space=pltpu.VMEM)] * 3 + [pl.BlockSpec(memory_space=pl.ANY)],

time: 94.3 us -> 94 us (level)
  waiting for transfers between devices: 5.1 us -> 20.4 us
  blocking collectives: 39.1 us -> 27.8 us
  starting transfers between devices: 38.5 us -> 35.1 us
    all_gather x1 -> x0, blocking collectives: 14.5 us -> none  [on_device(): rows = lax.all_gather(rows, 'half', axis=0, tiled=True)]
    all_to_all x1, waiting for transfers between devices: 5.1 us -> 15.5 us  [on_device(): lax.all_to_all(send_rows, ep, split_axis=0, concat_axis=0, tiled=True)]
    all_to_all x1, waiting for transfers between devices: 0.01 us -> 4.92 us  [on_device(): lax.all_to_all(dots.reshape(sources, 1, pair_rows), ep, split_axis=0, con...]
    all_to_all x1, starting transfers between devices: 11.2 us -> 7.78 us  [on_device(): lax.all_to_all(dots.reshape(sources, 1, pair_rows), ep, split_axis=0, con...]
    psum x1, blocking collectives: 6.86 us -> 9 us  [on_device(): return (down_grad[None], lax.psum(route_part, 'rep').T)]
    all_gather x1, blocking collectives: 7.67 us -> 8.64 us  [on_device(): twin_hidden = lax.all_gather(twin_part, 'rep', axis=1, tiled=True)]
    unnamed x10 -> x8, local copies, waits for them, and re-layouts: 2.46 us -> 2.46 us
  transfers between devices with their start and end apart: 3 -> 3, of which waited for: 1 -> 2; matrix products, arithmetic and copies ran while one was open for 0% -> 0% of each run, Pallas kernels for 5% -> 5%
where the time goes in v6:
time: 94 us; the launch traced here: 93.7 us
  starting transfers between devices  35.1 us (37%)
  blocking collectives  27.8 us (30%)
  waiting for transfers between devices  20.4 us (22%)
  Pallas kernels  7.2 us (8%)
  local copies, waits for them, and re-layouts  2.46 us (3%)
    all_to_all x1, starting transfers between devices, on_device(): lax.all_to_all(send_rows, ep, split_axis=0, concat_axis=0, tiled=True)  23 us
    all_to_all x1, waiting for transfers between devices, on_device(): lax.all_to_all(send_rows, ep, split_axis=0, concat_axis=0, tiled=True)  15.5 us
    all_gather x1, blocking collectives, on_device(): hidden = lax.all_gather(part, 'rep', axis=1, tiled=True)  10.2 us
    psum x1, blocking collectives, on_device(): return (down_grad[None], lax.psum(route_part, 'rep').T)  9 us
    all_gather x1, blocking collectives, on_device(): twin_hidden = lax.all_gather(twin_part, 'rep', axis=1, tiled=True)  8.64 us
    all_to_all x1, starting transfers between devices, on_device(): lax.all_to_all(dots.reshape(sources, 1, pair_rows), ep, split_axis=0, con...  7.78 us
    all_to_all x1, waiting for transfers between devices, on_device(): lax.all_to_all(dots.reshape(sources, 1, pair_rows), ep, split_axis=0, con...  4.92 us
    ppermute x1, starting transfers between devices, on_device(): twin_part = lax.ppermute(part, 'half', [(0, 1), (1, 0)])  4.3 us
  transfers between devices with their start and end apart: 3, of which 2 were waited for; matrix products, arithmetic and copies ran while one was open for 0% of the time, Pallas kernels for 5%

profile of v6, /device:TPU:1, one launch (start us, length us, event | category | flops | bytes accessed | tf_op | source)
XLA Modules:
  0.0 93.7 jit_solution(11255576727106484253)
XLA Ops:
  0.6 2.3 %pack.1 = (bf16[128,2,1024]{2,1,0:T(2,128)(2,1)}, s32[4,32]{1,0:T(4,128)}) custom-call(s32[4,32]{1,0:T(4,128)} %bitcast.17, f32[4,32]{1,0:T(4,128)} %bitcast.14, s32[1,128]{1,0:T(1,128)} %bitcast.18, s32[1,96]{1,0:T(1,128)} %pick_ref.1, bf16[32,896]{1,0:T(8,128)(2,1)} %grad_ref.1), custom_call_target="tpu_custom_call" | custom-call | tf_op jit(solution)/shard_map/pack/pallas_call | solution.py:127
  2.9 23.0 %all-to-all-start = ((bf16[128,2,1024]{2,1,0:T(2,128)(2,1)}), bf16[128,2,1024]{2,1,0:T(2,128)(2,1)S(1)}, u32[]{:S(2)}, u32[]{:S(2)}) async-start(bf16[128,2,1024]{2,1,0:T(2,128)(2,1)} %get-tuple-element.6), calls=%async_computation | async-start | bytes 1048576 | tf_op jit(solution)/shard_map/all_to_all | solution.py:135
  25.9 0.0 copy-start.1
  25.9 0.9 %copy-done.1 = bf16[1,256,2,256]{3,2,1,0:T(2,128)(2,1)S(1)} copy-done((bf16[1,256,2,256]{3,2,1,0:T(2,128)(2,1)S(1)}, bf16[1,256,2,256]{3,2,1,0:T(2,128)(2,1)}, u32[]{:S(2)}) %copy-start.1) | copy-done | bytes 262168
  26.9 0.7 hidden.1
  27.5 4.3 %collective-permute-start = (bf16[256,256]{1,0:T(8,128)(2,1)S(1)}, bf16[256,256]{1,0:T(8,128)(2,1)S(1)}, u32[]{:S(2)}, u32[]{:S(2)}) collective-permute-start(bf16[256,256]{1,0:T(8,128)(2,1)S(1)} %hidden.1), channel_id=1, source_target_pairs={{0,256},{256,0},{1,257},{257,1},{2,258},{258,2},{3,259},{259,3},{4... | collective-permute-start | bytes 393224 | tf_op jit(solution)/shard_map/ppermute | solution.py:142
  31.8 10.2 %all_gather.6.hidden_ref = bf16[256,1024]{1,0:T(8,128)(2,1)S(1)} all-gather(bf16[256,256]{1,0:T(8,128)(2,1)S(1)} %hidden.1), channel_id=1, replica_groups=mesh['half'=2,'place'=64,'rep'=4] {'rep'}, dimensions={1}, use_global_device_ids=true | all-gather | bytes 655360 | tf_op jit(solution)/shard_map/all_gather | solution.py:143
  42.0 0.0 copy-start
  42.0 1.5 %copy-done = bf16[1,1024,896]{2,1,0:T(8,128)(2,1)S(1)} copy-done((bf16[1,1024,896]{2,1,0:T(8,128)(2,1)S(1)}, bf16[1,1024,896]{2,1,0:T(8,128)(2,1)}, u32[]{:S(2)}) %copy-start) | copy-done | bytes 1835032
  43.5 0.7 forward.1.outputs_ref
  44.2 0.0 copy-start.2
  44.2 0.0 copy-start.3
  44.2 15.5 %all-to-all-done.arrived_ref = bf16[128,2,1024]{2,1,0:T(2,128)(2,1)S(1)} async-done(((bf16[128,2,1024]{2,1,0:T(2,128)(2,1)}), bf16[128,2,1024]{2,1,0:T(2,128)(2,1)S(1)}, u32[]{:S(2)}, u32[]{:S(2)}) %all-to-all-start) | async-done | bytes 524320 | tf_op jit(solution)/shard_map/all_to_all | solution.py:135
  59.8 1.0 %dots.1._ = f32[128,2]{1,0:T(8,128)} custom-call(bf16[128,2,1024]{2,1,0:T(2,128)(2,1)S(1)} %all-to-all-done.arrived_ref, f32[256,896]{1,0:T(8,128)S(1)} %forward.1.outputs_ref), custom_call_target="tpu_custom_call" | custom-call | tf_op jit(solution)/shard_map/dots/pallas_call | solution.py:151
  60.7 7.8 %all-to-all-start.1 = ((f32[128,1,2]{2,1,0:T(1,128)}), f32[128,1,2]{2,1,0:T(1,128)S(1)}, u32[]{:S(2)}, u32[]{:S(2)}) async-start(f32[128,1,2]{2,1,0:T(1,128)} %bitcast.7), calls=%async_computation.1 | async-start | bytes 131072 | tf_op jit(solution)/shard_map/all_to_all | solution.py:159
  68.5 0.0 collective-permute-done
  68.5 8.6 %all_gather.7.twin_hidden_ref = bf16[256,1024]{1,0:T(8,128)(2,1)S(1)} all-gather(bf16[256,256]{1,0:T(8,128)(2,1)S(1)} %collective-permute-done), channel_id=1, replica_groups=mesh['half'=2,'place'=64,'rep'=4] {'rep'}, dimensions={1}, use_global_device_ids=true | all-gather | bytes 655360 | tf_op jit(solution)/shard_map/all_gather | solution.py:144
  77.2 2.3 %down_grad.1 = (bf16[1024,896]{1,0:T(8,128)(2,1)}, f32[8,128]{1,0:T(8,128)S(1)}) custom-call(f32[128,2]{1,0:T(8,128)} %dots.1._, bf16[128,2,1024]{2,1,0:T(2,128)(2,1)S(1)} %all-to-all-done.arrived_ref, bf16[256,1024]{1,0:T(8,128)(2,1)S(1)} %all_gather.6.hidden_ref, bf16[256,1024]{1,0:T(8,128)(2,1)S(1)} %all_gather.7.twin_hidden_ref), custom_call_target="tpu_custom_call" | custom-call | tf_op jit(solution)/shard_map/down_grad/pallas_call | solution.py:164
  79.5 4.9 %all-to-all-done.1 = f32[128,1,2]{2,1,0:T(1,128)S(1)} async-done(((f32[128,1,2]{2,1,0:T(1,128)}), f32[128,1,2]{2,1,0:T(1,128)S(1)}, u32[]{:S(2)}, u32[]{:S(2)}) %all-to-all-start.1) | async-done | bytes 1056 | tf_op jit(solution)/shard_map/all_to_all | solution.py:159
  84.4 0.0 copy-done.2
  84.4 0.0 copy-done.3
  84.4 0.2 pick.1
  84.7 9.0 %psum.7 = f32[32,4]{0,1:T(4,128)} all-reduce(f32[32,4]{0,1:T(4,128)S(1)} %bitcast.16), channel_id=1, replica_groups=mesh['half'=2,'place'=64,'rep'=4] {'rep'}, use_global_device_ids=true, to_apply=%region_0.0 | all-reduce | flops 128 | bytes 1024 | tf_op jit(solution)/shard_map/psum | solution.py:195
Async XLA Ops:
  2.9 56.8 %all-to-all-start = ((bf16[128,2,1024]{2,1,0:T(2,128)(2,1)}), bf16[128,2,1024]{2,1,0:T(2,128)(2,1)S(1)}, u32[]{:S(2)}, u32[]{:S(2)}) async-start(bf16[128,2,1024]{2,1,0:T(2,128)(2,1)} %get-tuple-element.6), calls=%async_computation | async-start | bytes 1048576 | tf_op jit(solution)/shard_map/all_to_all | solution.py:135
  25.9 1.0 %copy-start.1 = (bf16[1,256,2,256]{3,2,1,0:T(2,128)(2,1)S(1)}, bf16[1,256,2,256]{3,2,1,0:T(2,128)(2,1)}, u32[]{:S(2)}) copy-start(bf16[1,256,2,256]{3,2,1,0:T(2,128)(2,1)} %param.12) | copy-start | bytes 786436
  27.5 41.0 %collective-permute-start = (bf16[256,256]{1,0:T(8,128)(2,1)S(1)}, bf16[256,256]{1,0:T(8,128)(2,1)S(1)}, u32[]{:S(2)}, u32[]{:S(2)}) collective-permute-start(bf16[256,256]{1,0:T(8,128)(2,1)S(1)} %hidden.1), channel_id=1, source_target_pairs={{0,256},{256,0},{1,257},{257,1},{2,258},{258,2},{3,259},{259,3},{4... | collective-permute-start | bytes 393224 | tf_op jit(solution)/shard_map/ppermute | solution.py:142
  42.0 1.5 %copy-start = (bf16[1,1024,896]{2,1,0:T(8,128)(2,1)S(1)}, bf16[1,1024,896]{2,1,0:T(8,128)(2,1)}, u32[]{:S(2)}) copy-start(bf16[1,1024,896]{2,1,0:T(8,128)(2,1)} %param.13) | copy-start | bytes 5505028
  44.2 40.2 %copy-start.2 = (f32[32,4]{0,1:T(4,128)S(1)}, f32[32,4]{0,1:T(4,128)}, u32[]{:S(2)}) copy-start(f32[32,4]{0,1:T(4,128)} %param.8) | copy-start | bytes 1540
  44.2 40.2 %copy-start.3 = (s32[4,32]{1,0:T(4,128)S(1)}, s32[4,32]{1,0:T(4,128)}, u32[]{:S(2)}) copy-start(s32[4,32]{1,0:T(4,128)} %get-tuple-element.8.target_ref) | copy-start | bytes 1540
  60.7 23.7 %all-to-all-start.1 = ((f32[128,1,2]{2,1,0:T(1,128)}), f32[128,1,2]{2,1,0:T(1,128)S(1)}, u32[]{:S(2)}, u32[]{:S(2)}) async-start(f32[128,1,2]{2,1,0:T(1,128)} %bitcast.7), calls=%async_computation.1 | async-start | bytes 131072 | tf_op jit(solution)/shard_map/all_to_all | solution.py:159

commit v7 on v6

--- a/solution.py
+++ b/solution.py
@@ -1,3 +1,5 @@
+import functools
+
 import jax
 import jax.numpy as jnp
 from jax import lax
@@ -73,23 +75,48 @@
     rows = arrived_ref[:, :, : outputs_ref.shape[1]].reshape(outputs_ref.shape)
     total = jnp.sum(rows.astype(jnp.float32) * outputs_ref[...], axis=1, keepdims=True)
     scratch[...] = jnp.broadcast_to(total, scratch.shape)
-    sources, pair_rows = dots_ref.shape
-    lane = lax.broadcasted_iota(jnp.int32, (sources, scratch.shape[1]), 1)
-    found = scratch[pl.ds(0, sources, stride=pair_rows), :]
+    depth = dots_ref.shape[0]
+    run = scratch.shape[0] // (2 * depth)
+    lane = lax.broadcasted_iota(jnp.int32, dots_ref.shape, 1)
+    found = jnp.zeros(dots_ref.shape, jnp.float32)
+    for half in range(2):
+        for step in range(run):
+            part = scratch[pl.ds(half * depth * run + step, depth, stride=run), :]
+            found = jnp.where(lane == half * run + step, part, found)
+    dots_ref[...] = found
+
+
+def turn_kernel(arrived_ref, _, out_ref, scratch, *, pair_rows, copies):
+    depth = arrived_ref.shape[0]
+    scratch[...] = jnp.zeros_like(scratch)
+    scratch[:depth, :] = arrived_ref[...]
+    scratch[...] = scratch[...].T
+    count = out_ref.shape[0] // copies
+    turned = scratch[pl.ds(0, count, stride=pair_rows), :]
     for p in range(1, pair_rows):
-        found = jnp.where(lane == p, scratch[pl.ds(p, sources, stride=pair_rows), :], found)
-    dots_ref[...] = found[:, :pair_rows]
-
-
-def pick_kernel(returned_ref, target_ref, weight_ref, _, out_ref):
+        turned += pltpu.roll(scratch[pl.ds(p, count, stride=pair_rows), :], p * depth, 1)
+    for copy in range(copies):
+        out_ref[pl.ds(copy, count, stride=copies), :] = turned
+
+
+def pick_kernel(returned_ref, target_ref, weight_ref, _, out_ref, scratch, *, depth, width, copies):
     top, tokens = target_ref.shape
-    slots, pair_rows = returned_ref.shape
-    slot = lax.broadcasted_iota(jnp.int32, (slots, tokens), 0)
+    count = returned_ref.shape[0] // copies
+    pair_rows = 2
+    scratch[...] = jnp.zeros_like(scratch)
+    scratch[:count, :] = sum(
+        returned_ref[pl.ds(copy, count, stride=copies), :] for copy in range(copies)
+    )
+    returned = scratch[...].T[: pair_rows * depth, :]
+    row = lax.broadcasted_iota(jnp.int32, (pair_rows * depth, tokens), 0)
     for k in range(top):
         target = target_ref[k : k + 1, :]
-        found = jnp.zeros((slots, tokens), jnp.float32)
-        for p in range(pair_rows):
-            found += jnp.where(slot * pair_rows + p == target, returned_ref[:, p : p + 1], 0.0)
+        slot = target // pair_rows
+        place = (target % pair_rows) * depth + slot // width % depth
+        column = slot // (width * depth) * width + slot % width
+        found = jnp.zeros(row.shape, jnp.float32)
+        for c in range(count):
+            found += jnp.where((row == place) & (column == c), returned[:, c : c + 1], 0.0)
         weight = weight_ref[k : k + 1, :].astype(jnp.bfloat16).astype(jnp.float32)
         out_ref[k : k + 1, :] = jnp.sum(found, axis=0, keepdims=True) / weight
 
@@ -114,8 +141,9 @@
 
 
 def on_device(out_grad, route_weight, expert_ids, slot_expert, replica_pick, saved_gu, down_weight):
-    ep = ("half", "place")
+    ep = ("half", "z", "x")
     sources = lax.axis_size(ep)
+    depth, width, copies = lax.axis_size("z"), lax.axis_size("x"), lax.axis_size("rep")
     token_count, top_count = expert_ids.shape
     slot_count = slot_expert.shape[0]
     rows_total = saved_gu.shape[1]
@@ -151,13 +179,29 @@
     dots = pl.pallas_call(
         dots_kernel,
         in_specs=[pl.BlockSpec(memory_space=pltpu.VMEM)] * 2,
-        out_shape=jax.ShapeDtypeStruct((sources, pair_rows), jnp.float32),
+        out_shape=jax.ShapeDtypeStruct((depth, 128), jnp.float32),
         scratch_shapes=[pltpu.VMEM((rows_total, 128), jnp.float32)],
         compiler_params=pltpu.CompilerParams(vmem_limit_bytes=8 << 20),
         name="dots",
     )(arrived, outputs)
+    along_z = lax.all_to_all(
+        dots.reshape(depth, 1, 128), "z", split_axis=0, concat_axis=0, tiled=True
+    )
+    group = 2 * width * copies
+    turned = pl.pallas_call(
+        functools.partial(turn_kernel, pair_rows=pair_rows, copies=copies),
+        in_specs=[pl.BlockSpec(memory_space=pltpu.VMEM), pl.BlockSpec(memory_space=pl.ANY)],
+        out_shape=jax.ShapeDtypeStruct((group, 128), jnp.float32),
+        scratch_shapes=[pltpu.VMEM((128, 128), jnp.float32)],
+        compiler_params=pltpu.CompilerParams(vmem_limit_bytes=4 << 20),
+        name="turn",
+    )(along_z.reshape(depth, 128), twin_hidden)
     returned = lax.all_to_all(
-        dots.reshape(sources, 1, pair_rows), ep, split_axis=0, concat_axis=0, tiled=True
+        turned.reshape(group, 1, 128),
+        ("half", "x", "rep"),
+        split_axis=0,
+        concat_axis=0,
+        tiled=True,
     )
     steps = 2
     block = hidden_units // steps
@@ -185,20 +229,24 @@
         compiler_params=pltpu.CompilerParams(vmem_limit_bytes=24 << 20),
         name="down_grad",
     )(dots, arrived, hidden, twin_hidden)
-    route_part = pl.pallas_call(
-        pick_kernel,
+    route_grad = pl.pallas_call(
+        functools.partial(pick_kernel, depth=depth, width=width, copies=copies),
         in_specs=[pl.BlockSpec(memory_space=pltpu.VMEM)] * 3 + [pl.BlockSpec(memory_space=pl.ANY)],
         out_shape=jax.ShapeDtypeStruct((top_count, token_count), jnp.float32),
+        scratch_shapes=[pltpu.VMEM((128, 128), jnp.float32)],
         compiler_params=pltpu.CompilerParams(vmem_limit_bytes=4 << 20),
         name="pick",
-    )(returned.reshape(slot_count, pair_rows), target, weight_t, order)
-    return (down_grad[None], lax.psum(route_part, "rep").T)
+    )(returned.reshape(group, 128), target, weight_t, order)
+    return (down_grad[None], route_grad.T)
 
 
 def solution(mesh):
     ep, rep = mesh.shape["ep"], mesh.shape["rep"]
-    halves = Mesh(mesh.devices.reshape(2, ep // 2, rep), ("half", "place", "rep"))
-    ep = ("half", "place")
+    width = 4
+    finer = Mesh(
+        mesh.devices.reshape(2, ep // (2 * width), width, rep), ("half", "z", "x", "rep")
+    )
+    ep = ("half", "z", "x")
     placed = (
         P(ep, "rep"),
         P(ep, None),
@@ -210,7 +258,7 @@
     )
     return jax.shard_map(
         on_device,
-        mesh=halves,
+        mesh=finer,
         in_specs=placed,
         out_specs=(P(ep, None, "rep"), P(ep, None)),
         check_vma=False,

time: 94 us -> 92.8 us (0.987)
  blocking collectives: 27.8 us -> 18.9 us
  starting transfers between devices: 35.1 us -> 39.1 us
  waiting for transfers between devices: 20.4 us -> 22.7 us
  Pallas kernels: 7.2 us -> 8.5 us
    psum x1 -> x0, blocking collectives: 9 us -> none  [on_device(): return (down_grad[None], lax.psum(route_part, 'rep').T)]
    all_to_all x1 -> x2, starting transfers between devices: 7.78 us -> 11.8 us  [the longest x1 7.01 us: on_device(): lax.all_to_all(turned.reshape(group, 1, 128), ('half', 'x', 'rep'), split...]
    all_to_all x1 -> x2, waiting for transfers between devices: 4.92 us -> 7.15 us  [the longest x1 4.7 us: on_device(): lax.all_to_all(turned.reshape(group, 1, 128), ('half', 'x', 'rep'), split...]
    pallas_call x1 -> x2, Pallas kernels: 0.22 us -> 1.54 us  [the longest x1 0.8 us: on_device(): pl.pallas_call(functools.partial(pick_kernel, depth=depth, width=width, c...]
  transfers between devices with their start and end apart: 3 -> 4, of which waited for: 2 -> 3; matrix products, arithmetic and copies ran while one was open for 0% -> 0% of each run, Pallas kernels for 5% -> 5%
where the time goes in v7:
time: 92.8 us; the launch traced here: 92.4 us
  starting transfers between devices  39.1 us (42%)
  waiting for transfers between devices  22.7 us (24%)
  blocking collectives  18.9 us (20%)
  Pallas kernels  8.5 us (9%)
  local copies, waits for them, and re-layouts  2.46 us (3%)
    all_to_all x1, starting transfers between devices, on_device(): lax.all_to_all(send_rows, ep, split_axis=0, concat_axis=0, tiled=True)  23 us
    all_to_all x1, waiting for transfers between devices, on_device(): lax.all_to_all(send_rows, ep, split_axis=0, concat_axis=0, tiled=True)  15.5 us
    all_gather x1, blocking collectives, on_device(): hidden = lax.all_gather(part, 'rep', axis=1, tiled=True)  10.2 us
    all_gather x1, blocking collectives, on_device(): twin_hidden = lax.all_gather(twin_part, 'rep', axis=1, tiled=True)  8.78 us
    all_to_all x1, starting transfers between devices, on_device(): lax.all_to_all(turned.reshape(group, 1, 128), ('half', 'x', 'rep'), split...  7.01 us
    all_to_all x1, starting transfers between devices, on_device(): lax.all_to_all(dots.reshape(depth, 1, 128), 'z', split_axis=0, concat_axi...  4.83 us
    all_to_all x1, waiting for transfers between devices, on_device(): lax.all_to_all(turned.reshape(group, 1, 128), ('half', 'x', 'rep'), split...  4.7 us
    ppermute x1, starting transfers between devices, on_device(): twin_part = lax.ppermute(part, 'half', [(0, 1), (1, 0)])  4.3 us
  transfers between devices with their start and end apart: 4, of which 3 were waited for; matrix products, arithmetic and copies ran while one was open for 0% of the time, Pallas kernels for 5%

profile of v7, /device:TPU:1, one launch (start us, length us, event | category | flops | bytes accessed | tf_op | source)
XLA Modules:
  0.0 92.4 jit_solution(15026263096318216710)
XLA Ops:
  0.6 2.3 %pack.1 = (bf16[128,2,1024]{2,1,0:T(2,128)(2,1)}, s32[4,32]{1,0:T(4,128)}) custom-call(s32[4,32]{1,0:T(4,128)} %bitcast.21, f32[4,32]{1,0:T(4,128)} %bitcast.19, s32[1,128]{1,0:T(1,128)} %bitcast.23, s32[1,96]{1,0:T(1,128)} %pick_ref.1, bf16[32,896]{1,0:T(8,128)(2,1)} %grad_ref.1), custom_call_target="tpu_custom_call" | custom-call | tf_op jit(solution)/shard_map/pack/pallas_call | solution.py:155
  2.9 23.0 %all-to-all-start = ((bf16[128,2,1024]{2,1,0:T(2,128)(2,1)}), bf16[128,2,1024]{2,1,0:T(2,128)(2,1)S(1)}, u32[]{:S(2)}, u32[]{:S(2)}) async-start(bf16[128,2,1024]{2,1,0:T(2,128)(2,1)} %get-tuple-element.6), calls=%async_computation | async-start | bytes 1048576 | tf_op jit(solution)/shard_map/all_to_all | solution.py:163
  25.9 0.0 copy-start.1
  25.9 0.9 %copy-done.1 = bf16[1,256,2,256]{3,2,1,0:T(2,128)(2,1)S(1)} copy-done((bf16[1,256,2,256]{3,2,1,0:T(2,128)(2,1)S(1)}, bf16[1,256,2,256]{3,2,1,0:T(2,128)(2,1)}, u32[]{:S(2)}) %copy-start.1) | copy-done | bytes 262168
  26.9 0.7 hidden.1
  27.5 4.3 %collective-permute-start = (bf16[256,256]{1,0:T(8,128)(2,1)S(1)}, bf16[256,256]{1,0:T(8,128)(2,1)S(1)}, u32[]{:S(2)}, u32[]{:S(2)}) collective-permute-start(bf16[256,256]{1,0:T(8,128)(2,1)S(1)} %hidden.1), channel_id=1, source_target_pairs={{0,256},{256,0},{1,257},{257,1},{2,258},{258,2},{3,259},{259,3},{4... | collective-permute-start | bytes 393224 | tf_op jit(solution)/shard_map/ppermute | solution.py:170
  31.8 10.2 %all_gather.6.hidden_ref = bf16[256,1024]{1,0:T(8,128)(2,1)S(1)} all-gather(bf16[256,256]{1,0:T(8,128)(2,1)S(1)} %hidden.1), channel_id=1, replica_groups=mesh['half'=2,'z'=16,'x'=4,'rep'=4] {'rep'}, dimensions={1}, use_global_device_ids=true | all-gather | bytes 655360 | tf_op jit(solution)/shard_map/all_gather | solution.py:171
  42.0 0.0 copy-start
  42.0 1.5 %copy-done = bf16[1,1024,896]{2,1,0:T(8,128)(2,1)S(1)} copy-done((bf16[1,1024,896]{2,1,0:T(8,128)(2,1)S(1)}, bf16[1,1024,896]{2,1,0:T(8,128)(2,1)}, u32[]{:S(2)}) %copy-start) | copy-done | bytes 1835032
  43.5 0.7 forward.1.outputs_ref
  44.2 0.0 copy-start.2
  44.2 0.0 copy-start.3
  44.2 15.5 %all-to-all-done.arrived_ref = bf16[128,2,1024]{2,1,0:T(2,128)(2,1)S(1)} async-done(((bf16[128,2,1024]{2,1,0:T(2,128)(2,1)}), bf16[128,2,1024]{2,1,0:T(2,128)(2,1)S(1)}, u32[]{:S(2)}, u32[]{:S(2)}) %all-to-all-start) | async-done | bytes 524320 | tf_op jit(solution)/shard_map/all_to_all | solution.py:163
  59.8 1.0 %dots.1._ = f32[16,128]{1,0:T(8,128)} custom-call(bf16[128,2,1024]{2,1,0:T(2,128)(2,1)S(1)} %all-to-all-done.arrived_ref, f32[256,896]{1,0:T(8,128)S(1)} %forward.1.outputs_ref), custom_call_target="tpu_custom_call" | custom-call | tf_op jit(solution)/shard_map/dots/pallas_call | solution.py:179
  60.7 4.8 %all-to-all-start.1 = ((f32[16,1,128]{2,1,0:T(1,128)}), f32[16,1,128]{2,1,0:T(1,128)S(1)}, u32[]{:S(2)}, u32[]{:S(2)}) async-start(f32[16,1,128]{2,1,0:T(1,128)} %bitcast.7), calls=%async_computation.1 | async-start | bytes 16384 | tf_op jit(solution)/shard_map/all_to_all | solution.py:187
  65.5 0.0 collective-permute-done
  65.6 8.8 %all_gather.7.twin_hidden_ref._ = bf16[256,1024]{1,0:T(8,128)(2,1)S(1)} all-gather(bf16[256,256]{1,0:T(8,128)(2,1)S(1)} %collective-permute-done), channel_id=1, replica_groups=mesh['half'=2,'z'=16,'x'=4,'rep'=4] {'rep'}, dimensions={1}, use_global_device_ids=true | all-gather | bytes 655360 | tf_op jit(solution)/shard_map/all_gather | solution.py:172
  74.3 2.4 %all-to-all-done.1 = f32[16,1,128]{2,1,0:T(1,128)S(1)} async-done(((f32[16,1,128]{2,1,0:T(1,128)}), f32[16,1,128]{2,1,0:T(1,128)S(1)}, u32[]{:S(2)}, u32[]{:S(2)}) %all-to-all-start.1) | async-done | bytes 8224 | tf_op jit(solution)/shard_map/all_to_all | solution.py:187
  76.8 0.7 turn.1
  77.5 7.0 %all-to-all-start.2 = ((f32[32,1,128]{2,1,0:T(1,128)}), f32[32,1,128]{2,1,0:T(1,128)S(1)}, u32[]{:S(2)}, u32[]{:S(2)}) async-start(f32[32,1,128]{2,1,0:T(1,128)} %bitcast.10), calls=%async_computation.2 | async-start | bytes 32768 | tf_op jit(solution)/shard_map/all_to_all | solution.py:199
  84.5 2.3 %down_grad.1 = (bf16[1024,896]{1,0:T(8,128)(2,1)}, f32[8,128]{1,0:T(8,128)S(1)}) custom-call(f32[16,128]{1,0:T(8,128)} %dots.1._, bf16[128,2,1024]{2,1,0:T(2,128)(2,1)S(1)} %all-to-all-done.arrived_ref, bf16[256,1024]{1,0:T(8,128)(2,1)S(1)} %all_gather.6.hidden_ref, bf16[256,1024]{1,0:T(8,128)(2,1)S(1)} %all_gather.7.twin_hidden_ref._), custom_call_target="tpu_custom_call" | custom-call | tf_op jit(solution)/shard_map/down_grad/pallas_call | solution.py:208
  86.9 4.7 %all-to-all-done.2 = f32[32,1,128]{2,1,0:T(1,128)S(1)} async-done(((f32[32,1,128]{2,1,0:T(1,128)}), f32[32,1,128]{2,1,0:T(1,128)S(1)}, u32[]{:S(2)}, u32[]{:S(2)}) %all-to-all-start.2) | async-done | bytes 16416 | tf_op jit(solution)/shard_map/all_to_all | solution.py:199
  91.6 0.0 copy-done.2
  91.6 0.0 copy-done.3
  91.6 0.8 pick.1
Async XLA Ops:
  2.9 56.8 %all-to-all-start = ((bf16[128,2,1024]{2,1,0:T(2,128)(2,1)}), bf16[128,2,1024]{2,1,0:T(2,128)(2,1)S(1)}, u32[]{:S(2)}, u32[]{:S(2)}) async-start(bf16[128,2,1024]{2,1,0:T(2,128)(2,1)} %get-tuple-element.6), calls=%async_computation | async-start | bytes 1048576 | tf_op jit(solution)/shard_map/all_to_all | solution.py:163
  25.9 1.0 %copy-start.1 = (bf16[1,256,2,256]{3,2,1,0:T(2,128)(2,1)S(1)}, bf16[1,256,2,256]{3,2,1,0:T(2,128)(2,1)}, u32[]{:S(2)}) copy-start(bf16[1,256,2,256]{3,2,1,0:T(2,128)(2,1)} %param.12) | copy-start | bytes 786436
  27.5 38.0 %collective-permute-start = (bf16[256,256]{1,0:T(8,128)(2,1)S(1)}, bf16[256,256]{1,0:T(8,128)(2,1)S(1)}, u32[]{:S(2)}, u32[]{:S(2)}) collective-permute-start(bf16[256,256]{1,0:T(8,128)(2,1)S(1)} %hidden.1), channel_id=1, source_target_pairs={{0,256},{256,0},{1,257},{257,1},{2,258},{258,2},{3,259},{259,3},{4... | collective-permute-start | bytes 393224 | tf_op jit(solution)/shard_map/ppermute | solution.py:170
  42.0 1.5 %copy-start = (bf16[1,1024,896]{2,1,0:T(8,128)(2,1)S(1)}, bf16[1,1024,896]{2,1,0:T(8,128)(2,1)}, u32[]{:S(2)}) copy-start(bf16[1,1024,896]{2,1,0:T(8,128)(2,1)} %param.13) | copy-start | bytes 5505028
  44.2 47.4 %copy-start.2 = (f32[32,4]{0,1:T(4,128)S(1)}, f32[32,4]{0,1:T(4,128)}, u32[]{:S(2)}) copy-start(f32[32,4]{0,1:T(4,128)} %param.8) | copy-start | bytes 1540
  44.2 47.4 %copy-start.3 = (s32[4,32]{1,0:T(4,128)S(1)}, s32[4,32]{1,0:T(4,128)}, u32[]{:S(2)}) copy-start(s32[4,32]{1,0:T(4,128)} %get-tuple-element.8.target_ref) | copy-start | bytes 1540
  60.7 16.1 %all-to-all-start.1 = ((f32[16,1,128]{2,1,0:T(1,128)}), f32[16,1,128]{2,1,0:T(1,128)S(1)}, u32[]{:S(2)}, u32[]{:S(2)}) async-start(f32[16,1,128]{2,1,0:T(1,128)} %bitcast.7), calls=%async_computation.1 | async-start | bytes 16384 | tf_op jit(solution)/shard_map/all_to_all | solution.py:187
  77.5 14.1 %all-to-all-start.2 = ((f32[32,1,128]{2,1,0:T(1,128)}), f32[32,1,128]{2,1,0:T(1,128)S(1)}, u32[]{:S(2)}, u32[]{:S(2)}) async-start(f32[32,1,128]{2,1,0:T(1,128)} %bitcast.10), calls=%async_computation.2 | async-start | bytes 32768 | tf_op jit(solution)/shard_map/all_to_all | solution.py:199

commit v8 on v6

--- a/solution.py
+++ b/solution.py
@@ -1,3 +1,5 @@
+import functools
+
 import jax
 import jax.numpy as jnp
 from jax import lax
@@ -10,7 +12,6 @@
     top, tokens = ids_ref.shape
     experts = pick_ref.shape[1]
     slots, pair_rows, _ = rows_ref.shape
-    features = grad_ref.shape[1]
     slot_expert = slot_expert_ref[...]
     lane = lax.broadcasted_iota(jnp.int32, (1, slots), 1)
     twin = pltpu.roll(slot_expert, slots // 2, 1)
@@ -51,59 +52,113 @@
         here = (row == target) | (row == twin_target.astype(jnp.int32))
         mix += jnp.where(here, weight_ref[k : k + 1, :], 0.0)
     rows = jnp.dot(mix.astype(jnp.bfloat16), grad_ref[...], preferred_element_type=jnp.float32)
-    rows_ref[:, :, :features] = rows.astype(rows_ref.dtype).reshape(slots, pair_rows, features)
-    slot = lax.broadcasted_iota(jnp.int32, (slots * pair_rows, slots), 0) // pair_rows
-    chosen_slot = (slot == lane) & picked
-    rows_ref[:, :, features:] = (
-        jnp.where(chosen_slot, 1.0, 0.0).astype(rows_ref.dtype).reshape(slots, pair_rows, slots)
-    )
-
-
-def hidden_kernel(saved_ref, out_ref):
+    rows_ref[...] = rows.astype(rows_ref.dtype).reshape(rows_ref.shape)
+
+
+def hidden_kernel(saved_ref, pick_ref, out_ref, bundle_ref):
     gate = saved_ref[:, 0, :].astype(jnp.float32)
     up = saved_ref[:, 1, :].astype(jnp.float32)
-    out_ref[...] = (gate / (1.0 + jnp.exp(-gate)) * up).astype(out_ref.dtype)
+    hidden = (gate / (1.0 + jnp.exp(-gate)) * up).astype(out_ref.dtype)
+    out_ref[...] = hidden
+    rows, experts = out_ref.shape[0], pick_ref.shape[1]
+    bundle_ref[:rows, :] = hidden
+    below = bundle_ref.shape[0] - rows
+    bundle_ref[rows:, :] = jnp.zeros((below, out_ref.shape[1]), out_ref.dtype)
+    pick = pick_ref[...].astype(jnp.float32).astype(out_ref.dtype)
+    bundle_ref[rows:, :experts] = jnp.broadcast_to(pick, (below, experts))
+
+
+def mark_kernel(pick_ref, twin_ref, slot_expert_ref, out_ref, scratch, *, first):
+    experts = pick_ref.shape[1]
+    slots = slot_expert_ref.shape[1]
+    slot_expert = slot_expert_ref[...]
+    lane = lax.broadcasted_iota(jnp.int32, (1, slots), 1)
+    twin = pltpu.roll(slot_expert, slots // 2, 1)
+    rank = jnp.where((lane >= slots // 2) & (twin == slot_expert), 1.0, 0.0)
+    holds = lax.broadcasted_iota(jnp.int32, (experts, slots), 0) == slot_expert
+    holds = jnp.where(holds, 1.0, 0.0).astype(jnp.bfloat16)
+    half = lax.axis_index("half")
+    own = jnp.dot(pick_ref[...].astype(jnp.bfloat16), holds, preferred_element_type=jnp.float32)
+    other = twin_ref[twin_ref.shape[0] - 16 :, :experts]
+    other = jnp.dot(other, holds, preferred_element_type=jnp.float32)[:1, :]
+    scratch[...] = jnp.zeros_like(scratch)
+    for source in range(2):
+        pick = jnp.where(half == source, own, other)
+        scratch[source : source + 1, :] = jnp.where(pick == rank, 1.0, 0.0)
+    scratch[...] = scratch[...].T
+    places = out_ref.shape[0]
+    held = scratch[pl.ds(pl.multiple_of(half * places, places), places), :]
+    out_ref[...] = pltpu.roll(held, first, 1)
 
 
 def forward_kernel(hidden_ref, weight_ref, out_ref):
     out_ref[...] = jnp.dot(hidden_ref[...], weight_ref[...], preferred_element_type=jnp.float32)
 
 
-def dots_kernel(arrived_ref, outputs_ref, dots_ref, scratch):
-    rows = arrived_ref[:, :, : outputs_ref.shape[1]].reshape(outputs_ref.shape)
+def dots_kernel(arrived_ref, outputs_ref, marks_ref, dots_ref, scratch):
+    rows = arrived_ref[...].reshape(outputs_ref.shape)
     total = jnp.sum(rows.astype(jnp.float32) * outputs_ref[...], axis=1, keepdims=True)
     scratch[...] = jnp.broadcast_to(total, scratch.shape)
-    sources, pair_rows = dots_ref.shape
-    lane = lax.broadcasted_iota(jnp.int32, (sources, scratch.shape[1]), 1)
-    found = scratch[pl.ds(0, sources, stride=pair_rows), :]
-    for p in range(1, pair_rows):
-        found = jnp.where(lane == p, scratch[pl.ds(p, sources, stride=pair_rows), :], found)
-    dots_ref[...] = found[:, :pair_rows]
-
-
-def pick_kernel(returned_ref, target_ref, weight_ref, _, out_ref):
+    places = dots_ref.shape[0]
+    pair_rows = arrived_ref.shape[1]
+    lane = lax.broadcasted_iota(jnp.int32, dots_ref.shape, 1)
+    found = marks_ref[...]
+    for half in range(2):
+        for p in range(pair_rows):
+            part = scratch[pl.ds(half * places * pair_rows + p, places, stride=pair_rows), :]
+            found = jnp.where(lane == half * pair_rows + p, part, found)
+    dots_ref[...] = found
+
+
+def turn_kernel(arrived_ref, _, out_ref, scratch, *, pair_rows, copies):
+    places = arrived_ref.shape[0]
+    scratch[...] = jnp.zeros_like(scratch)
+    scratch[:places, :] = arrived_ref[...]
+    turned = scratch[...].T
+    for half in range(2):
+        row = turned[half * pair_rows : half * pair_rows + 1, :]
+        for p in range(1, pair_rows):
+            other = turned[half * pair_rows + p : half * pair_rows + p + 1, :]
+            row += pltpu.roll(other, p * places, 1)
+        out_ref[half * copies : (half + 1) * copies, :] = jnp.broadcast_to(
+            row, (copies, out_ref.shape[1])
+        )
+
+
+def pick_kernel(returned_ref, target_ref, weight_ref, _, out_ref, scratch, *, places, copies):
     top, tokens = target_ref.shape
-    slots, pair_rows = returned_ref.shape
-    slot = lax.broadcasted_iota(jnp.int32, (slots, tokens), 0)
+    pair_rows = 2
+    scratch[...] = jnp.zeros_like(scratch)
+    for half in range(2):
+        scratch[half : half + 1, :] = jnp.sum(
+            returned_ref[half * copies : (half + 1) * copies, :], axis=0, keepdims=True
+        )
+    returned = scratch[...].T
+    row = lax.broadcasted_iota(jnp.int32, (returned.shape[0], tokens), 0)
     for k in range(top):
         target = target_ref[k : k + 1, :]
-        found = jnp.zeros((slots, tokens), jnp.float32)
-        for p in range(pair_rows):
-            found += jnp.where(slot * pair_rows + p == target, returned_ref[:, p : p + 1], 0.0)
+        slot = target // pair_rows
+        here = row == (target % pair_rows) * places + slot % places
+        found = jnp.where(here, jnp.where(slot < places, returned[:, :1], returned[:, 1:2]), 0.0)
         weight = weight_ref[k : k + 1, :].astype(jnp.bfloat16).astype(jnp.float32)
         out_ref[k : k + 1, :] = jnp.sum(found, axis=0, keepdims=True) / weight
 
 
-def grad_kernel(_, arrived_ref, hidden_ref, twin_hidden_ref, out_ref, order_ref, rows_ref, own_ref):
-    features = out_ref.shape[1]
-    rows = rows_ref.shape[0]
+def grad_kernel(
+    _, arrived_ref, marks_ref, hidden_ref, twin_hidden_ref, out_ref, order_ref, rows_ref, own_ref, *, first
+):
+    places = marks_ref.shape[0]
+    pair_rows = arrived_ref.shape[1]
 
     @pl.when(pl.program_id(0) == 0)
     def _():
-        rows_ref[...] = arrived_ref[:, :, :features].reshape(rows_ref.shape)
-        picked = arrived_ref[:, :, features:].reshape(rows, arrived_ref.shape[2] - features)
-        picked = jnp.sum(picked.astype(jnp.float32), axis=1, keepdims=True)
-        own_ref[...] = jnp.broadcast_to(picked, own_ref.shape)
+        rows_ref[...] = arrived_ref[...].reshape(rows_ref.shape)
+        for half in range(2):
+            mark = jnp.broadcast_to(
+                marks_ref[:, first + half : first + half + 1], (places, own_ref.shape[1])
+            )
+            for p in range(pair_rows):
+                own_ref[pl.ds(half * places * pair_rows + p, places, stride=pair_rows), :] = mark
         order_ref[...] = jnp.zeros_like(order_ref)
 
     own = own_ref[:, :1] > 0.5
@@ -116,6 +171,7 @@
 def on_device(out_grad, route_weight, expert_ids, slot_expert, replica_pick, saved_gu, down_weight):
     ep = ("half", "place")
     sources = lax.axis_size(ep)
+    places, copies = lax.axis_size("place"), lax.axis_size("rep")
     token_count, top_count = expert_ids.shape
     slot_count = slot_expert.shape[0]
     rows_total = saved_gu.shape[1]
@@ -127,21 +183,34 @@
     send_rows, target = pl.pallas_call(
         pack_kernel,
         out_shape=(
-            jax.ShapeDtypeStruct((slot_count, pair_rows, features + slot_count), jnp.bfloat16),
+            jax.ShapeDtypeStruct((slot_count, pair_rows, features), jnp.bfloat16),
             jax.ShapeDtypeStruct((top_count, token_count), jnp.int32),
         ),
         name="pack",
     )(ids_t, weight_t, slot_expert[None], replica_pick, out_grad)
     arrived = lax.all_to_all(send_rows, ep, split_axis=0, concat_axis=0, tiled=True)
-    part = pl.pallas_call(
+    marked = 2 * pair_rows
+    units = saved_gu.shape[3]
+    part, bundle = pl.pallas_call(
         hidden_kernel,
-        out_shape=jax.ShapeDtypeStruct((rows_total, saved_gu.shape[3]), jnp.bfloat16),
+        out_shape=(
+            jax.ShapeDtypeStruct((rows_total, units), jnp.bfloat16),
+            jax.ShapeDtypeStruct((rows_total + 16, units), jnp.bfloat16),
+        ),
         compiler_params=pltpu.CompilerParams(vmem_limit_bytes=8 << 20),
         name="hidden",
-    )(saved_gu[0])
-    twin_part = lax.ppermute(part, "half", [(0, 1), (1, 0)])
+    )(saved_gu[0], replica_pick)
+    bundle = lax.ppermute(bundle, "half", [(0, 1), (1, 0)])
+    marks = pl.pallas_call(
+        functools.partial(mark_kernel, first=marked),
+        in_specs=[pl.BlockSpec(memory_space=pltpu.VMEM)] * 3,
+        out_shape=jax.ShapeDtypeStruct((places, slot_count), jnp.float32),
+        scratch_shapes=[pltpu.VMEM((slot_count, slot_count), jnp.float32)],
+        compiler_params=pltpu.CompilerParams(vmem_limit_bytes=4 << 20),
+        name="marks",
+    )(replica_pick, bundle, slot_expert[None])
     hidden = lax.all_gather(part, "rep", axis=1, tiled=True)
-    twin_hidden = lax.all_gather(twin_part, "rep", axis=1, tiled=True)
+    twin_hidden = lax.all_gather(bundle, "rep", axis=1, tiled=True)
     outputs = pl.pallas_call(
         forward_kernel,
         out_shape=pltpu.VMEM((rows_total, features), jnp.float32),
@@ -150,23 +219,40 @@
     )(hidden, down_weight[0])
     dots = pl.pallas_call(
         dots_kernel,
-        in_specs=[pl.BlockSpec(memory_space=pltpu.VMEM)] * 2,
-        out_shape=jax.ShapeDtypeStruct((sources, pair_rows), jnp.float32),
+        in_specs=[pl.BlockSpec(memory_space=pltpu.VMEM)] * 3,
+        out_shape=jax.ShapeDtypeStruct((places, 128), jnp.float32),
         scratch_shapes=[pltpu.VMEM((rows_total, 128), jnp.float32)],
         compiler_params=pltpu.CompilerParams(vmem_limit_bytes=8 << 20),
         name="dots",
-    )(arrived, outputs)
+    )(arrived, outputs, marks)
+    met = lax.all_to_all(
+        dots.reshape(places, 1, 128), "place", split_axis=0, concat_axis=0, tiled=True
+    ).reshape(places, 128)
+    group = 2 * copies
+    turned = pl.pallas_call(
+        functools.partial(turn_kernel, pair_rows=pair_rows, copies=copies),
+        in_specs=[pl.BlockSpec(memory_space=pltpu.VMEM), pl.BlockSpec(memory_space=pl.ANY)],
+        out_shape=jax.ShapeDtypeStruct((group, 128), jnp.float32),
+        scratch_shapes=[pltpu.VMEM((128, 128), jnp.float32)],
+        compiler_params=pltpu.CompilerParams(vmem_limit_bytes=4 << 20),
+        name="turn",
+    )(met, twin_hidden)
     returned = lax.all_to_all(
-        dots.reshape(sources, 1, pair_rows), ep, split_axis=0, concat_axis=0, tiled=True
+        turned.reshape(group, 1, 128),
+        ("half", "rep"),
+        split_axis=0,
+        concat_axis=0,
+        tiled=True,
     )
     steps = 2
     block = hidden_units // steps
     down_grad, order = pl.pallas_call(
-        grad_kernel,
+        functools.partial(grad_kernel, first=marked),
         grid=(steps,),
         in_specs=[
             pl.BlockSpec(memory_space=pl.ANY),
             pl.BlockSpec(arrived.shape, lambda i: (0, 0, 0)),
+            pl.BlockSpec((places, 128), lambda i: (0, 0)),
             pl.BlockSpec((rows_total, block), lambda i: (0, i)),
             pl.BlockSpec((rows_total, block), lambda i: (0, i)),
         ],
@@ -184,15 +270,16 @@
         ],
         compiler_params=pltpu.CompilerParams(vmem_limit_bytes=24 << 20),
         name="down_grad",
-    )(dots, arrived, hidden, twin_hidden)
-    route_part = pl.pallas_call(
-        pick_kernel,
+    )(turned, arrived, met, hidden, twin_hidden)
+    route_grad = pl.pallas_call(
+        functools.partial(pick_kernel, places=places, copies=copies),
         in_specs=[pl.BlockSpec(memory_space=pltpu.VMEM)] * 3 + [pl.BlockSpec(memory_space=pl.ANY)],
         out_shape=jax.ShapeDtypeStruct((top_count, token_count), jnp.float32),
+        scratch_shapes=[pltpu.VMEM((128, 128), jnp.float32)],
         compiler_params=pltpu.CompilerParams(vmem_limit_bytes=4 << 20),
         name="pick",
-    )(returned.reshape(slot_count, pair_rows), target, weight_t, order)
-    return (down_grad[None], lax.psum(route_part, "rep").T)
+    )(returned.reshape(group, 128), target, weight_t, order)
+    return (down_grad[None], route_grad.T)
 
 
 def solution(mesh):

time: 94 us -> 90.8 us (0.966)
  blocking collectives: 27.8 us -> 18.8 us
  starting transfers between devices: 35.1 us -> 40.3 us
  waiting for transfers between devices: 20.4 us -> 18.8 us
  Pallas kernels: 7.2 us -> 8.66 us
    psum x1 -> x0, blocking collectives: 9 us -> none  [on_device(): return (down_grad[None], lax.psum(route_part, 'rep').T)]
    all_to_all x1 -> x2, starting transfers between devices: 7.78 us -> 13 us  [the longest x1 6.7 us: on_device(): lax.all_to_all(dots.reshape(places, 1, 128), 'place', split_axis=0, conca...]
    all_to_all x1, waiting for transfers between devices: 15.5 us -> 11.4 us  [on_device(): lax.all_to_all(send_rows, ep, split_axis=0, concat_axis=0, tiled=True)]
    all_to_all x1 -> x2, waiting for transfers between devices: 4.92 us -> 7.42 us  [the longest x1 5.05 us: on_device(): lax.all_to_all(dots.reshape(places, 1, 128), 'place', split_axis=0, conca...]
    pallas_call x3 -> x5, Pallas kernels: 3.19 us -> 4.72 us  [the longest x1 2.22 us: on_device(): pl.pallas_call(functools.partial(grad_kernel, first=marked), grid=(steps,...]
    unnamed x8 -> x14, local copies, waits for them, and re-layouts: 2.46 us -> 3.12 us
  transfers between devices with their start and end apart: 3 -> 4, of which waited for: 2 -> 3; matrix products, arithmetic and copies ran while one was open for 0% -> 0% of each run, Pallas kernels for 5% -> 4%
where the time goes in v8:
time: 90.8 us; the launch traced here: 90.4 us
  starting transfers between devices  40.3 us (44%)
  blocking collectives  18.8 us (21%)
  waiting for transfers between devices  18.8 us (21%)
  Pallas kernels  8.66 us (10%)
  local copies, waits for them, and re-layouts  3.12 us (3%)
    all_to_all x1, starting transfers between devices, on_device(): lax.all_to_all(send_rows, ep, split_axis=0, concat_axis=0, tiled=True)  23 us
    all_to_all x1, waiting for transfers between devices, on_device(): lax.all_to_all(send_rows, ep, split_axis=0, concat_axis=0, tiled=True)  11.4 us
    all_gather x1, blocking collectives, on_device(): hidden = lax.all_gather(part, 'rep', axis=1, tiled=True)  10.5 us
    all_gather x1, blocking collectives, on_device(): twin_hidden = lax.all_gather(bundle, 'rep', axis=1, tiled=True)  8.33 us
    all_to_all x1, starting transfers between devices, on_device(): lax.all_to_all(dots.reshape(places, 1, 128), 'place', split_axis=0, conca...  6.7 us
    all_to_all x1, starting transfers between devices, on_device(): lax.all_to_all(turned.reshape(group, 1, 128), ('half', 'rep'), split_axis...  6.32 us
    all_to_all x1, waiting for transfers between devices, on_device(): lax.all_to_all(dots.reshape(places, 1, 128), 'place', split_axis=0, conca...  5.05 us
    ppermute x1, starting transfers between devices, on_device(): bundle = lax.ppermute(bundle, 'half', [(0, 1), (1, 0)])  4.3 us
  transfers between devices with their start and end apart: 4, of which 3 were waited for; matrix products, arithmetic and copies ran while one was open for 0% of the time, Pallas kernels for 4%

profile of v8, /device:TPU:1, one launch (start us, length us, event | category | flops | bytes accessed | tf_op | source)
XLA Modules:
  0.0 90.4 jit_solution(2719090452250291645)
XLA Ops:
  0.6 2.3 %pack.1 = (bf16[128,2,896]{2,1,0:T(2,128)(2,1)}, s32[4,32]{1,0:T(4,128)}) custom-call(s32[4,32]{1,0:T(4,128)} %bitcast.24, f32[4,32]{1,0:T(4,128)} %bitcast.20, s32[1,128]{1,0:T(1,128)} %bitcast.22, s32[1,96]{1,0:T(1,128)} %pick_ref.5, bf16[32,896]{1,0:T(8,128)(2,1)} %grad_ref.1), custom_call_target="tpu_custom_call" | custom-call | tf_op jit(solution)/shard_map/pack/pallas_call | solution.py:183
  2.9 23.0 %all-to-all-start = ((bf16[128,2,896]{2,1,0:T(2,128)(2,1)}), bf16[128,2,896]{2,1,0:T(2,128)(2,1)S(1)}, u32[]{:S(2)}, u32[]{:S(2)}) async-start(bf16[128,2,896]{2,1,0:T(2,128)(2,1)} %get-tuple-element.8), calls=%async_computation | async-start | bytes 917504 | tf_op jit(solution)/shard_map/all_to_all | solution.py:191
  25.9 0.0 copy-start.1
  25.9 0.9 %copy-done.1 = bf16[1,256,2,256]{3,2,1,0:T(2,128)(2,1)S(1)} copy-done((bf16[1,256,2,256]{3,2,1,0:T(2,128)(2,1)S(1)}, bf16[1,256,2,256]{3,2,1,0:T(2,128)(2,1)}, u32[]{:S(2)}) %copy-start.1) | copy-done | bytes 262168
  26.8 0.0 copy-start.3
  26.8 0.7 copy-done.3
  27.5 0.7 hidden.1
  28.1 4.3 %collective-permute-start = (bf16[272,256]{1,0:T(8,128)(2,1)S(1)}, bf16[272,256]{1,0:T(8,128)(2,1)S(1)}, u32[]{:S(2)}, u32[]{:S(2)}) collective-permute-start(bf16[272,256]{1,0:T(8,128)(2,1)S(1)} %get-tuple-element.10), channel_id=1, source_target_pairs={{0,256},{256,0},{1,257},{257,1},{2,258},{258,2},{3,259},{259,3},{4... | collective-permute-start | bytes 417800 | tf_op jit(solution)/shard_map/ppermute | solution.py:203
  32.4 0.0 copy-start.4
  32.4 0.0 copy-start.5
  32.5 10.5 %all_gather.6.hidden_ref = bf16[256,1024]{1,0:T(8,128)(2,1)S(1)} all-gather(bf16[256,256]{1,0:T(8,128)(2,1)S(1)} %get-tuple-element.9), channel_id=1, replica_groups=mesh['half'=2,'place'=64,'rep'=4] {'rep'}, dimensions={1}, use_global_device_ids=true | all-gather | bytes 655360 | tf_op jit(solution)/shard_map/all_gather | solution.py:212
  42.9 0.0 copy-start
  42.9 1.5 %copy-done = bf16[1,1024,896]{2,1,0:T(8,128)(2,1)S(1)} copy-done((bf16[1,1024,896]{2,1,0:T(8,128)(2,1)S(1)}, bf16[1,1024,896]{2,1,0:T(8,128)(2,1)}, u32[]{:S(2)}) %copy-start) | copy-done | bytes 1835032
  44.4 0.7 forward.1.outputs_ref
  45.2 0.0 collective-permute-done.twin_ref
  45.2 0.0 copy-done.4
  45.2 0.0 copy-done.5
  45.2 0.3 marks.1.marks_ref
  45.5 11.4 %all-to-all-done.arrived_ref = bf16[128,2,896]{2,1,0:T(2,128)(2,1)S(1)} async-done(((bf16[128,2,896]{2,1,0:T(2,128)(2,1)}), bf16[128,2,896]{2,1,0:T(2,128)(2,1)S(1)}, u32[]{:S(2)}, u32[]{:S(2)}) %all-to-all-start) | async-done | bytes 458784 | tf_op jit(solution)/shard_map/all_to_all | solution.py:191
  56.9 1.0 %dots.1 = f32[64,128]{1,0:T(8,128)} custom-call(bf16[128,2,896]{2,1,0:T(2,128)(2,1)S(1)} %all-to-all-done.arrived_ref, f32[256,896]{1,0:T(8,128)S(1)} %forward.1.outputs_ref, f32[64,128]{1,0:T(8,128)S(1)} %marks.1.marks_ref), custom_call_target="tpu_custom_call" | custom-call | tf_op jit(solution)/shard_map/dots/pallas_call | solution.py:220
  57.8 0.0 copy-start.2
  57.8 0.0 copy-start.6
  57.8 6.7 %all-to-all-start.1 = ((f32[64,1,128]{2,1,0:T(1,128)}), f32[64,1,128]{2,1,0:T(1,128)S(1)}, u32[]{:S(2)}, u32[]{:S(2)}) async-start(f32[64,1,128]{2,1,0:T(1,128)} %bitcast.6), calls=%async_computation.1 | async-start | bytes 65536 | tf_op jit(solution)/shard_map/all_to_all | solution.py:228
  64.5 8.3 %all_gather.7._.twin_hidden_ref = bf16[272,1024]{1,0:T(8,128)(2,1)S(1)} all-gather(bf16[272,256]{1,0:T(8,128)(2,1)S(1)} %collective-permute-done.twin_ref), channel_id=1, replica_groups=mesh['half'=2,'place'=64,'rep'=4] {'rep'}, dimensions={1}, use_global_device_ids=true | all-gather | bytes 696320 | tf_op jit(solution)/shard_map/all_gather | solution.py:213
  72.9 5.0 %all-to-all-done.1 = f32[64,1,128]{2,1,0:T(1,128)S(1)} async-done(((f32[64,1,128]{2,1,0:T(1,128)}), f32[64,1,128]{2,1,0:T(1,128)S(1)}, u32[]{:S(2)}, u32[]{:S(2)}) %all-to-all-start.1) | async-done | bytes 32800 | tf_op jit(solution)/shard_map/all_to_all | solution.py:228
  77.9 0.7 turn.1._
  78.6 6.3 %all-to-all-start.2 = ((f32[8,1,128]{2,1,0:T(1,128)}), f32[8,1,128]{2,1,0:T(1,128)S(1)}, u32[]{:S(2)}, u32[]{:S(2)}) async-start(f32[8,1,128]{2,1,0:T(1,128)} %bitcast.10), calls=%async_computation.2 | async-start | bytes 8192 | tf_op jit(solution)/shard_map/all_to_all | solution.py:240
  85.0 2.2 %down_grad.1 = (bf16[1024,896]{1,0:T(8,128)(2,1)}, f32[8,128]{1,0:T(8,128)S(1)}) custom-call(f32[8,128]{1,0:T(8,128)} %turn.1._, bf16[128,2,896]{2,1,0:T(2,128)(2,1)S(1)} %all-to-all-done.arrived_ref, f32[64,128]{1,0:T(8,128)S(1)} %bitcast.17, bf16[256,1024]{1,0:T(8,128)(2,1)S(1)} %all_gather.6.hidden_ref, bf16[272,1024]{1,0:T(8,128)(2,1)S(1)} %all_gather.7._.twin_hidden_ref), custom_call_target="tpu_custom_call" | custom-call | tf_op jit(solution)/shard_map/down_grad/pallas_call | solution.py:249
  87.2 2.4 %all-to-all-done.2 = f32[8,1,128]{2,1,0:T(1,128)S(1)} async-done(((f32[8,1,128]{2,1,0:T(1,128)}), f32[8,1,128]{2,1,0:T(1,128)S(1)}, u32[]{:S(2)}, u32[]{:S(2)}) %all-to-all-start.2) | async-done | bytes 4128 | tf_op jit(solution)/shard_map/all_to_all | solution.py:240
  89.6 0.0 copy-done.2
  89.6 0.0 copy-done.6
  89.6 0.8 pick.1
Async XLA Ops:
  2.9 54.0 %all-to-all-start = ((bf16[128,2,896]{2,1,0:T(2,128)(2,1)}), bf16[128,2,896]{2,1,0:T(2,128)(2,1)S(1)}, u32[]{:S(2)}, u32[]{:S(2)}) async-start(bf16[128,2,896]{2,1,0:T(2,128)(2,1)} %get-tuple-element.8), calls=%async_computation | async-start | bytes 917504 | tf_op jit(solution)/shard_map/all_to_all | solution.py:191
  25.9 1.0 %copy-start.1 = (bf16[1,256,2,256]{3,2,1,0:T(2,128)(2,1)S(1)}, bf16[1,256,2,256]{3,2,1,0:T(2,128)(2,1)}, u32[]{:S(2)}) copy-start(bf16[1,256,2,256]{3,2,1,0:T(2,128)(2,1)} %param.12) | copy-start | bytes 786436
  26.8 0.7 copy-start.3
  28.1 17.0 %collective-permute-start = (bf16[272,256]{1,0:T(8,128)(2,1)S(1)}, bf16[272,256]{1,0:T(8,128)(2,1)S(1)}, u32[]{:S(2)}, u32[]{:S(2)}) collective-permute-start(bf16[272,256]{1,0:T(8,128)(2,1)S(1)} %get-tuple-element.10), channel_id=1, source_target_pairs={{0,256},{256,0},{1,257},{257,1},{2,258},{258,2},{3,259},{259,3},{4... | collective-permute-start | bytes 417800 | tf_op jit(solution)/shard_map/ppermute | solution.py:203
  32.4 12.7 %copy-start.4 = (s32[1,96]{1,0:T(1,128)S(1)}, s32[1,96]{1,0:T(1,128)}, u32[]{:S(2)}) copy-start(s32[1,96]{1,0:T(1,128)} %pick_ref.5) | copy-start | bytes 1156
  32.4 12.7 %copy-start.5 = (s32[128]{0:T(128)S(1)}, s32[128]{0:T(128)}, u32[]{:S(2)}) copy-start(s32[128]{0:T(128)} %param.10) | copy-start | bytes 1540
  42.9 1.5 %copy-start = (bf16[1,1024,896]{2,1,0:T(8,128)(2,1)S(1)}, bf16[1,1024,896]{2,1,0:T(8,128)(2,1)}, u32[]{:S(2)}) copy-start(bf16[1,1024,896]{2,1,0:T(8,128)(2,1)} %param.13) | copy-start | bytes 5505028
  57.8 31.7 %copy-start.2 = (f32[32,4]{0,1:T(4,128)S(1)}, f32[32,4]{0,1:T(4,128)}, u32[]{:S(2)}) copy-start(f32[32,4]{0,1:T(4,128)} %param.8) | copy-start | bytes 1540
  57.8 31.7 %copy-start.6 = (s32[4,32]{1,0:T(4,128)S(1)}, s32[4,32]{1,0:T(4,128)}, u32[]{:S(2)}) copy-start(s32[4,32]{1,0:T(4,128)} %get-tuple-element.12.target_ref) | copy-start | bytes 1540
  57.8 20.1 %all-to-all-start.1 = ((f32[64,1,128]{2,1,0:T(1,128)}), f32[64,1,128]{2,1,0:T(1,128)S(1)}, u32[]{:S(2)}, u32[]{:S(2)}) async-start(f32[64,1,128]{2,1,0:T(1,128)} %bitcast.6), calls=%async_computation.1 | async-start | bytes 65536 | tf_op jit(solution)/shard_map/all_to_all | solution.py:228
  78.6 10.9 %all-to-all-start.2 = ((f32[8,1,128]{2,1,0:T(1,128)}), f32[8,1,128]{2,1,0:T(1,128)S(1)}, u32[]{:S(2)}, u32[]{:S(2)}) async-start(f32[8,1,128]{2,1,0:T(1,128)} %bitcast.10), calls=%async_computation.2 | async-start | bytes 8192 | tf_op jit(solution)/shard_map/all_to_all | solution.py:240

commit v9 on v8

--- a/solution.py
+++ b/solution.py
@@ -43,7 +43,7 @@
     )
     place = slot_of * pair_rows + before
     twin_place = twin_of * pair_rows + before
-    row = lax.broadcasted_iota(jnp.int32, (slots * pair_rows, tokens), 0)
+    row = lax.broadcasted_iota(jnp.int32, (slots * pair_rows, tokens), 0) ^ (slots // 4 * pair_rows)
     mix = jnp.zeros((slots * pair_rows, tokens), jnp.float32)
     for k in range(top):
         target = jnp.sum(jnp.where(chosen[k], place, 0.0), axis=0, keepdims=True).astype(jnp.int32)
@@ -53,6 +53,11 @@
         mix += jnp.where(here, weight_ref[k : k + 1, :], 0.0)
     rows = jnp.dot(mix.astype(jnp.bfloat16), grad_ref[...], preferred_element_type=jnp.float32)
     rows_ref[...] = rows.astype(rows_ref.dtype).reshape(rows_ref.shape)
+
+
+def in_place(ref, start, count):
+    middle = count // 2
+    return [ref[start + middle : start + count], ref[start : start + middle]]
 
 
 def hidden_kernel(saved_ref, pick_ref, out_ref, bundle_ref):
@@ -96,24 +101,30 @@
 
 
 def dots_kernel(arrived_ref, outputs_ref, marks_ref, dots_ref, scratch):
-    rows = arrived_ref[...].reshape(outputs_ref.shape)
-    total = jnp.sum(rows.astype(jnp.float32) * outputs_ref[...], axis=1, keepdims=True)
-    scratch[...] = jnp.broadcast_to(total, scratch.shape)
     places = dots_ref.shape[0]
-    pair_rows = arrived_ref.shape[1]
+    pair_rows, features = arrived_ref.shape[1:]
+    size = places // 2 * pair_rows
+    blocks = in_place(arrived_ref, 0, places) + in_place(arrived_ref, places, places)
+    for number, block in enumerate(blocks):
+        here = slice(number * size, (number + 1) * size)
+        rows = block.reshape(size, features).astype(jnp.float32)
+        total = jnp.sum(rows * outputs_ref[here, :], axis=1, keepdims=True)
+        scratch[here, :] = jnp.broadcast_to(total, (size, scratch.shape[1]))
     lane = lax.broadcasted_iota(jnp.int32, dots_ref.shape, 1)
     found = marks_ref[...]
     for half in range(2):
         for p in range(pair_rows):
             part = scratch[pl.ds(half * places * pair_rows + p, places, stride=pair_rows), :]
             found = jnp.where(lane == half * pair_rows + p, part, found)
-    dots_ref[...] = found
+    dots_ref[: places // 2, :] = found[places // 2 :, :]
+    dots_ref[places // 2 :, :] = found[: places // 2, :]
 
 
 def turn_kernel(arrived_ref, _, out_ref, scratch, *, pair_rows, copies):
     places = arrived_ref.shape[0]
     scratch[...] = jnp.zeros_like(scratch)
-    scratch[:places, :] = arrived_ref[...]
+    for number, block in enumerate(in_place(arrived_ref, 0, places)):
+        scratch[number * places // 2 : (number + 1) * places // 2, :] = block
     turned = scratch[...].T
     for half in range(2):
         row = turned[half * pair_rows : half * pair_rows + 1, :]
@@ -152,13 +163,18 @@
 
     @pl.when(pl.program_id(0) == 0)
     def _():
-        rows_ref[...] = arrived_ref[...].reshape(rows_ref.shape)
-        for half in range(2):
+        size = places // 2 * pair_rows
+        blocks = in_place(arrived_ref, 0, places) + in_place(arrived_ref, places, places)
+        for number, block in enumerate(blocks):
+            rows_ref[number * size : (number + 1) * size, :] = block.reshape(size, block.shape[2])
+        marks = in_place(marks_ref, 0, places)
+        for number in range(4):
+            half = number // 2
             mark = jnp.broadcast_to(
-                marks_ref[:, first + half : first + half + 1], (places, own_ref.shape[1])
+                marks[number % 2][:, first + half : first + half + 1], (places // 2, own_ref.shape[1])
             )
             for p in range(pair_rows):
-                own_ref[pl.ds(half * places * pair_rows + p, places, stride=pair_rows), :] = mark
+                own_ref[pl.ds(number * size + p, places // 2, stride=pair_rows), :] = mark
         order_ref[...] = jnp.zeros_like(order_ref)
 
     own = own_ref[:, :1] > 0.5
@@ -188,7 +204,15 @@
         ),
         name="pack",
     )(ids_t, weight_t, slot_expert[None], replica_pick, out_grad)
-    arrived = lax.all_to_all(send_rows, ep, split_axis=0, concat_axis=0, tiled=True)
+    around = [(i + places // 2) % places for i in range(places)]
+    arrived = lax.all_to_all(
+        send_rows,
+        ep,
+        split_axis=0,
+        concat_axis=0,
+        axis_index_groups=[around + [places + i for i in around]],
+        tiled=True,
+    )
     marked = 2 * pair_rows
     units = saved_gu.shape[3]
     part, bundle = pl.pallas_call(
@@ -226,7 +250,12 @@
         name="dots",
     )(arrived, outputs, marks)
     met = lax.all_to_all(
-        dots.reshape(places, 1, 128), "place", split_axis=0, concat_axis=0, tiled=True
+        dots.reshape(places, 1, 128),
+        "place",
+        split_axis=0,
+        concat_axis=0,
+        axis_index_groups=[around],
+        tiled=True,
     ).reshape(places, 128)
     group = 2 * copies
     turned = pl.pallas_call(

time: 90.8 us -> 86.2 us (0.949)
  waiting for transfers between devices: 18.8 us -> 7.07 us
  starting transfers between devices: 40.3 us -> 47.7 us
    all_to_all x1, starting transfers between devices: 6.7 us -> 13.7 us  [on_device(): lax.all_to_all(dots.reshape(places, 1, 128), 'place', split_axis=0, conca...]
    all_to_all x1, waiting for transfers between devices: 11.4 us -> 4.7 us  [on_device(): lax.all_to_all(send_rows, ep, split_axis=0, concat_axis=0, axis_index_gro...]
    all_to_all x1, waiting for transfers between devices: 5.05 us -> 0.01 us  [on_device(): lax.all_to_all(dots.reshape(places, 1, 128), 'place', split_axis=0, conca...]
    all_to_all x1, starting transfers between devices: 6.32 us -> 3.33 us  [on_device(): lax.all_to_all(turned.reshape(group, 1, 128), ('half', 'rep'), split_axis...]
    all_to_all x1, starting transfers between devices: 23 us -> 25.6 us  [on_device(): lax.all_to_all(send_rows, ep, split_axis=0, concat_axis=0, axis_index_gro...]
  transfers between devices with their start and end apart: 4 -> 4, of which waited for: 3 -> 2; matrix products, arithmetic and copies ran while one was open for 0% -> 0% of each run, Pallas kernels for 4% -> 5%
where the time goes in v9:
time: 86.2 us; the launch traced here: 85.7 us
  starting transfers between devices  47.7 us (55%)
  blocking collectives  18.5 us (21%)
  Pallas kernels  8.65 us (10%)
  waiting for transfers between devices  7.07 us (8%)
  local copies, waits for them, and re-layouts  3.12 us (4%)
    all_to_all x1, starting transfers between devices, on_device(): lax.all_to_all(send_rows, ep, split_axis=0, concat_axis=0, axis_index_gro...  25.6 us
    all_to_all x1, starting transfers between devices, on_device(): lax.all_to_all(dots.reshape(places, 1, 128), 'place', split_axis=0, conca...  13.7 us
    all_gather x1, blocking collectives, on_device(): hidden = lax.all_gather(part, 'rep', axis=1, tiled=True)  9.85 us
    all_gather x1, blocking collectives, on_device(): twin_hidden = lax.all_gather(bundle, 'rep', axis=1, tiled=True)  8.61 us
    ppermute x1, starting transfers between devices, on_device(): bundle = lax.ppermute(bundle, 'half', [(0, 1), (1, 0)])  5.03 us
    all_to_all x1, waiting for transfers between devices, on_device(): lax.all_to_all(send_rows, ep, split_axis=0, concat_axis=0, axis_index_gro...  4.7 us
    all_to_all x1, starting transfers between devices, on_device(): lax.all_to_all(turned.reshape(group, 1, 128), ('half', 'rep'), split_axis...  3.33 us
    unnamed x14, local copies, waits for them, and re-layouts  3.12 us
  transfers between devices with their start and end apart: 4, of which 2 were waited for; matrix products, arithmetic and copies ran while one was open for 0% of the time, Pallas kernels for 5%

profile of v9, /device:TPU:1, one launch (start us, length us, event | category | flops | bytes accessed | tf_op | source)
XLA Modules:
  0.0 85.7 jit_solution(15226465645859954778)
XLA Ops:
  0.6 2.2 %pack.1 = (bf16[128,2,896]{2,1,0:T(2,128)(2,1)}, s32[4,32]{1,0:T(4,128)}) custom-call(s32[4,32]{1,0:T(4,128)} %bitcast.24, f32[4,32]{1,0:T(4,128)} %bitcast.20, s32[1,128]{1,0:T(1,128)} %bitcast.22, s32[1,96]{1,0:T(1,128)} %pick_ref.5, bf16[32,896]{1,0:T(8,128)(2,1)} %grad_ref.1), custom_call_target="tpu_custom_call" | custom-call | tf_op jit(solution)/shard_map/pack/pallas_call | solution.py:199
  2.9 25.6 %all-to-all-start = ((bf16[128,2,896]{2,1,0:T(2,128)(2,1)}), bf16[128,2,896]{2,1,0:T(2,128)(2,1)S(1)}, u32[]{:S(2)}, u32[]{:S(2)}) async-start(bf16[128,2,896]{2,1,0:T(2,128)(2,1)} %get-tuple-element.8), calls=%async_computation | async-start | bytes 917504 | tf_op jit(solution)/shard_map/all_to_all | solution.py:208
  28.5 0.0 copy-start.1
  28.5 0.9 %copy-done.1 = bf16[1,256,2,256]{3,2,1,0:T(2,128)(2,1)S(1)} copy-done((bf16[1,256,2,256]{3,2,1,0:T(2,128)(2,1)S(1)}, bf16[1,256,2,256]{3,2,1,0:T(2,128)(2,1)}, u32[]{:S(2)}) %copy-start.1) | copy-done | bytes 262168
  29.5 0.0 copy-start.3
  29.5 0.7 copy-done.3
  30.1 0.7 hidden.1
  30.8 5.0 %collective-permute-start = (bf16[272,256]{1,0:T(8,128)(2,1)S(1)}, bf16[272,256]{1,0:T(8,128)(2,1)S(1)}, u32[]{:S(2)}, u32[]{:S(2)}) collective-permute-start(bf16[272,256]{1,0:T(8,128)(2,1)S(1)} %get-tuple-element.10), channel_id=1, source_target_pairs={{0,256},{256,0},{1,257},{257,1},{2,258},{258,2},{3,259},{259,3},{4... | collective-permute-start | bytes 417800 | tf_op jit(solution)/shard_map/ppermute | solution.py:227
  35.8 0.0 copy-start.4
  35.8 0.0 copy-start.5
  35.9 9.8 %all_gather.6.hidden_ref = bf16[256,1024]{1,0:T(8,128)(2,1)S(1)} all-gather(bf16[256,256]{1,0:T(8,128)(2,1)S(1)} %get-tuple-element.9), channel_id=1, replica_groups=mesh['half'=2,'place'=64,'rep'=4] {'rep'}, dimensions={1}, use_global_device_ids=true | all-gather | bytes 655360 | tf_op jit(solution)/shard_map/all_gather | solution.py:236
  45.7 0.0 copy-start
  45.7 1.5 %copy-done = bf16[1,1024,896]{2,1,0:T(8,128)(2,1)S(1)} copy-done((bf16[1,1024,896]{2,1,0:T(8,128)(2,1)S(1)}, bf16[1,1024,896]{2,1,0:T(8,128)(2,1)}, u32[]{:S(2)}) %copy-start) | copy-done | bytes 1835032
  47.2 0.7 forward.1.outputs_ref
  47.9 0.0 collective-permute-done.twin_ref
  47.9 0.0 copy-done.4
  47.9 0.0 copy-done.5
  48.0 0.3 marks.1.marks_ref
  48.3 4.7 %all-to-all-done.arrived_ref = bf16[128,2,896]{2,1,0:T(2,128)(2,1)S(1)} async-done(((bf16[128,2,896]{2,1,0:T(2,128)(2,1)}), bf16[128,2,896]{2,1,0:T(2,128)(2,1)S(1)}, u32[]{:S(2)}, u32[]{:S(2)}) %all-to-all-start) | async-done | bytes 458784 | tf_op jit(solution)/shard_map/all_to_all | solution.py:208
  52.9 1.0 %dots.1 = f32[64,128]{1,0:T(8,128)} custom-call(bf16[128,2,896]{2,1,0:T(2,128)(2,1)S(1)} %all-to-all-done.arrived_ref, f32[256,896]{1,0:T(8,128)S(1)} %forward.1.outputs_ref, f32[64,128]{1,0:T(8,128)S(1)} %marks.1.marks_ref), custom_call_target="tpu_custom_call" | custom-call | tf_op jit(solution)/shard_map/dots/pallas_call | solution.py:244
  53.9 0.0 copy-start.2
  53.9 0.0 copy-start.6
  53.9 13.7 %all-to-all-start.1 = ((f32[64,1,128]{2,1,0:T(1,128)}), f32[64,1,128]{2,1,0:T(1,128)S(1)}, u32[]{:S(2)}, u32[]{:S(2)}) async-start(f32[64,1,128]{2,1,0:T(1,128)} %bitcast.6), calls=%async_computation.1 | async-start | bytes 65536 | tf_op jit(solution)/shard_map/all_to_all | solution.py:252
  67.6 8.6 %all_gather.7._.twin_hidden_ref = bf16[272,1024]{1,0:T(8,128)(2,1)S(1)} all-gather(bf16[272,256]{1,0:T(8,128)(2,1)S(1)} %collective-permute-done.twin_ref), channel_id=1, replica_groups=mesh['half'=2,'place'=64,'rep'=4] {'rep'}, dimensions={1}, use_global_device_ids=true | all-gather | bytes 696320 | tf_op jit(solution)/shard_map/all_gather | solution.py:237
  76.2 0.0 all-to-all-done.1
  76.2 0.7 turn.1._
  77.0 3.3 %all-to-all-start.2 = ((f32[8,1,128]{2,1,0:T(1,128)}), f32[8,1,128]{2,1,0:T(1,128)S(1)}, u32[]{:S(2)}, u32[]{:S(2)}) async-start(f32[8,1,128]{2,1,0:T(1,128)} %bitcast.10), calls=%async_computation.2 | async-start | bytes 8192 | tf_op jit(solution)/shard_map/all_to_all | solution.py:269
  80.3 2.2 %down_grad.1 = (bf16[1024,896]{1,0:T(8,128)(2,1)}, f32[8,128]{1,0:T(8,128)S(1)}) custom-call(f32[8,128]{1,0:T(8,128)} %turn.1._, bf16[128,2,896]{2,1,0:T(2,128)(2,1)S(1)} %all-to-all-done.arrived_ref, f32[64,128]{1,0:T(8,128)S(1)} %bitcast.17, bf16[256,1024]{1,0:T(8,128)(2,1)S(1)} %all_gather.6.hidden_ref, bf16[272,1024]{1,0:T(8,128)(2,1)S(1)} %all_gather.7._.twin_hidden_ref), custom_call_target="tpu_custom_call" | custom-call | tf_op jit(solution)/shard_map/down_grad/pallas_call | solution.py:278
  82.5 2.4 %all-to-all-done.2 = f32[8,1,128]{2,1,0:T(1,128)S(1)} async-done(((f32[8,1,128]{2,1,0:T(1,128)}), f32[8,1,128]{2,1,0:T(1,128)S(1)}, u32[]{:S(2)}, u32[]{:S(2)}) %all-to-all-start.2) | async-done | bytes 4128 | tf_op jit(solution)/shard_map/all_to_all | solution.py:269
  84.9 0.0 copy-done.2
  84.9 0.0 copy-done.6
  84.9 0.8 pick.1
Async XLA Ops:
  2.9 50.1 %all-to-all-start = ((bf16[128,2,896]{2,1,0:T(2,128)(2,1)}), bf16[128,2,896]{2,1,0:T(2,128)(2,1)S(1)}, u32[]{:S(2)}, u32[]{:S(2)}) async-start(bf16[128,2,896]{2,1,0:T(2,128)(2,1)} %get-tuple-element.8), calls=%async_computation | async-start | bytes 917504 | tf_op jit(solution)/shard_map/all_to_all | solution.py:208
  28.5 1.0 %copy-start.1 = (bf16[1,256,2,256]{3,2,1,0:T(2,128)(2,1)S(1)}, bf16[1,256,2,256]{3,2,1,0:T(2,128)(2,1)}, u32[]{:S(2)}) copy-start(bf16[1,256,2,256]{3,2,1,0:T(2,128)(2,1)} %param.12) | copy-start | bytes 786436
  29.5 0.7 copy-start.3
  30.8 17.1 %collective-permute-start = (bf16[272,256]{1,0:T(8,128)(2,1)S(1)}, bf16[272,256]{1,0:T(8,128)(2,1)S(1)}, u32[]{:S(2)}, u32[]{:S(2)}) collective-permute-start(bf16[272,256]{1,0:T(8,128)(2,1)S(1)} %get-tuple-element.10), channel_id=1, source_target_pairs={{0,256},{256,0},{1,257},{257,1},{2,258},{258,2},{3,259},{259,3},{4... | collective-permute-start | bytes 417800 | tf_op jit(solution)/shard_map/ppermute | solution.py:227
  35.8 12.1 %copy-start.4 = (s32[1,96]{1,0:T(1,128)S(1)}, s32[1,96]{1,0:T(1,128)}, u32[]{:S(2)}) copy-start(s32[1,96]{1,0:T(1,128)} %pick_ref.5) | copy-start | bytes 1156
  35.8 12.1 %copy-start.5 = (s32[128]{0:T(128)S(1)}, s32[128]{0:T(128)}, u32[]{:S(2)}) copy-start(s32[128]{0:T(128)} %param.10) | copy-start | bytes 1540
  45.7 1.5 %copy-start = (bf16[1,1024,896]{2,1,0:T(8,128)(2,1)S(1)}, bf16[1,1024,896]{2,1,0:T(8,128)(2,1)}, u32[]{:S(2)}) copy-start(bf16[1,1024,896]{2,1,0:T(8,128)(2,1)} %param.13) | copy-start | bytes 5505028
  53.9 31.0 %copy-start.2 = (f32[32,4]{0,1:T(4,128)S(1)}, f32[32,4]{0,1:T(4,128)}, u32[]{:S(2)}) copy-start(f32[32,4]{0,1:T(4,128)} %param.8) | copy-start | bytes 1540
  53.9 31.0 %copy-start.6 = (s32[4,32]{1,0:T(4,128)S(1)}, s32[4,32]{1,0:T(4,128)}, u32[]{:S(2)}) copy-start(s32[4,32]{1,0:T(4,128)} %get-tuple-element.12.target_ref) | copy-start | bytes 1540
  53.9 22.3 %all-to-all-start.1 = ((f32[64,1,128]{2,1,0:T(1,128)}), f32[64,1,128]{2,1,0:T(1,128)S(1)}, u32[]{:S(2)}, u32[]{:S(2)}) async-start(f32[64,1,128]{2,1,0:T(1,128)} %bitcast.6), calls=%async_computation.1 | async-start | bytes 65536 | tf_op jit(solution)/shard_map/all_to_all | solution.py:252
  77.0 7.9 %all-to-all-start.2 = ((f32[8,1,128]{2,1,0:T(1,128)}), f32[8,1,128]{2,1,0:T(1,128)S(1)}, u32[]{:S(2)}, u32[]{:S(2)}) async-start(f32[8,1,128]{2,1,0:T(1,128)} %bitcast.10), calls=%async_computation.2 | async-start | bytes 8192 | tf_op jit(solution)/shard_map/all_to_all | solution.py:269

commit v10 on v9

--- a/solution.py
+++ b/solution.py
@@ -60,17 +60,10 @@
     return [ref[start + middle : start + count], ref[start : start + middle]]
 
 
-def hidden_kernel(saved_ref, pick_ref, out_ref, bundle_ref):
+def hidden_kernel(saved_ref, out_ref):
     gate = saved_ref[:, 0, :].astype(jnp.float32)
     up = saved_ref[:, 1, :].astype(jnp.float32)
-    hidden = (gate / (1.0 + jnp.exp(-gate)) * up).astype(out_ref.dtype)
-    out_ref[...] = hidden
-    rows, experts = out_ref.shape[0], pick_ref.shape[1]
-    bundle_ref[:rows, :] = hidden
-    below = bundle_ref.shape[0] - rows
-    bundle_ref[rows:, :] = jnp.zeros((below, out_ref.shape[1]), out_ref.dtype)
-    pick = pick_ref[...].astype(jnp.float32).astype(out_ref.dtype)
-    bundle_ref[rows:, :experts] = jnp.broadcast_to(pick, (below, experts))
+    out_ref[...] = (gate / (1.0 + jnp.exp(-gate)) * up).astype(out_ref.dtype)
 
 
 def mark_kernel(pick_ref, twin_ref, slot_expert_ref, out_ref, scratch, *, first):
@@ -83,9 +76,10 @@
     holds = lax.broadcasted_iota(jnp.int32, (experts, slots), 0) == slot_expert
     holds = jnp.where(holds, 1.0, 0.0).astype(jnp.bfloat16)
     half = lax.axis_index("half")
-    own = jnp.dot(pick_ref[...].astype(jnp.bfloat16), holds, preferred_element_type=jnp.float32)
-    other = twin_ref[twin_ref.shape[0] - 16 :, :experts]
-    other = jnp.dot(other, holds, preferred_element_type=jnp.float32)[:1, :]
+    own, other = (
+        jnp.dot(ref[...].astype(jnp.bfloat16), holds, preferred_element_type=jnp.float32)
+        for ref in (pick_ref, twin_ref)
+    )
     scratch[...] = jnp.zeros_like(scratch)
     for source in range(2):
         pick = jnp.where(half == source, own, other)
@@ -120,7 +114,7 @@
     dots_ref[places // 2 :, :] = found[: places // 2, :]
 
 
-def turn_kernel(arrived_ref, _, out_ref, scratch, *, pair_rows, copies):
+def turn_kernel(arrived_ref, out_ref, scratch, *, pair_rows, copies):
     places = arrived_ref.shape[0]
     scratch[...] = jnp.zeros_like(scratch)
     for number, block in enumerate(in_place(arrived_ref, 0, places)):
@@ -214,17 +208,12 @@
         tiled=True,
     )
     marked = 2 * pair_rows
-    units = saved_gu.shape[3]
-    part, bundle = pl.pallas_call(
+    part = pl.pallas_call(
         hidden_kernel,
-        out_shape=(
-            jax.ShapeDtypeStruct((rows_total, units), jnp.bfloat16),
-            jax.ShapeDtypeStruct((rows_total + 16, units), jnp.bfloat16),
-        ),
-        compiler_params=pltpu.CompilerParams(vmem_limit_bytes=8 << 20),
+        out_shape=jax.ShapeDtypeStruct((rows_total, saved_gu.shape[3]), jnp.bfloat16),
         name="hidden",
-    )(saved_gu[0], replica_pick)
-    bundle = lax.ppermute(bundle, "half", [(0, 1), (1, 0)])
+    )(saved_gu[0])
+    swap = [(0, 1), (1, 0)]
     marks = pl.pallas_call(
         functools.partial(mark_kernel, first=marked),
         in_specs=[pl.BlockSpec(memory_space=pltpu.VMEM)] * 3,
@@ -232,9 +221,9 @@
         scratch_shapes=[pltpu.VMEM((slot_count, slot_count), jnp.float32)],
         compiler_params=pltpu.CompilerParams(vmem_limit_bytes=4 << 20),
         name="marks",
-    )(replica_pick, bundle, slot_expert[None])
+    )(replica_pick, lax.ppermute(replica_pick, "half", swap), slot_expert[None])
     hidden = lax.all_gather(part, "rep", axis=1, tiled=True)
-    twin_hidden = lax.all_gather(bundle, "rep", axis=1, tiled=True)
+    twin_hidden = lax.ppermute(hidden, "half", swap)
     outputs = pl.pallas_call(
         forward_kernel,
         out_shape=pltpu.VMEM((rows_total, features), jnp.float32),
@@ -260,12 +249,11 @@
     group = 2 * copies
     turned = pl.pallas_call(
         functools.partial(turn_kernel, pair_rows=pair_rows, copies=copies),
-        in_specs=[pl.BlockSpec(memory_space=pltpu.VMEM), pl.BlockSpec(memory_space=pl.ANY)],
         out_shape=jax.ShapeDtypeStruct((group, 128), jnp.float32),
         scratch_shapes=[pltpu.VMEM((128, 128), jnp.float32)],
         compiler_params=pltpu.CompilerParams(vmem_limit_bytes=4 << 20),
         name="turn",
-    )(met, twin_hidden)
+    )(met)
     returned = lax.all_to_all(
         turned.reshape(group, 1, 128),
         ("half", "rep"),

time: 86.2 us -> 90.1 us (1.045)
  starting transfers between devices: 47.7 us -> 38.8 us
  blocking collectives: 18.5 us -> 26.8 us
  waiting for transfers between devices: 7.07 us -> 12.3 us
  local copies, waits for them, and re-layouts: 3.12 us -> 1.52 us
  Pallas kernels: 8.65 us -> 9.64 us
    all_to_all x0 -> x1, blocking collectives: none -> 18.2 us  [on_device(): lax.all_to_all(dots.reshape(places, 1, 128), 'place', split_axis=0, conca...]
    all_to_all x1 -> x0, starting transfers between devices: 13.7 us -> none  [on_device(): lax.all_to_all(dots.reshape(places, 1, 128), 'place', split_axis=0, conca...]
    ppermute x1 -> x2, waiting for transfers between devices: 0.01 us -> 9.9 us  [the longest x1 9.9 us: on_device(): lax.ppermute(replica_pick, 'half', swap)]
    all_gather x1 -> x0, blocking collectives: 8.61 us -> none  [on_device(): twin_hidden = lax.all_gather(bundle, 'rep', axis=1, tiled=True)]
    all_to_all x1, waiting for transfers between devices: 4.7 us -> 0.01 us  [on_device(): lax.all_to_all(send_rows, ep, split_axis=0, concat_axis=0, axis_index_gro...]
    all_to_all x1, starting transfers between devices: 3.33 us -> 5.88 us  [on_device(): lax.all_to_all(turned.reshape(group, 1, 128), ('half', 'rep'), split_axis...]
    ppermute x1 -> x2, starting transfers between devices: 5.03 us -> 7.26 us  [the longest x1 5.34 us: on_device(): twin_hidden = lax.ppermute(hidden, 'half', swap)]
    unnamed x14 -> x10, local copies, waits for them, and re-layouts: 3.12 us -> 1.52 us
  transfers between devices with their start and end apart: 4 -> 4, of which waited for: 2 -> 2; matrix products, arithmetic and copies ran while one was open for 0% -> 0% of each run, Pallas kernels for 5% -> 7%
where the time goes in v10:
time: 90.1 us; the launch traced here: 89.7 us
  starting transfers between devices  38.8 us (43%)
  blocking collectives  26.8 us (30%)
  waiting for transfers between devices  12.3 us (14%)
  Pallas kernels  9.64 us (11%)
  local copies, waits for them, and re-layouts  1.52 us (2%)
    all_to_all x1, starting transfers between devices, on_device(): lax.all_to_all(send_rows, ep, split_axis=0, concat_axis=0, axis_index_gro...  25.6 us
    all_to_all x1, blocking collectives, on_device(): lax.all_to_all(dots.reshape(places, 1, 128), 'place', split_axis=0, conca...  18.2 us
    ppermute x1, waiting for transfers between devices, on_device(): lax.ppermute(replica_pick, 'half', swap)  9.9 us
    all_gather x1, blocking collectives, on_device(): hidden = lax.all_gather(part, 'rep', axis=1, tiled=True)  8.53 us
    all_to_all x1, starting transfers between devices, on_device(): lax.all_to_all(turned.reshape(group, 1, 128), ('half', 'rep'), split_axis...  5.88 us
    ppermute x1, starting transfers between devices, on_device(): twin_hidden = lax.ppermute(hidden, 'half', swap)  5.34 us
    all_to_all x1, waiting for transfers between devices, on_device(): lax.all_to_all(turned.reshape(group, 1, 128), ('half', 'rep'), split_axis...  2.35 us
    pallas_call x1, Pallas kernels, on_device(): pl.pallas_call(hidden_kernel, out_shape=jax.ShapeDtypeStruct((rows_total,...  2.25 us
  transfers between devices with their start and end apart: 4, of which 2 were waited for; matrix products, arithmetic and copies ran while one was open for 0% of the time, Pallas kernels for 7%

profile of v10, /device:TPU:1, one launch (start us, length us, event | category | flops | bytes accessed | tf_op | source)
XLA Modules:
  0.0 89.7 jit_solution(6878231196808432052)
XLA Ops:
  0.6 0.0 copy-start.3
  0.6 2.3 %pack.1 = (bf16[128,2,896]{2,1,0:T(2,128)(2,1)}, s32[4,32]{1,0:T(4,128)}) custom-call(s32[4,32]{1,0:T(4,128)} %bitcast.25, f32[4,32]{1,0:T(4,128)} %bitcast.20, s32[1,128]{1,0:T(1,128)} %bitcast.22, s32[1,96]{1,0:T(1,128)} %pick_ref.3, bf16[32,896]{1,0:T(8,128)(2,1)} %grad_ref.1), custom_call_target="tpu_custom_call" | custom-call | tf_op jit(solution)/shard_map/pack/pallas_call | solution.py:193
  2.9 25.6 %all-to-all-start = ((bf16[128,2,896]{2,1,0:T(2,128)(2,1)}), bf16[128,2,896]{2,1,0:T(2,128)(2,1)S(1)}, u32[]{:S(2)}, u32[]{:S(2)}) async-start(bf16[128,2,896]{2,1,0:T(2,128)(2,1)} %get-tuple-element.6), calls=%async_computation | async-start | bytes 917504 | tf_op jit(solution)/shard_map/all_to_all | solution.py:202
  28.5 2.3 %hidden.1 = bf16[256,256]{1,0:T(8,128)(2,1)} custom-call(bf16[256,2,256]{2,1,0:T(2,128)(2,1)} %bitcast.24), custom_call_target="tpu_custom_call" | custom-call | tf_op jit(solution)/shard_map/hidden/pallas_call | solution.py:211
  30.8 0.0 copy-start.2
  30.8 8.5 %all_gather.3.hidden_ref = bf16[256,1024]{1,0:T(8,128)(2,1)S(1)} all-gather(bf16[256,256]{1,0:T(8,128)(2,1)} %hidden.1), channel_id=1, replica_groups=mesh['half'=2,'place'=64,'rep'=4] {'rep'}, dimensions={1}, use_global_device_ids=true | all-gather | bytes 655360 | tf_op jit(solution)/shard_map/all_gather | solution.py:225
  39.3 5.3 %collective-permute-start.1 = (bf16[256,1024]{1,0:T(8,128)(2,1)S(1)}, bf16[256,1024]{1,0:T(8,128)(2,1)S(1)}, u32[]{:S(2)}, u32[]{:S(2)}) collective-permute-start(bf16[256,1024]{1,0:T(8,128)(2,1)S(1)} %all_gather.3.hidden_ref), channel_id=1, source_target_pairs={{0,256},{256,0},{1,257},{257,1},{2,258},{258,2},{3,259},{259,3},{4... | collective-permute-start | bytes 1572872 | tf_op jit(solution)/shard_map/ppermute | solution.py:226
  44.7 0.0 copy-done.3
  44.7 1.9 %collective-permute-start = (s32[1,96]{1,0:T(1,128)S(1)}, s32[1,96]{1,0:T(1,128)S(1)}, u32[]{:S(2)}, u32[]{:S(2)}) collective-permute-start(s32[1,96]{1,0:T(1,128)S(1)} %copy-done.3), channel_id=1, source_target_pairs={{0,256},{256,0},{1,257},{257,1},{2,258},{258,2},{3,259},{259,3},{4... | collective-permute-start | bytes 1160 | tf_op jit(solution)/shard_map/ppermute | solution.py:224
  46.6 0.0 copy-start
  46.6 1.5 %copy-done = bf16[1,1024,896]{2,1,0:T(8,128)(2,1)S(1)} copy-done((bf16[1,1024,896]{2,1,0:T(8,128)(2,1)S(1)}, bf16[1,1024,896]{2,1,0:T(8,128)(2,1)}, u32[]{:S(2)}) %copy-start) | copy-done | bytes 1835032
  48.1 0.7 forward.1.outputs_ref
  48.8 0.0 copy-start.1
  48.8 0.0 copy-start.4
  48.9 9.9 %collective-permute-done.twin_ref = s32[1,96]{1,0:T(1,128)S(1)} collective-permute-done((s32[1,96]{1,0:T(1,128)S(1)}, s32[1,96]{1,0:T(1,128)S(1)}, u32[]{:S(2)}, u32[]{:S(2)}) %collective-permute-start) | collective-permute-done | bytes 416 | tf_op jit(solution)/shard_map/ppermute | solution.py:224
  58.8 0.0 copy-done.2
  58.8 0.3 marks.1.marks_ref
  59.1 0.0 all-to-all-done.arrived_ref
  59.1 0.4 dots.1
  59.4 18.2 %all_to_all.15 = f32[64,1,128]{2,1,0:T(1,128)S(1)} all-to-all(f32[64,1,128]{2,1,0:T(1,128)S(1)} %bitcast.18), channel_id=1, replica_groups={{128,132,136,140,144,148,152,156,160,164,168,172,176,180,184,188,192,19..., dimensions={0} | all-to-all | bytes 65536 | tf_op jit(solution)/shard_map/all_to_all | solution.py:241
  77.7 0.7 turn.1._
  78.4 5.9 %all-to-all-start.2 = ((f32[8,1,128]{2,1,0:T(1,128)}), f32[8,1,128]{2,1,0:T(1,128)S(1)}, u32[]{:S(2)}, u32[]{:S(2)}) async-start(f32[8,1,128]{2,1,0:T(1,128)} %bitcast.10), calls=%async_computation.2 | async-start | bytes 8192 | tf_op jit(solution)/shard_map/all_to_all | solution.py:257
  84.3 0.0 collective-permute-done.1.twin_hidden_ref
  84.3 2.2 %down_grad.1 = (bf16[1024,896]{1,0:T(8,128)(2,1)}, f32[8,128]{1,0:T(8,128)S(1)}) custom-call(f32[8,128]{1,0:T(8,128)} %turn.1._, bf16[128,2,896]{2,1,0:T(2,128)(2,1)S(1)} %all-to-all-done.arrived_ref, f32[64,128]{1,0:T(8,128)S(1)} %bitcast.17, bf16[256,1024]{1,0:T(8,128)(2,1)S(1)} %all_gather.3.hidden_ref, ...), custom_call_target="tpu_custom_call" | custom-call | tf_op jit(solution)/shard_map/down_grad/pallas_call | solution.py:266
  86.5 2.3 %all-to-all-done.2 = f32[8,1,128]{2,1,0:T(1,128)S(1)} async-done(((f32[8,1,128]{2,1,0:T(1,128)}), f32[8,1,128]{2,1,0:T(1,128)S(1)}, u32[]{:S(2)}, u32[]{:S(2)}) %all-to-all-start.2) | async-done | bytes 4128 | tf_op jit(solution)/shard_map/all_to_all | solution.py:257
  88.9 0.0 copy-done.1
  88.9 0.0 copy-done.4
  88.9 0.8 pick.1
Async XLA Ops:
  0.6 44.0 %copy-start.3 = (s32[1,96]{1,0:T(1,128)S(1)}, s32[1,96]{1,0:T(1,128)}, u32[]{:S(2)}) copy-start(s32[1,96]{1,0:T(1,128)} %pick_ref.3) | copy-start | bytes 1156
  2.9 56.2 %all-to-all-start = ((bf16[128,2,896]{2,1,0:T(2,128)(2,1)}), bf16[128,2,896]{2,1,0:T(2,128)(2,1)S(1)}, u32[]{:S(2)}, u32[]{:S(2)}) async-start(bf16[128,2,896]{2,1,0:T(2,128)(2,1)} %get-tuple-element.6), calls=%async_computation | async-start | bytes 917504 | tf_op jit(solution)/shard_map/all_to_all | solution.py:202
  30.8 28.0 %copy-start.2 = (s32[128]{0:T(128)S(1)}, s32[128]{0:T(128)}, u32[]{:S(2)}) copy-start(s32[128]{0:T(128)} %param.10) | copy-start | bytes 1540
  39.3 45.0 %collective-permute-start.1 = (bf16[256,1024]{1,0:T(8,128)(2,1)S(1)}, bf16[256,1024]{1,0:T(8,128)(2,1)S(1)}, u32[]{:S(2)}, u32[]{:S(2)}) collective-permute-start(bf16[256,1024]{1,0:T(8,128)(2,1)S(1)} %all_gather.3.hidden_ref), channel_id=1, source_target_pairs={{0,256},{256,0},{1,257},{257,1},{2,258},{258,2},{3,259},{259,3},{4... | collective-permute-start | bytes 1572872 | tf_op jit(solution)/shard_map/ppermute | solution.py:226
  44.7 14.1 %collective-permute-start = (s32[1,96]{1,0:T(1,128)S(1)}, s32[1,96]{1,0:T(1,128)S(1)}, u32[]{:S(2)}, u32[]{:S(2)}) collective-permute-start(s32[1,96]{1,0:T(1,128)S(1)} %copy-done.3), channel_id=1, source_target_pairs={{0,256},{256,0},{1,257},{257,1},{2,258},{258,2},{3,259},{259,3},{4... | collective-permute-start | bytes 1160 | tf_op jit(solution)/shard_map/ppermute | solution.py:224
  46.6 1.5 %copy-start = (bf16[1,1024,896]{2,1,0:T(8,128)(2,1)S(1)}, bf16[1,1024,896]{2,1,0:T(8,128)(2,1)}, u32[]{:S(2)}) copy-start(bf16[1,1024,896]{2,1,0:T(8,128)(2,1)} %param.13) | copy-start | bytes 5505028
  48.8 40.0 %copy-start.1 = (f32[32,4]{0,1:T(4,128)S(1)}, f32[32,4]{0,1:T(4,128)}, u32[]{:S(2)}) copy-start(f32[32,4]{0,1:T(4,128)} %param.8) | copy-start | bytes 1540
  48.8 40.0 %copy-start.4 = (s32[4,32]{1,0:T(4,128)S(1)}, s32[4,32]{1,0:T(4,128)}, u32[]{:S(2)}) copy-start(s32[4,32]{1,0:T(4,128)} %get-tuple-element.8.target_ref) | copy-start | bytes 1540
  78.4 10.5 %all-to-all-start.2 = ((f32[8,1,128]{2,1,0:T(1,128)}), f32[8,1,128]{2,1,0:T(1,128)S(1)}, u32[]{:S(2)}, u32[]{:S(2)}) async-start(f32[8,1,128]{2,1,0:T(1,128)} %bitcast.10), calls=%async_computation.2 | async-start | bytes 8192 | tf_op jit(solution)/shard_map/all_to_all | solution.py:257

commit v11 on v10

--- a/solution.py
+++ b/solution.py
@@ -88,6 +88,10 @@
     places = out_ref.shape[0]
     held = scratch[pl.ds(pl.multiple_of(half * places, places), places), :]
     out_ref[...] = pltpu.roll(held, first, 1)
+
+
+def pass_kernel(hidden_ref, _, out_ref):
+    out_ref[...] = hidden_ref[...]
 
 
 def forward_kernel(hidden_ref, weight_ref, out_ref):
@@ -211,6 +215,7 @@
     part = pl.pallas_call(
         hidden_kernel,
         out_shape=jax.ShapeDtypeStruct((rows_total, saved_gu.shape[3]), jnp.bfloat16),
+        compiler_params=pltpu.CompilerParams(vmem_limit_bytes=8 << 20),
         name="hidden",
     )(saved_gu[0])
     swap = [(0, 1), (1, 0)]
@@ -223,13 +228,20 @@
         name="marks",
     )(replica_pick, lax.ppermute(replica_pick, "half", swap), slot_expert[None])
     hidden = lax.all_gather(part, "rep", axis=1, tiled=True)
-    twin_hidden = lax.ppermute(hidden, "half", swap)
     outputs = pl.pallas_call(
         forward_kernel,
         out_shape=pltpu.VMEM((rows_total, features), jnp.float32),
         compiler_params=pltpu.CompilerParams(vmem_limit_bytes=12 << 20),
         name="forward",
     )(hidden, down_weight[0])
+    sent = pl.pallas_call(
+        pass_kernel,
+        in_specs=[pl.BlockSpec(memory_space=pltpu.VMEM), pl.BlockSpec(memory_space=pl.ANY)],
+        out_shape=jax.ShapeDtypeStruct(hidden.shape, hidden.dtype),
+        compiler_params=pltpu.CompilerParams(vmem_limit_bytes=4 << 20),
+        name="pass",
+    )(hidden, marks)
+    twin_hidden = lax.ppermute(sent, "half", swap)
     dots = pl.pallas_call(
         dots_kernel,
         in_specs=[pl.BlockSpec(memory_space=pltpu.VMEM)] * 3,

time: 90.1 us -> 82.8 us (0.919)
  waiting for transfers between devices: 12.3 us -> 7.66 us
  Pallas kernels: 9.64 us -> 8.07 us
  blocking collectives: 26.8 us -> 25.6 us
    ppermute x1, waiting for transfers between devices: 9.9 us -> 0.01 us  [on_device(): lax.ppermute(replica_pick, 'half', swap)]
    all_to_all x1, waiting for transfers between devices: 0.01 us -> 5.43 us  [on_device(): lax.all_to_all(send_rows, ep, split_axis=0, concat_axis=0, axis_index_gro...]
    ppermute x1, starting transfers between devices: 1.92 us -> 5.17 us  [on_device(): lax.ppermute(replica_pick, 'half', swap)]
    ppermute x1, starting transfers between devices: 5.34 us -> 3 us  [on_device(): twin_hidden = lax.ppermute(sent, 'half', swap)]
    pallas_call x1, Pallas kernels: 2.25 us -> 0.65 us  [on_device(): pl.pallas_call(hidden_kernel, out_shape=jax.ShapeDtypeStruct((rows_total,...]
  transfers between devices with their start and end apart: 4 -> 4, of which waited for: 2 -> 2; matrix products, arithmetic and copies ran while one was open for 0% -> 0% of each run, Pallas kernels for 7% -> 6%
where the time goes in v11:
time: 82.8 us; the launch traced here: 82.4 us
  starting transfers between devices  39.3 us (47%)
  blocking collectives  25.6 us (31%)
  Pallas kernels  8.07 us (10%)
  waiting for transfers between devices  7.66 us (9%)
  local copies, waits for them, and re-layouts  0.97 us (1%)
    all_to_all x1, starting transfers between devices, on_device(): lax.all_to_all(send_rows, ep, split_axis=0, concat_axis=0, axis_index_gro...  25.6 us
    all_to_all x1, blocking collectives, on_device(): lax.all_to_all(dots.reshape(places, 1, 128), 'place', split_axis=0, conca...  17.5 us
    all_gather x1, blocking collectives, on_device(): hidden = lax.all_gather(part, 'rep', axis=1, tiled=True)  8.07 us
    all_to_all x1, starting transfers between devices, on_device(): lax.all_to_all(turned.reshape(group, 1, 128), ('half', 'rep'), split_axis...  5.51 us
    all_to_all x1, waiting for transfers between devices, on_device(): lax.all_to_all(send_rows, ep, split_axis=0, concat_axis=0, axis_index_gro...  5.43 us
    ppermute x1, starting transfers between devices, on_device(): lax.ppermute(replica_pick, 'half', swap)  5.17 us
    ppermute x1, starting transfers between devices, on_device(): twin_hidden = lax.ppermute(sent, 'half', swap)  3 us
    pallas_call x1, Pallas kernels, on_device(): pl.pallas_call(pack_kernel, out_shape=(jax.ShapeDtypeStruct((slot_count,...  2.25 us
  transfers between devices with their start and end apart: 4, of which 2 were waited for; matrix products, arithmetic and copies ran while one was open for 0% of the time, Pallas kernels for 6%

profile of v11, /device:TPU:1, one launch (start us, length us, event | category | flops | bytes accessed | tf_op | source)
XLA Modules:
  0.0 82.4 jit_solution(4626462665628366370)
XLA Ops:
  0.6 0.0 copy-start.3
  0.6 0.0 copy-start.4
  0.7 2.3 %pack.1 = (bf16[128,2,896]{2,1,0:T(2,128)(2,1)}, s32[4,32]{1,0:T(4,128)}) custom-call(s32[4,32]{1,0:T(4,128)} %bitcast.25, f32[4,32]{1,0:T(4,128)} %bitcast.21, s32[1,128]{1,0:T(1,128)} %bitcast.23, s32[1,96]{1,0:T(1,128)} %pick_ref.3, bf16[32,896]{1,0:T(8,128)(2,1)} %grad_ref.1), custom_call_target="tpu_custom_call" | custom-call | tf_op jit(solution)/shard_map/pack/pallas_call | solution.py:197
  2.9 25.6 %all-to-all-start = ((bf16[128,2,896]{2,1,0:T(2,128)(2,1)}), bf16[128,2,896]{2,1,0:T(2,128)(2,1)S(1)}, u32[]{:S(2)}, u32[]{:S(2)}) async-start(bf16[128,2,896]{2,1,0:T(2,128)(2,1)} %get-tuple-element.6), calls=%async_computation | async-start | bytes 917504 | tf_op jit(solution)/shard_map/all_to_all | solution.py:206
  28.5 0.0 copy-start
  28.6 5.2 %collective-permute-start = (s32[1,96]{1,0:T(1,128)}, s32[1,96]{1,0:T(1,128)S(1)}, u32[]{:S(2)}, u32[]{:S(2)}) collective-permute-start(s32[1,96]{1,0:T(1,128)} %pick_ref.3), channel_id=1, source_target_pairs={{0,256},{256,0},{1,257},{257,1},{2,258},{258,2},{3,259},{259,3},{4... | collective-permute-start | bytes 1160 | tf_op jit(solution)/shard_map/ppermute | solution.py:229
  33.7 0.0 copy-start.1
  33.7 0.9 %copy-done.1 = bf16[1,256,2,256]{3,2,1,0:T(2,128)(2,1)S(1)} copy-done((bf16[1,256,2,256]{3,2,1,0:T(2,128)(2,1)S(1)}, bf16[1,256,2,256]{3,2,1,0:T(2,128)(2,1)}, u32[]{:S(2)}) %copy-start.1) | copy-done | bytes 262168
  34.7 0.7 hidden.1
  35.3 8.1 %all_gather.3.hidden_ref = bf16[256,1024]{1,0:T(8,128)(2,1)S(1)} all-gather(bf16[256,256]{1,0:T(8,128)(2,1)S(1)} %hidden.1), channel_id=1, replica_groups=mesh['half'=2,'place'=64,'rep'=4] {'rep'}, dimensions={1}, use_global_device_ids=true | all-gather | bytes 655360 | tf_op jit(solution)/shard_map/all_gather | solution.py:230
  43.4 0.0 collective-permute-done.twin_ref
  43.4 0.0 copy-done.3
  43.4 0.0 copy-done.4
  43.4 0.3 marks.1.marks_ref._
  43.8 3.0 %collective-permute-start.1 = (bf16[256,1024]{1,0:T(8,128)(2,1)S(1)}, bf16[256,1024]{1,0:T(8,128)(2,1)S(1)}, u32[]{:S(2)}, u32[]{:S(2)}) collective-permute-start(bf16[256,1024]{1,0:T(8,128)(2,1)S(1)} %pass.1), channel_id=1, source_target_pairs={{0,256},{256,0},{1,257},{257,1},{2,258},{258,2},{3,259},{259,3},{4... | collective-permute-start | bytes 1572872 | tf_op jit(solution)/shard_map/ppermute | solution.py:244
  46.8 0.0 copy-done
  46.8 0.7 forward.1.outputs_ref
  47.5 0.0 copy-start.2
  47.5 0.0 copy-start.5
  47.5 5.4 %all-to-all-done.arrived_ref = bf16[128,2,896]{2,1,0:T(2,128)(2,1)S(1)} async-done(((bf16[128,2,896]{2,1,0:T(2,128)(2,1)}), bf16[128,2,896]{2,1,0:T(2,128)(2,1)S(1)}, u32[]{:S(2)}, u32[]{:S(2)}) %all-to-all-start) | async-done | bytes 458784 | tf_op jit(solution)/shard_map/all_to_all | solution.py:206
  53.0 0.4 dots.1
  53.3 17.5 %all_to_all.15 = f32[64,1,128]{2,1,0:T(1,128)S(1)} all-to-all(f32[64,1,128]{2,1,0:T(1,128)S(1)} %bitcast.19), channel_id=1, replica_groups={{128,132,136,140,144,148,152,156,160,164,168,172,176,180,184,188,192,19..., dimensions={0} | all-to-all | bytes 65536 | tf_op jit(solution)/shard_map/all_to_all | solution.py:253
  70.9 0.7 turn.1._
  71.6 5.5 %all-to-all-start.2 = ((f32[8,1,128]{2,1,0:T(1,128)}), f32[8,1,128]{2,1,0:T(1,128)S(1)}, u32[]{:S(2)}, u32[]{:S(2)}) async-start(f32[8,1,128]{2,1,0:T(1,128)} %bitcast.10), calls=%async_computation.2 | async-start | bytes 8192 | tf_op jit(solution)/shard_map/all_to_all | solution.py:269
  77.1 0.0 collective-permute-done.1.twin_hidden_ref
  77.1 2.2 %down_grad.1 = (bf16[1024,896]{1,0:T(8,128)(2,1)}, f32[8,128]{1,0:T(8,128)S(1)}) custom-call(f32[8,128]{1,0:T(8,128)} %turn.1._, bf16[128,2,896]{2,1,0:T(2,128)(2,1)S(1)} %all-to-all-done.arrived_ref, f32[64,128]{1,0:T(8,128)S(1)} %bitcast.17, bf16[256,1024]{1,0:T(8,128)(2,1)S(1)} %all_gather.3.hidden_ref, ...), custom_call_target="tpu_custom_call" | custom-call | tf_op jit(solution)/shard_map/down_grad/pallas_call | solution.py:278
  79.3 2.2 %all-to-all-done.2 = f32[8,1,128]{2,1,0:T(1,128)S(1)} async-done(((f32[8,1,128]{2,1,0:T(1,128)}), f32[8,1,128]{2,1,0:T(1,128)S(1)}, u32[]{:S(2)}, u32[]{:S(2)}) %all-to-all-start.2) | async-done | bytes 4128 | tf_op jit(solution)/shard_map/all_to_all | solution.py:269
  81.5 0.0 copy-done.2
  81.5 0.0 copy-done.5
  81.6 0.8 pick.1
  (1 shorter events, 0.0 us)
Async XLA Ops:
  0.6 42.8 %copy-start.3 = (s32[128]{0:T(128)S(1)}, s32[128]{0:T(128)}, u32[]{:S(2)}) copy-start(s32[128]{0:T(128)} %param.10) | copy-start | bytes 1540
  0.6 42.8 %copy-start.4 = (s32[1,96]{1,0:T(1,128)S(1)}, s32[1,96]{1,0:T(1,128)}, u32[]{:S(2)}) copy-start(s32[1,96]{1,0:T(1,128)} %pick_ref.3) | copy-start | bytes 1156
  2.9 50.1 %all-to-all-start = ((bf16[128,2,896]{2,1,0:T(2,128)(2,1)}), bf16[128,2,896]{2,1,0:T(2,128)(2,1)S(1)}, u32[]{:S(2)}, u32[]{:S(2)}) async-start(bf16[128,2,896]{2,1,0:T(2,128)(2,1)} %get-tuple-element.6), calls=%async_computation | async-start | bytes 917504 | tf_op jit(solution)/shard_map/all_to_all | solution.py:206
  28.5 18.2 %copy-start = (bf16[1,1024,896]{2,1,0:T(8,128)(2,1)S(1)}, bf16[1,1024,896]{2,1,0:T(8,128)(2,1)}, u32[]{:S(2)}) copy-start(bf16[1,1024,896]{2,1,0:T(8,128)(2,1)} %param.13) | copy-start | bytes 5505028
  28.6 14.9 %collective-permute-start = (s32[1,96]{1,0:T(1,128)}, s32[1,96]{1,0:T(1,128)S(1)}, u32[]{:S(2)}, u32[]{:S(2)}) collective-permute-start(s32[1,96]{1,0:T(1,128)} %pick_ref.3), channel_id=1, source_target_pairs={{0,256},{256,0},{1,257},{257,1},{2,258},{258,2},{3,259},{259,3},{4... | collective-permute-start | bytes 1160 | tf_op jit(solution)/shard_map/ppermute | solution.py:229
  33.7 1.0 %copy-start.1 = (bf16[1,256,2,256]{3,2,1,0:T(2,128)(2,1)S(1)}, bf16[1,256,2,256]{3,2,1,0:T(2,128)(2,1)}, u32[]{:S(2)}) copy-start(bf16[1,256,2,256]{3,2,1,0:T(2,128)(2,1)} %param.12) | copy-start | bytes 786436
  43.8 33.3 %collective-permute-start.1 = (bf16[256,1024]{1,0:T(8,128)(2,1)S(1)}, bf16[256,1024]{1,0:T(8,128)(2,1)S(1)}, u32[]{:S(2)}, u32[]{:S(2)}) collective-permute-start(bf16[256,1024]{1,0:T(8,128)(2,1)S(1)} %pass.1), channel_id=1, source_target_pairs={{0,256},{256,0},{1,257},{257,1},{2,258},{258,2},{3,259},{259,3},{4... | collective-permute-start | bytes 1572872 | tf_op jit(solution)/shard_map/ppermute | solution.py:244
  47.5 34.0 %copy-start.2 = (f32[32,4]{0,1:T(4,128)S(1)}, f32[32,4]{0,1:T(4,128)}, u32[]{:S(2)}) copy-start(f32[32,4]{0,1:T(4,128)} %param.8) | copy-start | bytes 1540
  47.5 34.0 %copy-start.5 = (s32[4,32]{1,0:T(4,128)S(1)}, s32[4,32]{1,0:T(4,128)}, u32[]{:S(2)}) copy-start(s32[4,32]{1,0:T(4,128)} %get-tuple-element.8.target_ref) | copy-start | bytes 1540
  71.6 10.0 %all-to-all-start.2 = ((f32[8,1,128]{2,1,0:T(1,128)}), f32[8,1,128]{2,1,0:T(1,128)S(1)}, u32[]{:S(2)}, u32[]{:S(2)}) async-start(f32[8,1,128]{2,1,0:T(1,128)} %bitcast.10), calls=%async_computation.2 | async-start | bytes 8192 | tf_op jit(solution)/shard_map/all_to_all | solution.py:269

commit v12 on v11

--- a/solution.py
+++ b/solution.py
@@ -6,6 +6,31 @@
 from jax.experimental import pallas as pl
 from jax.experimental.pallas import tpu as pltpu
 from jax.sharding import Mesh, PartitionSpec as P
+
+
+DISPATCH_FIRST = 114
+PLACE_FIRST = 34
+LINE_FIRST = 4
+
+
+def turned_order(count, first):
+    return [[m ^ first for m in range(count)]]
+
+
+def sources_of(ref):
+    step = DISPATCH_FIRST & -DISPATCH_FIRST
+    return jnp.concatenate(
+        [ref[k ^ DISPATCH_FIRST : (k ^ DISPATCH_FIRST) + step] for k in range(0, ref.shape[0], step)],
+        axis=0,
+    )
+
+
+def swap_places(rows):
+    count = rows.shape[0]
+    row = lax.broadcasted_iota(jnp.int32, rows.shape, 0)
+    for bit in (b for b in (1, 2, 4, 8, 16, 32) if b & PLACE_FIRST):
+        rows = jnp.where(row & bit == 0, pltpu.roll(rows, count - bit, 0), pltpu.roll(rows, bit, 0))
+    return rows
 
 
 def pack_kernel(ids_ref, weight_ref, slot_expert_ref, pick_ref, grad_ref, rows_ref, target_ref):
@@ -43,7 +68,8 @@
     )
     place = slot_of * pair_rows + before
     twin_place = twin_of * pair_rows + before
-    row = lax.broadcasted_iota(jnp.int32, (slots * pair_rows, tokens), 0) ^ (slots // 4 * pair_rows)
+    row = lax.broadcasted_iota(jnp.int32, (slots * pair_rows, tokens), 0)
+    row = row ^ (DISPATCH_FIRST * pair_rows)
     mix = jnp.zeros((slots * pair_rows, tokens), jnp.float32)
     for k in range(top):
         target = jnp.sum(jnp.where(chosen[k], place, 0.0), axis=0, keepdims=True).astype(jnp.int32)
@@ -53,11 +79,6 @@
         mix += jnp.where(here, weight_ref[k : k + 1, :], 0.0)
     rows = jnp.dot(mix.astype(jnp.bfloat16), grad_ref[...], preferred_element_type=jnp.float32)
     rows_ref[...] = rows.astype(rows_ref.dtype).reshape(rows_ref.shape)
-
-
-def in_place(ref, start, count):
-    middle = count // 2
-    return [ref[start + middle : start + count], ref[start : start + middle]]
 
 
 def hidden_kernel(saved_ref, out_ref):
@@ -100,38 +121,31 @@
 
 def dots_kernel(arrived_ref, outputs_ref, marks_ref, dots_ref, scratch):
     places = dots_ref.shape[0]
-    pair_rows, features = arrived_ref.shape[1:]
-    size = places // 2 * pair_rows
-    blocks = in_place(arrived_ref, 0, places) + in_place(arrived_ref, places, places)
-    for number, block in enumerate(blocks):
-        here = slice(number * size, (number + 1) * size)
-        rows = block.reshape(size, features).astype(jnp.float32)
-        total = jnp.sum(rows * outputs_ref[here, :], axis=1, keepdims=True)
-        scratch[here, :] = jnp.broadcast_to(total, (size, scratch.shape[1]))
+    pair_rows = arrived_ref.shape[1]
+    rows = sources_of(arrived_ref).reshape(outputs_ref.shape)
+    total = jnp.sum(rows.astype(jnp.float32) * outputs_ref[...], axis=1, keepdims=True)
+    scratch[...] = jnp.broadcast_to(total, scratch.shape)
     lane = lax.broadcasted_iota(jnp.int32, dots_ref.shape, 1)
     found = marks_ref[...]
     for half in range(2):
         for p in range(pair_rows):
             part = scratch[pl.ds(half * places * pair_rows + p, places, stride=pair_rows), :]
             found = jnp.where(lane == half * pair_rows + p, part, found)
-    dots_ref[: places // 2, :] = found[places // 2 :, :]
-    dots_ref[places // 2 :, :] = found[: places // 2, :]
+    dots_ref[...] = swap_places(found)
 
 
 def turn_kernel(arrived_ref, out_ref, scratch, *, pair_rows, copies):
     places = arrived_ref.shape[0]
     scratch[...] = jnp.zeros_like(scratch)
-    for number, block in enumerate(in_place(arrived_ref, 0, places)):
-        scratch[number * places // 2 : (number + 1) * places // 2, :] = block
+    scratch[:places, :] = arrived_ref[...]
     turned = scratch[...].T
     for half in range(2):
         row = turned[half * pair_rows : half * pair_rows + 1, :]
         for p in range(1, pair_rows):
             other = turned[half * pair_rows + p : half * pair_rows + p + 1, :]
             row += pltpu.roll(other, p * places, 1)
-        out_ref[half * copies : (half + 1) * copies, :] = jnp.broadcast_to(
-            row, (copies, out_ref.shape[1])
-        )
+        start = half * copies ^ LINE_FIRST
+        out_ref[start : start + copies, :] = jnp.broadcast_to(row, (copies, out_ref.shape[1]))
 
 
 def pick_kernel(returned_ref, target_ref, weight_ref, _, out_ref, scratch, *, places, copies):
@@ -139,15 +153,16 @@
     pair_rows = 2
     scratch[...] = jnp.zeros_like(scratch)
     for half in range(2):
+        start = half * copies ^ LINE_FIRST
         scratch[half : half + 1, :] = jnp.sum(
-            returned_ref[half * copies : (half + 1) * copies, :], axis=0, keepdims=True
+            returned_ref[start : start + copies, :], axis=0, keepdims=True
         )
     returned = scratch[...].T
     row = lax.broadcasted_iota(jnp.int32, (returned.shape[0], tokens), 0)
     for k in range(top):
         target = target_ref[k : k + 1, :]
         slot = target // pair_rows
-        here = row == (target % pair_rows) * places + slot % places
+        here = row == (target % pair_rows) * places + (slot % places ^ PLACE_FIRST)
         found = jnp.where(here, jnp.where(slot < places, returned[:, :1], returned[:, 1:2]), 0.0)
         weight = weight_ref[k : k + 1, :].astype(jnp.bfloat16).astype(jnp.float32)
         out_ref[k : k + 1, :] = jnp.sum(found, axis=0, keepdims=True) / weight
@@ -161,18 +176,12 @@
 
     @pl.when(pl.program_id(0) == 0)
     def _():
-        size = places // 2 * pair_rows
-        blocks = in_place(arrived_ref, 0, places) + in_place(arrived_ref, places, places)
-        for number, block in enumerate(blocks):
-            rows_ref[number * size : (number + 1) * size, :] = block.reshape(size, block.shape[2])
-        marks = in_place(marks_ref, 0, places)
-        for number in range(4):
-            half = number // 2
-            mark = jnp.broadcast_to(
-                marks[number % 2][:, first + half : first + half + 1], (places // 2, own_ref.shape[1])
-            )
+        rows_ref[...] = sources_of(arrived_ref).reshape(rows_ref.shape)
+        marks = swap_places(marks_ref[...])
+        for half in range(2):
+            mark = jnp.broadcast_to(marks[:, first + half : first + half + 1], marks.shape)
             for p in range(pair_rows):
-                own_ref[pl.ds(number * size + p, places // 2, stride=pair_rows), :] = mark
+                own_ref[pl.ds(half * places * pair_rows + p, places, stride=pair_rows), :] = mark
         order_ref[...] = jnp.zeros_like(order_ref)
 
     own = own_ref[:, :1] > 0.5
@@ -202,13 +211,12 @@
         ),
         name="pack",
     )(ids_t, weight_t, slot_expert[None], replica_pick, out_grad)
-    around = [(i + places // 2) % places for i in range(places)]
     arrived = lax.all_to_all(
         send_rows,
         ep,
         split_axis=0,
         concat_axis=0,
-        axis_index_groups=[around + [places + i for i in around]],
+        axis_index_groups=turned_order(sources, DISPATCH_FIRST),
         tiled=True,
     )
     marked = 2 * pair_rows
@@ -255,7 +263,7 @@
         "place",
         split_axis=0,
         concat_axis=0,
-        axis_index_groups=[around],
+        axis_index_groups=turned_order(places, PLACE_FIRST),
         tiled=True,
     ).reshape(places, 128)
     group = 2 * copies
@@ -271,6 +279,7 @@
         ("half", "rep"),
         split_axis=0,
         concat_axis=0,
+        axis_index_groups=turned_order(group, LINE_FIRST),
         tiled=True,
     )
     steps = 2

time: 82.8 us -> 80.5 us (0.972)
  waiting for transfers between devices: 7.66 us -> 4.2 us
  starting transfers between devices: 39.3 us -> 40.7 us
    all_to_all x1, starting transfers between devices: 5.51 us -> 9.47 us  [on_device(): lax.all_to_all(turned.reshape(group, 1, 128), ('half', 'rep'), split_axis...]
    ppermute x1, starting transfers between devices: 5.17 us -> 2.05 us  [on_device(): lax.ppermute(replica_pick, 'half', swap)]
    ppermute x1, starting transfers between devices: 3 us -> 5.58 us  [on_device(): twin_hidden = lax.ppermute(sent, 'half', swap)]
    all_to_all x1, waiting for transfers between devices: 2.22 us -> 0.01 us  [on_device(): lax.all_to_all(turned.reshape(group, 1, 128), ('half', 'rep'), split_axis...]
    all_to_all x1, starting transfers between devices: 25.6 us -> 23.6 us  [on_device(): lax.all_to_all(send_rows, ep, split_axis=0, concat_axis=0, axis_index_gro...]
    all_to_all x1, blocking collectives: 17.5 us -> 16.1 us  [on_device(): lax.all_to_all(dots.reshape(places, 1, 128), 'place', split_axis=0, conca...]
    all_to_all x1, waiting for transfers between devices: 5.43 us -> 4.2 us  [on_device(): lax.all_to_all(send_rows, ep, split_axis=0, concat_axis=0, axis_index_gro...]
    all_gather x1, blocking collectives: 8.07 us -> 9.22 us  [on_device(): hidden = lax.all_gather(part, 'rep', axis=1, tiled=True)]
  transfers between devices with their start and end apart: 4 -> 4, of which waited for: 2 -> 1; matrix products, arithmetic and copies ran while one was open for 0% -> 0% of each run, Pallas kernels for 6% -> 6%
where the time goes in v12:
time: 80.5 us; the launch traced here: 80.1 us
  starting transfers between devices  40.7 us (51%)
  blocking collectives  25.3 us (31%)
  Pallas kernels  8.14 us (10%)
  waiting for transfers between devices  4.2 us (5%)
  local copies, waits for them, and re-layouts  0.97 us (1%)
    all_to_all x1, starting transfers between devices, on_device(): lax.all_to_all(send_rows, ep, split_axis=0, concat_axis=0, axis_index_gro...  23.6 us
    all_to_all x1, blocking collectives, on_device(): lax.all_to_all(dots.reshape(places, 1, 128), 'place', split_axis=0, conca...  16.1 us
    all_to_all x1, starting transfers between devices, on_device(): lax.all_to_all(turned.reshape(group, 1, 128), ('half', 'rep'), split_axis...  9.47 us
    all_gather x1, blocking collectives, on_device(): hidden = lax.all_gather(part, 'rep', axis=1, tiled=True)  9.22 us
    ppermute x1, starting transfers between devices, on_device(): twin_hidden = lax.ppermute(sent, 'half', swap)  5.58 us
    all_to_all x1, waiting for transfers between devices, on_device(): lax.all_to_all(send_rows, ep, split_axis=0, concat_axis=0, axis_index_gro...  4.2 us
    pallas_call x1, Pallas kernels, on_device(): pl.pallas_call(functools.partial(grad_kernel, first=marked), grid=(steps,...  2.29 us
    pallas_call x1, Pallas kernels, on_device(): pl.pallas_call(pack_kernel, out_shape=(jax.ShapeDtypeStruct((slot_count,...  2.25 us
  transfers between devices with their start and end apart: 4, of which 1 were waited for; matrix products, arithmetic and copies ran while one was open for 0% of the time, Pallas kernels for 6%

profile of v12, /device:TPU:1, one launch (start us, length us, event | category | flops | bytes accessed | tf_op | source)
XLA Modules:
  0.0 80.1 jit_solution(1675056646697065292)
XLA Ops:
  0.6 0.0 copy-start.3
  0.6 0.0 copy-start.4
  0.7 2.3 %pack.1 = (bf16[128,2,896]{2,1,0:T(2,128)(2,1)}, s32[4,32]{1,0:T(4,128)}) custom-call(s32[4,32]{1,0:T(4,128)} %bitcast.25, f32[4,32]{1,0:T(4,128)} %bitcast.21, s32[1,128]{1,0:T(1,128)} %bitcast.23, s32[1,96]{1,0:T(1,128)} %pick_ref.3, bf16[32,896]{1,0:T(8,128)(2,1)} %grad_ref.1), custom_call_target="tpu_custom_call" | custom-call | tf_op jit(solution)/shard_map/pack/pallas_call | solution.py:206
  2.9 23.6 %all-to-all-start = ((bf16[128,2,896]{2,1,0:T(2,128)(2,1)}), bf16[128,2,896]{2,1,0:T(2,128)(2,1)S(1)}, u32[]{:S(2)}, u32[]{:S(2)}) async-start(bf16[128,2,896]{2,1,0:T(2,128)(2,1)} %get-tuple-element.6), calls=%async_computation | async-start | bytes 917504 | tf_op jit(solution)/shard_map/all_to_all | solution.py:214
  26.6 0.0 copy-start
  26.6 2.1 %collective-permute-start = (s32[1,96]{1,0:T(1,128)}, s32[1,96]{1,0:T(1,128)S(1)}, u32[]{:S(2)}, u32[]{:S(2)}) collective-permute-start(s32[1,96]{1,0:T(1,128)} %pick_ref.3), channel_id=1, source_target_pairs={{0,256},{256,0},{1,257},{257,1},{2,258},{258,2},{3,259},{259,3},{4... | collective-permute-start | bytes 1160 | tf_op jit(solution)/shard_map/ppermute | solution.py:237
  28.6 0.0 copy-start.1
  28.6 0.9 %copy-done.1 = bf16[1,256,2,256]{3,2,1,0:T(2,128)(2,1)S(1)} copy-done((bf16[1,256,2,256]{3,2,1,0:T(2,128)(2,1)S(1)}, bf16[1,256,2,256]{3,2,1,0:T(2,128)(2,1)}, u32[]{:S(2)}) %copy-start.1) | copy-done | bytes 262168
  29.6 0.7 hidden.1
  30.2 9.2 %all_gather.3.hidden_ref = bf16[256,1024]{1,0:T(8,128)(2,1)S(1)} all-gather(bf16[256,256]{1,0:T(8,128)(2,1)S(1)} %hidden.1), channel_id=1, replica_groups=mesh['half'=2,'place'=64,'rep'=4] {'rep'}, dimensions={1}, use_global_device_ids=true | all-gather | bytes 655360 | tf_op jit(solution)/shard_map/all_gather | solution.py:238
  39.5 0.0 collective-permute-done.twin_ref
  39.5 0.0 copy-done.3
  39.5 0.0 copy-done.4
  39.5 0.3 marks.1.marks_ref._
  39.8 5.6 %collective-permute-start.1 = (bf16[256,1024]{1,0:T(8,128)(2,1)S(1)}, bf16[256,1024]{1,0:T(8,128)(2,1)S(1)}, u32[]{:S(2)}, u32[]{:S(2)}) collective-permute-start(bf16[256,1024]{1,0:T(8,128)(2,1)S(1)} %pass.1), channel_id=1, source_target_pairs={{0,256},{256,0},{1,257},{257,1},{2,258},{258,2},{3,259},{259,3},{4... | collective-permute-start | bytes 1572872 | tf_op jit(solution)/shard_map/ppermute | solution.py:252
  45.4 0.0 copy-done
  45.4 0.7 forward.1.outputs_ref
  46.1 0.0 copy-start.2
  46.1 0.0 copy-start.5
  46.2 4.2 %all-to-all-done.arrived_ref = bf16[128,2,896]{2,1,0:T(2,128)(2,1)S(1)} async-done(((bf16[128,2,896]{2,1,0:T(2,128)(2,1)}), bf16[128,2,896]{2,1,0:T(2,128)(2,1)S(1)}, u32[]{:S(2)}, u32[]{:S(2)}) %all-to-all-start) | async-done | bytes 458784 | tf_op jit(solution)/shard_map/all_to_all | solution.py:214
  50.4 0.4 dots.1
  50.7 16.1 %all_to_all.15 = f32[64,1,128]{2,1,0:T(1,128)S(1)} all-to-all(f32[64,1,128]{2,1,0:T(1,128)S(1)} %bitcast.19), channel_id=1, replica_groups={{136,140,128,132,152,156,144,148,168,172,160,164,184,188,176,180,200,20..., dimensions={0} | all-to-all | bytes 65536 | tf_op jit(solution)/shard_map/all_to_all | solution.py:261
  66.8 0.7 turn.1._
  67.5 9.5 %all-to-all-start.2 = ((f32[8,1,128]{2,1,0:T(1,128)}), f32[8,1,128]{2,1,0:T(1,128)S(1)}, u32[]{:S(2)}, u32[]{:S(2)}) async-start(f32[8,1,128]{2,1,0:T(1,128)} %bitcast.10), calls=%async_computation.2 | async-start | bytes 8192 | tf_op jit(solution)/shard_map/all_to_all | solution.py:277
  77.0 0.0 collective-permute-done.1.twin_hidden_ref
  77.0 2.3 %down_grad.1 = (bf16[1024,896]{1,0:T(8,128)(2,1)}, f32[8,128]{1,0:T(8,128)S(1)}) custom-call(f32[8,128]{1,0:T(8,128)} %turn.1._, bf16[128,2,896]{2,1,0:T(2,128)(2,1)S(1)} %all-to-all-done.arrived_ref, f32[64,128]{1,0:T(8,128)S(1)} %bitcast.17, bf16[256,1024]{1,0:T(8,128)(2,1)S(1)} %all_gather.3.hidden_ref, ...), custom_call_target="tpu_custom_call" | custom-call | tf_op jit(solution)/shard_map/down_grad/pallas_call | solution.py:287
  79.3 0.0 all-to-all-done.2
  79.3 0.0 copy-done.2
  79.3 0.0 copy-done.5
  79.3 0.8 %pick.1 = f32[4,32]{1,0:T(4,128)} custom-call(f32[8,128]{1,0:T(8,128)S(1)} %bitcast.20, s32[4,32]{1,0:T(4,128)S(1)} %copy-done.5, f32[4,32]{1,0:T(4,128)S(1)} %bitcast.22, f32[8,128]{1,0:T(8,128)S(1)} %get-tuple-element.9._), custom_call_target="tpu_custom_call" | custom-call | tf_op jit(solution)/shard_map/pick/pallas_call | solution.py:312
  (1 shorter events, 0.0 us)
Async XLA Ops:
  0.6 38.8 %copy-start.3 = (s32[128]{0:T(128)S(1)}, s32[128]{0:T(128)}, u32[]{:S(2)}) copy-start(s32[128]{0:T(128)} %param.10) | copy-start | bytes 1540
  0.6 38.8 %copy-start.4 = (s32[1,96]{1,0:T(1,128)S(1)}, s32[1,96]{1,0:T(1,128)}, u32[]{:S(2)}) copy-start(s32[1,96]{1,0:T(1,128)} %pick_ref.3) | copy-start | bytes 1156
  2.9 47.4 %all-to-all-start = ((bf16[128,2,896]{2,1,0:T(2,128)(2,1)}), bf16[128,2,896]{2,1,0:T(2,128)(2,1)S(1)}, u32[]{:S(2)}, u32[]{:S(2)}) async-start(bf16[128,2,896]{2,1,0:T(2,128)(2,1)} %get-tuple-element.6), calls=%async_computation | async-start | bytes 917504 | tf_op jit(solution)/shard_map/all_to_all | solution.py:214
  26.6 18.9 %copy-start = (bf16[1,1024,896]{2,1,0:T(8,128)(2,1)S(1)}, bf16[1,1024,896]{2,1,0:T(8,128)(2,1)}, u32[]{:S(2)}) copy-start(bf16[1,1024,896]{2,1,0:T(8,128)(2,1)} %param.13) | copy-start | bytes 5505028
  26.6 12.9 %collective-permute-start = (s32[1,96]{1,0:T(1,128)}, s32[1,96]{1,0:T(1,128)S(1)}, u32[]{:S(2)}, u32[]{:S(2)}) collective-permute-start(s32[1,96]{1,0:T(1,128)} %pick_ref.3), channel_id=1, source_target_pairs={{0,256},{256,0},{1,257},{257,1},{2,258},{258,2},{3,259},{259,3},{4... | collective-permute-start | bytes 1160 | tf_op jit(solution)/shard_map/ppermute | solution.py:237
  28.6 1.0 %copy-start.1 = (bf16[1,256,2,256]{3,2,1,0:T(2,128)(2,1)S(1)}, bf16[1,256,2,256]{3,2,1,0:T(2,128)(2,1)}, u32[]{:S(2)}) copy-start(bf16[1,256,2,256]{3,2,1,0:T(2,128)(2,1)} %param.12) | copy-start | bytes 786436
  39.8 37.2 %collective-permute-start.1 = (bf16[256,1024]{1,0:T(8,128)(2,1)S(1)}, bf16[256,1024]{1,0:T(8,128)(2,1)S(1)}, u32[]{:S(2)}, u32[]{:S(2)}) collective-permute-start(bf16[256,1024]{1,0:T(8,128)(2,1)S(1)} %pass.1), channel_id=1, source_target_pairs={{0,256},{256,0},{1,257},{257,1},{2,258},{258,2},{3,259},{259,3},{4... | collective-permute-start | bytes 1572872 | tf_op jit(solution)/shard_map/ppermute | solution.py:252
  46.1 33.2 %copy-start.2 = (f32[32,4]{0,1:T(4,128)S(1)}, f32[32,4]{0,1:T(4,128)}, u32[]{:S(2)}) copy-start(f32[32,4]{0,1:T(4,128)} %param.8) | copy-start | bytes 1540
  46.1 33.2 %copy-start.5 = (s32[4,32]{1,0:T(4,128)S(1)}, s32[4,32]{1,0:T(4,128)}, u32[]{:S(2)}) copy-start(s32[4,32]{1,0:T(4,128)} %get-tuple-element.8.target_ref) | copy-start | bytes 1540
  67.5 11.8 %all-to-all-start.2 = ((f32[8,1,128]{2,1,0:T(1,128)}), f32[8,1,128]{2,1,0:T(1,128)S(1)}, u32[]{:S(2)}, u32[]{:S(2)}) async-start(f32[8,1,128]{2,1,0:T(1,128)} %bitcast.10), calls=%async_computation.2 | async-start | bytes 8192 | tf_op jit(solution)/shard_map/all_to_all | solution.py:277

commit v13 on v12

--- a/solution.py
+++ b/solution.py
@@ -8,9 +8,9 @@
 from jax.sharding import Mesh, PartitionSpec as P
 
 
-DISPATCH_FIRST = 114
+DISPATCH_FIRST = 106
 PLACE_FIRST = 34
-LINE_FIRST = 4
+LINE_FIRST = 6
 
 
 def turned_order(count, first):
@@ -144,7 +144,7 @@
         for p in range(1, pair_rows):
             other = turned[half * pair_rows + p : half * pair_rows + p + 1, :]
             row += pltpu.roll(other, p * places, 1)
-        start = half * copies ^ LINE_FIRST
+        start = half * copies ^ LINE_FIRST // copies * copies
         out_ref[start : start + copies, :] = jnp.broadcast_to(row, (copies, out_ref.shape[1]))
 
 
@@ -153,7 +153,7 @@
     pair_rows = 2
     scratch[...] = jnp.zeros_like(scratch)
     for half in range(2):
-        start = half * copies ^ LINE_FIRST
+        start = half * copies ^ LINE_FIRST // copies * copies
         scratch[half : half + 1, :] = jnp.sum(
             returned_ref[start : start + copies, :], axis=0, keepdims=True
         )
@@ -185,7 +185,9 @@
         order_ref[...] = jnp.zeros_like(order_ref)
 
     own = own_ref[:, :1] > 0.5
-    hidden = jnp.where(own, hidden_ref[...], twin_hidden_ref[...])
+    block = out_ref.shape[0]
+    here = pl.ds(pl.multiple_of(pl.program_id(0) * block, block), block)
+    hidden = jnp.where(own, hidden_ref[:, here], twin_hidden_ref[:, here])
     out_ref[...] = lax.dot_general(
         hidden, rows_ref[...], (((0,), (0,)), ((), ())), preferred_element_type=jnp.float32
     ).astype(out_ref.dtype)
@@ -289,11 +291,8 @@
         grid=(steps,),
         in_specs=[
             pl.BlockSpec(memory_space=pl.ANY),
-            pl.BlockSpec(arrived.shape, lambda i: (0, 0, 0)),
-            pl.BlockSpec((places, 128), lambda i: (0, 0)),
-            pl.BlockSpec((rows_total, block), lambda i: (0, i)),
-            pl.BlockSpec((rows_total, block), lambda i: (0, i)),
-        ],
+        ]
+        + [pl.BlockSpec(memory_space=pltpu.VMEM)] * 4,
         out_specs=(
             pl.BlockSpec((block, features), lambda i: (i, 0)),
             pl.BlockSpec((8, 128), lambda i: (0, 0)),

time: 80.5 us -> 79.5 us (0.988)
  waiting for transfers between devices: 4.2 us -> 2.8 us
    all_to_all x1, waiting for transfers between devices: 4.2 us -> 2.16 us  [on_device(): lax.all_to_all(send_rows, ep, split_axis=0, concat_axis=0, axis_index_gro...]
    all_to_all x1, starting transfers between devices: 23.6 us -> 25 us  [on_device(): lax.all_to_all(send_rows, ep, split_axis=0, concat_axis=0, axis_index_gro...]
    all_to_all x1, starting transfers between devices: 9.47 us -> 8.66 us  [on_device(): lax.all_to_all(turned.reshape(group, 1, 128), ('half', 'rep'), split_axis...]
  transfers between devices with their start and end apart: 4 -> 4, of which waited for: 1 -> 2; matrix products, arithmetic and copies ran while one was open for 0% -> 0% of each run, Pallas kernels for 6% -> 6%
where the time goes in v13:
time: 79.5 us; the launch traced here: 79.1 us
  starting transfers between devices  41 us (52%)
  blocking collectives  25.5 us (32%)
  Pallas kernels  8.05 us (10%)
  waiting for transfers between devices  2.8 us (4%)
  local copies, waits for them, and re-layouts  0.97 us (1%)
    all_to_all x1, starting transfers between devices, on_device(): lax.all_to_all(send_rows, ep, split_axis=0, concat_axis=0, axis_index_gro...  25 us
    all_to_all x1, blocking collectives, on_device(): lax.all_to_all(dots.reshape(places, 1, 128), 'place', split_axis=0, conca...  16.1 us
    all_gather x1, blocking collectives, on_device(): hidden = lax.all_gather(part, 'rep', axis=1, tiled=True)  9.44 us
    all_to_all x1, starting transfers between devices, on_device(): lax.all_to_all(turned.reshape(group, 1, 128), ('half', 'rep'), split_axis...  8.66 us
    ppermute x1, starting transfers between devices, on_device(): twin_hidden = lax.ppermute(sent, 'half', swap)  5.36 us
    pallas_call x1, Pallas kernels, on_device(): pl.pallas_call(pack_kernel, out_shape=(jax.ShapeDtypeStruct((slot_count,...  2.25 us
    pallas_call x1, Pallas kernels, on_device(): pl.pallas_call(functools.partial(grad_kernel, first=marked), grid=(steps,...  2.2 us
    all_to_all x1, waiting for transfers between devices, on_device(): lax.all_to_all(send_rows, ep, split_axis=0, concat_axis=0, axis_index_gro...  2.16 us
  transfers between devices with their start and end apart: 4, of which 2 were waited for; matrix products, arithmetic and copies ran while one was open for 0% of the time, Pallas kernels for 6%

profile of v13, /device:TPU:1, one launch (start us, length us, event | category | flops | bytes accessed | tf_op | source)
XLA Modules:
  0.0 79.1 jit_solution(5728933443589170034)
XLA Ops:
  0.6 0.0 copy-start.3
  0.6 0.0 copy-start.4
  0.7 2.3 %pack.1 = (bf16[128,2,896]{2,1,0:T(2,128)(2,1)}, s32[4,32]{1,0:T(4,128)}) custom-call(s32[4,32]{1,0:T(4,128)} %bitcast.25, f32[4,32]{1,0:T(4,128)} %bitcast.21, s32[1,128]{1,0:T(1,128)} %bitcast.23, s32[1,96]{1,0:T(1,128)} %pick_ref.3, bf16[32,896]{1,0:T(8,128)(2,1)} %grad_ref.1), custom_call_target="tpu_custom_call" | custom-call | tf_op jit(solution)/shard_map/pack/pallas_call | solution.py:208
  2.9 25.0 %all-to-all-start = ((bf16[128,2,896]{2,1,0:T(2,128)(2,1)}), bf16[128,2,896]{2,1,0:T(2,128)(2,1)S(1)}, u32[]{:S(2)}, u32[]{:S(2)}) async-start(bf16[128,2,896]{2,1,0:T(2,128)(2,1)} %get-tuple-element.6), calls=%async_computation | async-start | bytes 917504 | tf_op jit(solution)/shard_map/all_to_all | solution.py:216
  27.9 0.0 copy-start
  27.9 2.1 %collective-permute-start = (s32[1,96]{1,0:T(1,128)}, s32[1,96]{1,0:T(1,128)S(1)}, u32[]{:S(2)}, u32[]{:S(2)}) collective-permute-start(s32[1,96]{1,0:T(1,128)} %pick_ref.3), channel_id=1, source_target_pairs={{0,256},{256,0},{1,257},{257,1},{2,258},{258,2},{3,259},{259,3},{4... | collective-permute-start | bytes 1160 | tf_op jit(solution)/shard_map/ppermute | solution.py:239
  30.0 0.0 copy-start.1
  30.0 0.9 %copy-done.1 = bf16[1,256,2,256]{3,2,1,0:T(2,128)(2,1)S(1)} copy-done((bf16[1,256,2,256]{3,2,1,0:T(2,128)(2,1)S(1)}, bf16[1,256,2,256]{3,2,1,0:T(2,128)(2,1)}, u32[]{:S(2)}) %copy-start.1) | copy-done | bytes 262168
  30.9 0.7 hidden.1
  31.6 9.4 %all_gather.3.hidden_ref = bf16[256,1024]{1,0:T(8,128)(2,1)S(1)} all-gather(bf16[256,256]{1,0:T(8,128)(2,1)S(1)} %hidden.1), channel_id=1, replica_groups=mesh['half'=2,'place'=64,'rep'=4] {'rep'}, dimensions={1}, use_global_device_ids=true | all-gather | bytes 655360 | tf_op jit(solution)/shard_map/all_gather | solution.py:240
  41.0 0.0 collective-permute-done.twin_ref
  41.0 0.0 copy-done.3
  41.0 0.0 copy-done.4
  41.0 0.3 marks.1.marks_ref._
  41.4 5.4 %collective-permute-start.1 = (bf16[256,1024]{1,0:T(8,128)(2,1)S(1)}, bf16[256,1024]{1,0:T(8,128)(2,1)S(1)}, u32[]{:S(2)}, u32[]{:S(2)}) collective-permute-start(bf16[256,1024]{1,0:T(8,128)(2,1)S(1)} %pass.1), channel_id=1, source_target_pairs={{0,256},{256,0},{1,257},{257,1},{2,258},{258,2},{3,259},{259,3},{4... | collective-permute-start | bytes 1572872 | tf_op jit(solution)/shard_map/ppermute | solution.py:254
  46.7 0.0 copy-done
  46.8 0.7 forward.1.outputs_ref
  47.5 0.0 copy-start.2
  47.5 0.0 copy-start.5
  47.5 2.2 %all-to-all-done.arrived_ref = bf16[128,2,896]{2,1,0:T(2,128)(2,1)S(1)} async-done(((bf16[128,2,896]{2,1,0:T(2,128)(2,1)}), bf16[128,2,896]{2,1,0:T(2,128)(2,1)S(1)}, u32[]{:S(2)}, u32[]{:S(2)}) %all-to-all-start) | async-done | bytes 458784 | tf_op jit(solution)/shard_map/all_to_all | solution.py:216
  49.7 0.4 dots.1
  50.0 16.1 %all_to_all.15 = f32[64,1,128]{2,1,0:T(1,128)S(1)} all-to-all(f32[64,1,128]{2,1,0:T(1,128)S(1)} %bitcast.19), channel_id=1, replica_groups={{136,140,128,132,152,156,144,148,168,172,160,164,184,188,176,180,200,20..., dimensions={0} | all-to-all | bytes 65536 | tf_op jit(solution)/shard_map/all_to_all | solution.py:263
  66.1 0.7 turn.1._
  66.8 8.7 %all-to-all-start.2 = ((f32[8,1,128]{2,1,0:T(1,128)}), f32[8,1,128]{2,1,0:T(1,128)S(1)}, u32[]{:S(2)}, u32[]{:S(2)}) async-start(f32[8,1,128]{2,1,0:T(1,128)} %bitcast.10), calls=%async_computation.2 | async-start | bytes 8192 | tf_op jit(solution)/shard_map/all_to_all | solution.py:279
  75.5 0.0 collective-permute-done.1.twin_hidden_ref
  75.5 2.2 %down_grad.1 = (bf16[1024,896]{1,0:T(8,128)(2,1)}, f32[8,128]{1,0:T(8,128)S(1)}) custom-call(f32[8,128]{1,0:T(8,128)} %turn.1._, bf16[128,2,896]{2,1,0:T(2,128)(2,1)S(1)} %all-to-all-done.arrived_ref, f32[64,128]{1,0:T(8,128)S(1)} %bitcast.17, bf16[256,1024]{1,0:T(8,128)(2,1)S(1)} %all_gather.3.hidden_ref, ...), custom_call_target="tpu_custom_call" | custom-call | tf_op jit(solution)/shard_map/down_grad/pallas_call | solution.py:289
  77.7 0.6 all-to-all-done.2
  78.3 0.0 copy-done.2
  78.3 0.0 copy-done.5
  78.3 0.8 %pick.1 = f32[4,32]{1,0:T(4,128)} custom-call(f32[8,128]{1,0:T(8,128)S(1)} %bitcast.20, s32[4,32]{1,0:T(4,128)S(1)} %copy-done.5, f32[4,32]{1,0:T(4,128)S(1)} %bitcast.22, f32[8,128]{1,0:T(8,128)S(1)} %get-tuple-element.9._), custom_call_target="tpu_custom_call" | custom-call | tf_op jit(solution)/shard_map/pick/pallas_call | solution.py:311
  (1 shorter events, 0.0 us)
Async XLA Ops:
  0.6 40.4 %copy-start.3 = (s32[128]{0:T(128)S(1)}, s32[128]{0:T(128)}, u32[]{:S(2)}) copy-start(s32[128]{0:T(128)} %param.10) | copy-start | bytes 1540
  0.6 40.4 %copy-start.4 = (s32[1,96]{1,0:T(1,128)S(1)}, s32[1,96]{1,0:T(1,128)}, u32[]{:S(2)}) copy-start(s32[1,96]{1,0:T(1,128)} %pick_ref.3) | copy-start | bytes 1156
  2.9 46.7 %all-to-all-start = ((bf16[128,2,896]{2,1,0:T(2,128)(2,1)}), bf16[128,2,896]{2,1,0:T(2,128)(2,1)S(1)}, u32[]{:S(2)}, u32[]{:S(2)}) async-start(bf16[128,2,896]{2,1,0:T(2,128)(2,1)} %get-tuple-element.6), calls=%async_computation | async-start | bytes 917504 | tf_op jit(solution)/shard_map/all_to_all | solution.py:216
  27.9 18.9 %copy-start = (bf16[1,1024,896]{2,1,0:T(8,128)(2,1)S(1)}, bf16[1,1024,896]{2,1,0:T(8,128)(2,1)}, u32[]{:S(2)}) copy-start(bf16[1,1024,896]{2,1,0:T(8,128)(2,1)} %param.13) | copy-start | bytes 5505028
  27.9 13.1 %collective-permute-start = (s32[1,96]{1,0:T(1,128)}, s32[1,96]{1,0:T(1,128)S(1)}, u32[]{:S(2)}, u32[]{:S(2)}) collective-permute-start(s32[1,96]{1,0:T(1,128)} %pick_ref.3), channel_id=1, source_target_pairs={{0,256},{256,0},{1,257},{257,1},{2,258},{258,2},{3,259},{259,3},{4... | collective-permute-start | bytes 1160 | tf_op jit(solution)/shard_map/ppermute | solution.py:239
  30.0 1.0 %copy-start.1 = (bf16[1,256,2,256]{3,2,1,0:T(2,128)(2,1)S(1)}, bf16[1,256,2,256]{3,2,1,0:T(2,128)(2,1)}, u32[]{:S(2)}) copy-start(bf16[1,256,2,256]{3,2,1,0:T(2,128)(2,1)} %param.12) | copy-start | bytes 786436
  41.4 34.1 %collective-permute-start.1 = (bf16[256,1024]{1,0:T(8,128)(2,1)S(1)}, bf16[256,1024]{1,0:T(8,128)(2,1)S(1)}, u32[]{:S(2)}, u32[]{:S(2)}) collective-permute-start(bf16[256,1024]{1,0:T(8,128)(2,1)S(1)} %pass.1), channel_id=1, source_target_pairs={{0,256},{256,0},{1,257},{257,1},{2,258},{258,2},{3,259},{259,3},{4... | collective-permute-start | bytes 1572872 | tf_op jit(solution)/shard_map/ppermute | solution.py:254
  47.5 30.8 %copy-start.2 = (f32[32,4]{0,1:T(4,128)S(1)}, f32[32,4]{0,1:T(4,128)}, u32[]{:S(2)}) copy-start(f32[32,4]{0,1:T(4,128)} %param.8) | copy-start | bytes 1540
  47.5 30.8 %copy-start.5 = (s32[4,32]{1,0:T(4,128)S(1)}, s32[4,32]{1,0:T(4,128)}, u32[]{:S(2)}) copy-start(s32[4,32]{1,0:T(4,128)} %get-tuple-element.8.target_ref) | copy-start | bytes 1540
  66.8 11.5 %all-to-all-start.2 = ((f32[8,1,128]{2,1,0:T(1,128)}), f32[8,1,128]{2,1,0:T(1,128)S(1)}, u32[]{:S(2)}, u32[]{:S(2)}) async-start(f32[8,1,128]{2,1,0:T(1,128)} %bitcast.10), calls=%async_computation.2 | async-start | bytes 8192 | tf_op jit(solution)/shard_map/all_to_all | solution.py:279

commit v14 on v13

--- a/solution.py
+++ b/solution.py
@@ -33,7 +33,7 @@
     return rows
 
 
-def pack_kernel(ids_ref, weight_ref, slot_expert_ref, pick_ref, grad_ref, rows_ref, target_ref):
+def pack_kernel(ids_ref, weight_ref, slot_expert_ref, pick_ref, grad_ref, out_ref, target_ref, rows_ref, sent):
     top, tokens = ids_ref.shape
     experts = pick_ref.shape[1]
     slots, pair_rows, _ = rows_ref.shape
@@ -77,8 +77,19 @@
         target_ref[k : k + 1, :] = target
         here = (row == target) | (row == twin_target.astype(jnp.int32))
         mix += jnp.where(here, weight_ref[k : k + 1, :], 0.0)
-    rows = jnp.dot(mix.astype(jnp.bfloat16), grad_ref[...], preferred_element_type=jnp.float32)
-    rows_ref[...] = rows.astype(rows_ref.dtype).reshape(rows_ref.shape)
+    mix = mix.astype(jnp.bfloat16)
+    count = slots // 2
+    copies = []
+    for part in range(2):
+        here = mix[part * count * pair_rows : (part + 1) * count * pair_rows, :]
+        rows = jnp.dot(here, grad_ref[...], preferred_element_type=jnp.float32)
+        half = pl.ds(part * count, count)
+        rows_ref[half] = rows.astype(rows_ref.dtype).reshape(count, pair_rows, rows.shape[1])
+        copy = pltpu.make_async_copy(rows_ref.at[half], out_ref.at[half], sent.at[part])
+        copy.start()
+        copies.append(copy)
+    for copy in copies:
+        copy.wait()
 
 
 def hidden_kernel(saved_ref, out_ref):
@@ -134,16 +145,12 @@
     dots_ref[...] = swap_places(found)
 
 
-def turn_kernel(arrived_ref, out_ref, scratch, *, pair_rows, copies):
-    places = arrived_ref.shape[0]
-    scratch[...] = jnp.zeros_like(scratch)
-    scratch[:places, :] = arrived_ref[...]
-    turned = scratch[...].T
+def turn_kernel(arrived_ref, out_ref, *, pair_rows, copies):
+    turned = arrived_ref[...].T
     for half in range(2):
-        row = turned[half * pair_rows : half * pair_rows + 1, :]
-        for p in range(1, pair_rows):
-            other = turned[half * pair_rows + p : half * pair_rows + p + 1, :]
-            row += pltpu.roll(other, p * places, 1)
+        row = jnp.concatenate(
+            [turned[half * pair_rows + p : half * pair_rows + p + 1, :] for p in range(pair_rows)], axis=1
+        )
         start = half * copies ^ LINE_FIRST // copies * copies
         out_ref[start : start + copies, :] = jnp.broadcast_to(row, (copies, out_ref.shape[1]))
 
@@ -211,6 +218,11 @@
             jax.ShapeDtypeStruct((slot_count, pair_rows, features), jnp.bfloat16),
             jax.ShapeDtypeStruct((top_count, token_count), jnp.int32),
         ),
+        out_specs=(pl.BlockSpec(memory_space=pl.ANY), pl.BlockSpec(memory_space=pltpu.VMEM)),
+        scratch_shapes=[
+            pltpu.VMEM((slot_count, pair_rows, features), jnp.bfloat16),
+            pltpu.SemaphoreType.DMA((2,)),
+        ],
         name="pack",
     )(ids_t, weight_t, slot_expert[None], replica_pick, out_grad)
     arrived = lax.all_to_all(
@@ -272,7 +284,6 @@
     turned = pl.pallas_call(
         functools.partial(turn_kernel, pair_rows=pair_rows, copies=copies),
         out_shape=jax.ShapeDtypeStruct((group, 128), jnp.float32),
-        scratch_shapes=[pltpu.VMEM((128, 128), jnp.float32)],
         compiler_params=pltpu.CompilerParams(vmem_limit_bytes=4 << 20),
         name="turn",
     )(met)
@@ -312,7 +323,7 @@
         functools.partial(pick_kernel, places=places, copies=copies),
         in_specs=[pl.BlockSpec(memory_space=pltpu.VMEM)] * 3 + [pl.BlockSpec(memory_space=pl.ANY)],
         out_shape=jax.ShapeDtypeStruct((top_count, token_count), jnp.float32),
-        scratch_shapes=[pltpu.VMEM((128, 128), jnp.float32)],
+        scratch_shapes=[pltpu.VMEM((8, 128), jnp.float32)],
         compiler_params=pltpu.CompilerParams(vmem_limit_bytes=4 << 20),
         name="pick",
     )(returned.reshape(group, 128), target, weight_t, order)

time: 79.5 us -> 80 us (level)
  no operation moved by 1% of the time
where the time goes in v14:
time: 80 us; the launch traced here: 79.6 us
  starting transfers between devices  41.1 us (51%)
  blocking collectives  25.5 us (32%)
  Pallas kernels  8.56 us (11%)
  waiting for transfers between devices  2.8 us (4%)
  local copies, waits for them, and re-layouts  0.97 us (1%)
    all_to_all x1, starting transfers between devices, on_device(): lax.all_to_all(send_rows, ep, split_axis=0, concat_axis=0, axis_index_gro...  25 us
    all_to_all x1, blocking collectives, on_device(): lax.all_to_all(dots.reshape(places, 1, 128), 'place', split_axis=0, conca...  16.1 us
    all_gather x1, blocking collectives, on_device(): hidden = lax.all_gather(part, 'rep', axis=1, tiled=True)  9.43 us
    all_to_all x1, starting transfers between devices, on_device(): lax.all_to_all(turned.reshape(group, 1, 128), ('half', 'rep'), split_axis...  8.65 us
    ppermute x1, starting transfers between devices, on_device(): twin_hidden = lax.ppermute(sent, 'half', swap)  5.36 us
    pallas_call x1, Pallas kernels, on_device(): pl.pallas_call(pack_kernel, out_shape=(jax.ShapeDtypeStruct((slot_count,...  2.76 us
    pallas_call x1, Pallas kernels, on_device(): pl.pallas_call(functools.partial(grad_kernel, first=marked), grid=(steps,...  2.2 us
    all_to_all x1, waiting for transfers between devices, on_device(): lax.all_to_all(send_rows, ep, split_axis=0, concat_axis=0, axis_index_gro...  2.17 us
  transfers between devices with their start and end apart: 4, of which 2 were waited for; matrix products, arithmetic and copies ran while one was open for 0% of the time, Pallas kernels for 6%

profile of v14, /device:TPU:1, one launch (start us, length us, event | category | flops | bytes accessed | tf_op | source)
XLA Modules:
  0.0 79.6 jit_solution(10913973146136688326)
XLA Ops:
  0.6 0.0 copy-start.3
  0.6 0.0 copy-start.4
  0.7 2.8 %pack.1 = (bf16[128,2,896]{2,1,0:T(2,128)(2,1)}, s32[4,32]{1,0:T(4,128)}) custom-call(s32[4,32]{1,0:T(4,128)} %bitcast.25, f32[4,32]{1,0:T(4,128)} %bitcast.21, s32[1,128]{1,0:T(1,128)} %bitcast.23, s32[1,96]{1,0:T(1,128)} %pick_ref.3, bf16[32,896]{1,0:T(8,128)(2,1)} %grad_ref.1), custom_call_target="tpu_custom_call" | custom-call | tf_op jit(solution)/shard_map/pack/pallas_call | solution.py:215
  3.4 25.0 %all-to-all-start = ((bf16[128,2,896]{2,1,0:T(2,128)(2,1)}), bf16[128,2,896]{2,1,0:T(2,128)(2,1)S(1)}, u32[]{:S(2)}, u32[]{:S(2)}) async-start(bf16[128,2,896]{2,1,0:T(2,128)(2,1)} %get-tuple-element.6), calls=%async_computation | async-start | bytes 917504 | tf_op jit(solution)/shard_map/all_to_all | solution.py:228
  28.4 0.0 copy-start
  28.4 2.1 %collective-permute-start = (s32[1,96]{1,0:T(1,128)}, s32[1,96]{1,0:T(1,128)S(1)}, u32[]{:S(2)}, u32[]{:S(2)}) collective-permute-start(s32[1,96]{1,0:T(1,128)} %pick_ref.3), channel_id=1, source_target_pairs={{0,256},{256,0},{1,257},{257,1},{2,258},{258,2},{3,259},{259,3},{4... | collective-permute-start | bytes 1160 | tf_op jit(solution)/shard_map/ppermute | solution.py:251
  30.5 0.0 copy-start.1
  30.5 0.9 %copy-done.1 = bf16[1,256,2,256]{3,2,1,0:T(2,128)(2,1)S(1)} copy-done((bf16[1,256,2,256]{3,2,1,0:T(2,128)(2,1)S(1)}, bf16[1,256,2,256]{3,2,1,0:T(2,128)(2,1)}, u32[]{:S(2)}) %copy-start.1) | copy-done | bytes 262168
  31.4 0.7 hidden.1
  32.1 9.4 %all_gather.3.hidden_ref = bf16[256,1024]{1,0:T(8,128)(2,1)S(1)} all-gather(bf16[256,256]{1,0:T(8,128)(2,1)S(1)} %hidden.1), channel_id=1, replica_groups=mesh['half'=2,'place'=64,'rep'=4] {'rep'}, dimensions={1}, use_global_device_ids=true | all-gather | bytes 655360 | tf_op jit(solution)/shard_map/all_gather | solution.py:252
  41.5 0.0 collective-permute-done.twin_ref
  41.5 0.0 copy-done.3
  41.5 0.0 copy-done.4
  41.5 0.3 marks.1.marks_ref._
  41.9 5.4 %collective-permute-start.1 = (bf16[256,1024]{1,0:T(8,128)(2,1)S(1)}, bf16[256,1024]{1,0:T(8,128)(2,1)S(1)}, u32[]{:S(2)}, u32[]{:S(2)}) collective-permute-start(bf16[256,1024]{1,0:T(8,128)(2,1)S(1)} %pass.1), channel_id=1, source_target_pairs={{0,256},{256,0},{1,257},{257,1},{2,258},{258,2},{3,259},{259,3},{4... | collective-permute-start | bytes 1572872 | tf_op jit(solution)/shard_map/ppermute | solution.py:266
  47.3 0.0 copy-done
  47.3 0.7 forward.1.outputs_ref
  48.0 0.0 copy-start.2
  48.0 0.0 copy-start.5
  48.0 2.2 %all-to-all-done.arrived_ref = bf16[128,2,896]{2,1,0:T(2,128)(2,1)S(1)} async-done(((bf16[128,2,896]{2,1,0:T(2,128)(2,1)}), bf16[128,2,896]{2,1,0:T(2,128)(2,1)S(1)}, u32[]{:S(2)}, u32[]{:S(2)}) %all-to-all-start) | async-done | bytes 458784 | tf_op jit(solution)/shard_map/all_to_all | solution.py:228
  50.2 0.4 dots.1
  50.5 16.1 %all_to_all.15 = f32[64,1,128]{2,1,0:T(1,128)S(1)} all-to-all(f32[64,1,128]{2,1,0:T(1,128)S(1)} %bitcast.19), channel_id=1, replica_groups={{136,140,128,132,152,156,144,148,168,172,160,164,184,188,176,180,200,20..., dimensions={0} | all-to-all | bytes 65536 | tf_op jit(solution)/shard_map/all_to_all | solution.py:275
  66.6 0.7 turn.1._
  67.3 8.7 %all-to-all-start.2 = ((f32[8,1,128]{2,1,0:T(1,128)}), f32[8,1,128]{2,1,0:T(1,128)S(1)}, u32[]{:S(2)}, u32[]{:S(2)}) async-start(f32[8,1,128]{2,1,0:T(1,128)} %bitcast.10), calls=%async_computation.2 | async-start | bytes 8192 | tf_op jit(solution)/shard_map/all_to_all | solution.py:290
  76.0 0.0 collective-permute-done.1.twin_hidden_ref
  76.0 2.2 %down_grad.1 = (bf16[1024,896]{1,0:T(8,128)(2,1)}, f32[8,128]{1,0:T(8,128)S(1)}) custom-call(f32[8,128]{1,0:T(8,128)} %turn.1._, bf16[128,2,896]{2,1,0:T(2,128)(2,1)S(1)} %all-to-all-done.arrived_ref, f32[64,128]{1,0:T(8,128)S(1)} %bitcast.17, bf16[256,1024]{1,0:T(8,128)(2,1)S(1)} %all_gather.3.hidden_ref, ...), custom_call_target="tpu_custom_call" | custom-call | tf_op jit(solution)/shard_map/down_grad/pallas_call | solution.py:300
  78.2 0.6 all-to-all-done.2
  78.8 0.0 copy-done.2
  78.8 0.0 copy-done.5
  78.8 0.8 %pick.1 = f32[4,32]{1,0:T(4,128)} custom-call(f32[8,128]{1,0:T(8,128)S(1)} %bitcast.20, s32[4,32]{1,0:T(4,128)S(1)} %copy-done.5, f32[4,32]{1,0:T(4,128)S(1)} %bitcast.22, f32[8,128]{1,0:T(8,128)S(1)} %get-tuple-element.9._), custom_call_target="tpu_custom_call" | custom-call | tf_op jit(solution)/shard_map/pick/pallas_call | solution.py:322
  (1 shorter events, 0.0 us)
Async XLA Ops:
  0.6 40.9 %copy-start.3 = (s32[128]{0:T(128)S(1)}, s32[128]{0:T(128)}, u32[]{:S(2)}) copy-start(s32[128]{0:T(128)} %param.10) | copy-start | bytes 1540
  0.6 40.9 %copy-start.4 = (s32[1,96]{1,0:T(1,128)S(1)}, s32[1,96]{1,0:T(1,128)}, u32[]{:S(2)}) copy-start(s32[1,96]{1,0:T(1,128)} %pick_ref.3) | copy-start | bytes 1156
  3.4 46.8 %all-to-all-start = ((bf16[128,2,896]{2,1,0:T(2,128)(2,1)}), bf16[128,2,896]{2,1,0:T(2,128)(2,1)S(1)}, u32[]{:S(2)}, u32[]{:S(2)}) async-start(bf16[128,2,896]{2,1,0:T(2,128)(2,1)} %get-tuple-element.6), calls=%async_computation | async-start | bytes 917504 | tf_op jit(solution)/shard_map/all_to_all | solution.py:228
  28.4 18.8 %copy-start = (bf16[1,1024,896]{2,1,0:T(8,128)(2,1)S(1)}, bf16[1,1024,896]{2,1,0:T(8,128)(2,1)}, u32[]{:S(2)}) copy-start(bf16[1,1024,896]{2,1,0:T(8,128)(2,1)} %param.13) | copy-start | bytes 5505028
  28.4 13.1 %collective-permute-start = (s32[1,96]{1,0:T(1,128)}, s32[1,96]{1,0:T(1,128)S(1)}, u32[]{:S(2)}, u32[]{:S(2)}) collective-permute-start(s32[1,96]{1,0:T(1,128)} %pick_ref.3), channel_id=1, source_target_pairs={{0,256},{256,0},{1,257},{257,1},{2,258},{258,2},{3,259},{259,3},{4... | collective-permute-start | bytes 1160 | tf_op jit(solution)/shard_map/ppermute | solution.py:251
  30.5 1.0 %copy-start.1 = (bf16[1,256,2,256]{3,2,1,0:T(2,128)(2,1)S(1)}, bf16[1,256,2,256]{3,2,1,0:T(2,128)(2,1)}, u32[]{:S(2)}) copy-start(bf16[1,256,2,256]{3,2,1,0:T(2,128)(2,1)} %param.12) | copy-start | bytes 786436
  41.9 34.1 %collective-permute-start.1 = (bf16[256,1024]{1,0:T(8,128)(2,1)S(1)}, bf16[256,1024]{1,0:T(8,128)(2,1)S(1)}, u32[]{:S(2)}, u32[]{:S(2)}) collective-permute-start(bf16[256,1024]{1,0:T(8,128)(2,1)S(1)} %pass.1), channel_id=1, source_target_pairs={{0,256},{256,0},{1,257},{257,1},{2,258},{258,2},{3,259},{259,3},{4... | collective-permute-start | bytes 1572872 | tf_op jit(solution)/shard_map/ppermute | solution.py:266
  48.0 30.8 %copy-start.2 = (f32[32,4]{0,1:T(4,128)S(1)}, f32[32,4]{0,1:T(4,128)}, u32[]{:S(2)}) copy-start(f32[32,4]{0,1:T(4,128)} %param.8) | copy-start | bytes 1540
  48.0 30.8 %copy-start.5 = (s32[4,32]{1,0:T(4,128)S(1)}, s32[4,32]{1,0:T(4,128)}, u32[]{:S(2)}) copy-start(s32[4,32]{1,0:T(4,128)} %get-tuple-element.8.target_ref) | copy-start | bytes 1540
  67.3 11.5 %all-to-all-start.2 = ((f32[8,1,128]{2,1,0:T(1,128)}), f32[8,1,128]{2,1,0:T(1,128)S(1)}, u32[]{:S(2)}, u32[]{:S(2)}) async-start(f32[8,1,128]{2,1,0:T(1,128)} %bitcast.10), calls=%async_computation.2 | async-start | bytes 8192 | tf_op jit(solution)/shard_map/all_to_all | solution.py:290
